TPU v7x, 32 devices: a whole 2x2x4 slice. The times are simulated.
32 devices in a mesh: ens: 2 (over y), tx: 4 (over z), ty: 2 (over x), tz: 2 (over core).
Axes of the slice: x: 2, y: 2, z: 4, core: 2. Of those that a mesh axis runs over, the one named last changes fastest.
Arguments:
- atm_flux: bfloat16 [1536, 8, 128], P(('ens', 'tx', 'ty', 'tz')), parts along dimension 0, may hold values from -6 to 6
- atm_rows: int32 [768], P(('tx', 'ty', 'tz')), may hold values from 1 to 128
- regrid_weights: bfloat16 [1536, 128, 128], P(('tx', 'ty', 'tz')), may hold values from -0.5 to 0.5
- pair_dest: int32 [1536, 1], P(('tx', 'ty', 'tz')), may hold values from 0 to 15; in each aligned block of 96 rows (0 to 95, 96 to 191, ...) at most 12 rows name the same one
- pair_atm: int32 [1536], P(('tx', 'ty', 'tz')), may hold values from 0 to 47
- pair_row: int32 [1536], P(('tx', 'ty', 'tz')), may hold values from 0 to 127
- tracers: float32 [12, 8, 512, 512], P('ens', None, ('ty', 'tz'), 'tx'), parts along dimension 0, may hold values from -6 to 6
- velocity: float32 [4, 8, 512, 512], P('ens', None, ('ty', 'tz'), 'tx'), parts along dimension 0, may hold values from -0.6 to 0.6
- mixing: float32 [14, 512, 512], P('ens', ('ty', 'tz'), 'tx'), parts along dimension 0, may hold values from 0.05 to 5
- land: int32 [512, 512], P(('ty', 'tz'), 'tx'), may hold values 0 or 1
Outputs:
- tracers_out: float32 [12, 8, 512, 512], P('ens', None, ('ty', 'tz'), 'tx'), parts along dimension 0
- atm_surface: float32 [1536, 6, 128], P(('ens', 'tx', 'ty', 'tz')), parts along dimension 0
There are 2 independent parts, one for each index of `ens`. A program takes and returns all parts, laid end to end along the dimension named above; an argument that names none is the same for every part. Nothing has to cross between parts.
Inputs may be any that keep to these rules, and one draw needn't show every extreme that they name: `pair_dest`: among the 96 pairs of one atmosphere owner no ocean device is named more than 12 times, and some device is named exactly 12 times.
All inputs are finite; a program needn't handle non-finite values. No bound on the sum of `land` on one device may be relied on, other than what follows from the above.
Results may differ from a plain program's by a relative error of at most 0.002.
Values may be sent and summed in bfloat16 or wider, within the bound.
No kernel may reach another device: no remote copies, remote signals or barrier semaphores. Data moves between devices by JAX's collectives and lax.ppermute only.
A program may use at most 128 MiB of HBM per device.

v0:
```python
import jax
import jax.numpy as jnp
from jax import lax
from jax.sharding import PartitionSpec as P

DIFFUSION = 0.2
FORCING = 0.5


def with_halo(shard, sides, width):
    for axis, dim in sides:
        size, length = (lax.axis_size(axis), shard.shape[dim])
        up = [(i, (i + 1) % size) for i in range(size - 1)]
        down = [(j, i) for i, j in up]
        last = lax.slice_in_dim(shard, length - width, length, axis=dim)
        leading = lax.slice_in_dim(shard, 0, width, axis=dim)
        before = lax.ppermute(last, axis, up)
        after = lax.ppermute(leading, axis, down)
        shard = jnp.concatenate([before, shard, after], axis=dim)
    return shard


def column_sides(centre):
    edges = jnp.concatenate([centre[..., :1], centre[..., -1:]], axis=-1)
    widened = with_halo(edges, (("tx", 3),), 1)
    east_cell = jnp.concatenate([centre[..., 1:], widened[..., 3:]], axis=-1)
    west_cell = jnp.concatenate([widened[..., :1], centre[..., :-1]], axis=-1)
    return (east_cell, west_cell)


def advect_rows(padded, vel_u, vel_v, sea_mask):
    centre = padded[..., 1:-1, :]
    north_cell = padded[..., 2:, :]
    south_cell = padded[..., :-2, :]
    east_cell, west_cell = column_sides(centre)
    tendency = -0.5 * (vel_u * (east_cell - west_cell) + vel_v * (north_cell - south_cell))
    tendency = tendency + DIFFUSION * (
        east_cell + west_cell + north_cell + south_cell - 4.0 * centre
    )
    return centre + sea_mask * tendency


def force_mix(tracer, surface_flux, coupling, sea_mask):
    count_tracers = tracer.shape[0]
    level_count = tracer.shape[1]
    surface_top = tracer[:, 0] + FORCING * sea_mask * surface_flux[:count_tracers]
    stirring = 1.0 + 0.5 * (
        surface_flux[-2] * surface_flux[-2] + surface_flux[-1] * surface_flux[-1]
    )
    couplings = [coupling[0] * stirring] + [coupling[k] for k in range(1, level_count - 1)]
    right_side = [surface_top] + [tracer[:, k] for k in range(1, level_count)]
    upper_prime = []
    rhs_prime = []
    for level_index in range(level_count):
        upper_link = couplings[level_index - 1] if level_index > 0 else 0.0
        lower_link = couplings[level_index] if level_index < level_count - 1 else 0.0
        diagonal = 1.0 + upper_link + lower_link
        if level_index == 0:
            pivot_value = diagonal
            new_rhs = right_side[0] / pivot_value
        else:
            pivot_value = diagonal - upper_link * upper_prime[-1]
            new_rhs = (right_side[level_index] + upper_link * rhs_prime[-1]) / pivot_value
        upper_prime.append(lower_link / pivot_value)
        rhs_prime.append(new_rhs)
    solution = [rhs_prime[-1]]
    for level_index in range(level_count - 2, -1, -1):
        solution.append(rhs_prime[level_index] + upper_prime[level_index] * solution[-1])
    solved = jnp.stack(solution[::-1], axis=1)
    return sea_mask * solved + (1.0 - sea_mask) * tracer


def on_device(
    atm_flux,
    atm_rows,
    regrid_weights,
    pair_dest,
    pair_atm,
    pair_row,
    tracers,
    velocity,
    mixing,
    land,
):
    count_x = lax.axis_size("tx")
    groups = lax.axis_size("ty") * lax.axis_size("tz")
    node_count = count_x * groups
    count_pairs = pair_atm.shape[0]
    capacity = max(2, (2 * count_pairs + node_count - 1) // node_count)
    fields = atm_flux.shape[1]
    atm_cells = atm_flux.shape[2]
    block_count = atm_flux.shape[0]
    count_tracers = tracers.shape[0]
    height = tracers.shape[2]
    tile_width = tracers.shape[3]
    valid_rows = jnp.arange(atm_cells, dtype=jnp.int32)[None, :] < atm_rows[:, None]
    masked = jnp.where(valid_rows[:, None, :], atm_flux, jnp.zeros((), jnp.bfloat16))
    picked = masked[pair_atm]
    contrib = jnp.einsum("pfa,pao->pfo", picked, regrid_weights, preferred_element_type=jnp.float32)
    target = pair_dest[:, 0]
    onehot = (target[:, None] == jnp.arange(node_count, dtype=jnp.int32)[None, :]).astype(jnp.int32)
    before = jnp.cumsum(onehot, axis=0) - onehot
    position = jnp.sum(before * onehot, axis=1)
    slot_index = target * capacity + position
    outgoing = (
        jnp.zeros((node_count * capacity, fields, tile_width), jnp.float32)
        .at[slot_index]
        .set(contrib)
    )
    out_rows = jnp.full((node_count * capacity,), -1, jnp.int32).at[slot_index].set(pair_row)
    incoming, in_rows = (
        lax.all_to_all(
            outgoing.reshape(node_count, capacity, fields, tile_width),
            ("tx", "ty", "tz"),
            split_axis=0,
            concat_axis=0,
            tiled=True,
        ),
        lax.all_to_all(
            out_rows.reshape(node_count, capacity),
            ("tx", "ty", "tz"),
            split_axis=0,
            concat_axis=0,
            tiled=True,
        ),
    )
    in_flat = in_rows.reshape(-1)
    selector = (jnp.arange(height, dtype=jnp.int32)[:, None] == in_flat[None, :]).astype(
        jnp.float32
    )
    surface_flux = jnp.einsum(
        "hr,rfo->fho",
        selector,
        incoming.reshape(node_count * capacity, fields, tile_width),
        precision=lax.Precision.HIGHEST,
    )
    sea_mask = land.astype(jnp.float32)
    ocean_state = tracers
    for repeat in range(2):
        padded = with_halo(ocean_state, ((("ty", "tz"), 2),), 1)
        ocean_state = advect_rows(padded, velocity[0], velocity[1], sea_mask)
        ocean_state = force_mix(ocean_state, surface_flux, mixing, sea_mask)
    surface_top = (ocean_state[:, 0] * sea_mask).astype(jnp.bfloat16)
    safe_rows = jnp.clip(in_flat, 0, height - 1)
    row_pick = (safe_rows[:, None] == jnp.arange(height, dtype=jnp.int32)[None, :]).astype(
        jnp.bfloat16
    )
    reply_rows = jnp.einsum(
        "rh,tho->rto", row_pick, surface_top, preferred_element_type=jnp.float32
    ).astype(jnp.bfloat16)
    reply_rows = reply_rows.reshape(node_count, capacity, count_tracers, tile_width)
    returned = lax.all_to_all(
        reply_rows, ("tx", "ty", "tz"), split_axis=0, concat_axis=0, tiled=True
    ).reshape(node_count * capacity, count_tracers, tile_width)
    pair_values = returned[slot_index]
    back_terms = jnp.einsum(
        "pto,pao->pta", pair_values, regrid_weights, preferred_element_type=jnp.float32
    )
    owner_map = (jnp.arange(block_count, dtype=jnp.int32)[:, None] == pair_atm[None, :]).astype(
        jnp.float32
    )
    atm_surface = jnp.dot(
        owner_map,
        back_terms.reshape(count_pairs, count_tracers * atm_cells),
        precision=lax.Precision.HIGHEST,
    )
    atm_surface = atm_surface.reshape(block_count, count_tracers, atm_cells)
    atm_surface = jnp.where(valid_rows[:, None, :], atm_surface, 0.0)
    return (ocean_state, atm_surface)


def solution(mesh):
    in_specs = (
        P(("ens", "tx", "ty", "tz"), None, None),
        P(("tx", "ty", "tz")),
        P(("tx", "ty", "tz"), None, None),
        P(("tx", "ty", "tz"), None),
        P(("tx", "ty", "tz")),
        P(("tx", "ty", "tz")),
        P("ens", None, ("ty", "tz"), "tx"),
        P("ens", None, ("ty", "tz"), "tx"),
        P("ens", ("ty", "tz"), "tx"),
        P(("ty", "tz"), "tx"),
    )
    out_specs = (P("ens", None, ("ty", "tz"), "tx"), P(("ens", "tx", "ty", "tz"), None, None))
    return jax.shard_map(
        on_device, mesh=mesh, in_specs=in_specs, out_specs=out_specs, check_vma=False
    )
```

profile of v0, /device:TPU:0, one launch (start us, length us, event | category | flops | bytes accessed | tf_op | source)
XLA Modules:
  0.0 169.5 jit_solution(16965443320396629343)
XLA Ops:
  4.9 7.4 %all-to-all-start.1 = ((s32[16,1,12]{2,1,0:T(1,128)}), s32[16,1,12]{2,1,0:T(1,128)S(1)}, u32[]{:S(2)}, u32[]{:S(2)}) async-start(s32[16,1,12]{2,1,0:T(1,128)} %bitcast.8), calls=%async_computation.1 | async-start | bytes 16384 | tf_op jit(solution)/shard_map/all_to_all | solution.py:119
  12.2 6.5 %fusion.76 = (f32[6,8,128,1]{3,2,1,0:T(8,128)}, f32[6,8,128,1]{3,2,1,0:T(8,128)}) fusion(f32[6,8,128,128]{3,2,1,0:T(8,128)} %param.16), kind=kLoop, calls=%fused_computation.171 | loop fusion | bytes 98304 | tf_op jit(solution)/shard_map/slice | solution.py:24
  18.8 3.0 %copy.62 = f32[6,8,128,1]{2,1,3,0:T(8,128)} copy(f32[6,8,128,1]{3,2,1,0:T(8,128)} %get-tuple-element.40) | data formatting | bytes 49152
  23.2 3.0 %copy.63 = f32[6,8,128,1]{2,1,3,0:T(8,128)} copy(f32[6,8,128,1]{3,2,1,0:T(8,128)} %get-tuple-element.41) | data formatting | bytes 49152
  26.1 5.1 %collective-permute-start.1 = (f32[6,8,128,1]{2,1,3,0:T(8,128)}, f32[6,8,128,1]{2,1,3,0:T(8,128)}, u32[]{:S(2)}, u32[]{:S(2)}) collective-permute-start(f32[6,8,128,1]{2,1,3,0:T(8,128)} %copy.63), channel_id=1, source_target_pairs={{0,4},{4,8},{8,12},{1,5},{5,9},{9,13},{2,6},{6,10},{10,14},{3,7},{... | collective-permute-start | bytes 73736 | tf_op jit(solution)/shard_map/ppermute | solution.py:17
  34.3 3.6 %collective-permute-start.3 = (f32[6,8,1,128]{3,2,0,1:T(1,128)}, f32[6,8,1,128]{3,2,0,1:T(1,128)}, u32[]{:S(2)}, u32[]{:S(2)}) collective-permute-start(f32[6,8,1,128]{3,2,0,1:T(1,128)} %get-tuple-element.42), channel_id=1, source_target_pairs={{0,1},{1,2},{2,3},{4,5},{5,6},{6,7},{8,9},{9,10},{10,11},{12,13},{... | collective-permute-start | bytes 73736 | tf_op jit(solution)/shard_map/ppermute | solution.py:17
  46.2 10.4 %scatter_fusion = f32[192,8,128]{2,1,0:T(8,128)} fusion(f32[192,8,128]{2,1,0:T(8,128)} %broadcast_in_dim.26, s32[96]{0:T(128)S(1)} %fusion.55, f32[96,8,128]{2,1,0:T(8,128)} %fusion.78), kind=kCustom, calls=%fused_computation.2 | custom fusion | bytes 1180032 | tf_op jit(solution)/shard_map/scatter | solution.py:108
  56.6 5.2 %all-to-all-start = ((f32[16,12,8,128]{3,2,1,0:T(8,128)}), f32[16,12,8,128]{3,2,1,0:T(8,128)}, u32[]{:S(2)}, u32[]{:S(2)}) async-start(f32[16,12,8,128]{3,2,1,0:T(8,128)} %bitcast.274), calls=%async_computation | async-start | bytes 1572864 | tf_op jit(solution)/shard_map/all_to_all | solution.py:112
  61.8 6.5 %fusion.75 = (f32[6,8,128,127]{3,2,0,1:T(8,128)}, f32[6,8,128,127]{3,2,0,1:T(8,128)}) fusion(f32[6,8,128,128]{3,2,1,0:T(8,128)} %param.16), kind=kLoop, calls=%fused_computation.170 | loop fusion | bytes 12533760 | tf_op jit(solution)/shard_map/slice | solution.py:26
  69.6 3.0 %copy.39 = f32[6,8,128,1]{3,2,0,1:T(8,128)} copy(f32[6,8,128,1]{2,1,3,0:T(8,128)} %collective-permute-done) | data formatting | bytes 49152 | tf_op jit(solution)/shard_map/ppermute | solution.py:18
  72.6 2.9 %copy.42 = f32[6,8,128,1]{3,2,0,1:T(8,128)} copy(f32[6,8,128,1]{2,1,3,0:T(8,128)} %collective-permute-done.1) | data formatting | bytes 49152 | tf_op jit(solution)/shard_map/ppermute | solution.py:17
  75.5 11.1 %multiply_add_fusion.3 = f32[6,8,128,128]{3,2,0,1:T(8,128)} fusion(f32[6,8,128,128]{3,2,0,1:T(8,128)} %copy.48, f32[6,8,1,128]{3,2,0,1:T(1,128)} %collective-permute-done.2, f32[6,8,1,128]{3,2,0,1:T(1,128)} %collective-permute-done.3, f32[6,8,128,127]{3,2,0,1:T(8,128)} %get-tuple-element.39, f32[6,8,128,1]{3,2,0,1:T(8,128)} %copy.42, ...), kind=kLoop, calls=%fused_computation.15 | loop fusion | flops 14942208 | bytes 13746176 | tf_op jit(solution)/shard_map/add | solution.py:40
  96.2 3.9 %fusion.73 = (f32[6,8,128,1]{3,2,0,1:T(8,128)}, f32[6,8,128,1]{3,2,0,1:T(8,128)}) fusion(f32[6,8,128,128]{3,2,0,1:T(8,128)S(1)} %multiply_add_fusion.2), kind=kLoop, calls=%fused_computation.168 | loop fusion | bytes 98304 | tf_op jit(solution)/shard_map/slice | solution.py:24
  100.7 3.0 %copy.51 = f32[6,8,128,1]{2,1,3,0:T(8,128)} copy(f32[6,8,128,1]{3,2,0,1:T(8,128)} %get-tuple-element.34) | data formatting | bytes 49152 | tf_op jit(solution)/shard_map/slice | solution.py:24
  105.0 3.0 %copy.53 = f32[6,8,128,1]{2,1,3,0:T(8,128)} copy(f32[6,8,128,1]{3,2,0,1:T(8,128)} %get-tuple-element.35) | data formatting | bytes 49152 | tf_op jit(solution)/shard_map/slice | solution.py:24
  107.9 5.1 %collective-permute-start.5 = (f32[6,8,128,1]{2,1,3,0:T(8,128)}, f32[6,8,128,1]{2,1,3,0:T(8,128)}, u32[]{:S(2)}, u32[]{:S(2)}) collective-permute-start(f32[6,8,128,1]{2,1,3,0:T(8,128)} %copy.53), channel_id=1, source_target_pairs={{0,4},{4,8},{8,12},{1,5},{5,9},{9,13},{2,6},{6,10},{10,14},{3,7},{... | collective-permute-start | bytes 73736 | tf_op jit(solution)/shard_map/ppermute | solution.py:17
  114.4 3.6 %collective-permute-start.7 = (f32[6,8,1,128]{3,2,0,1:T(1,128)}, f32[6,8,1,128]{3,2,0,1:T(1,128)}, u32[]{:S(2)}, u32[]{:S(2)}) collective-permute-start(f32[6,8,1,128]{3,2,0,1:T(1,128)} %get-tuple-element.36), channel_id=1, source_target_pairs={{0,1},{1,2},{2,3},{4,5},{5,6},{6,7},{8,9},{9,10},{10,11},{12,13},{... | collective-permute-start | bytes 73736 | tf_op jit(solution)/shard_map/ppermute | solution.py:17
  118.0 6.5 %fusion.72 = (f32[6,8,128,127]{3,2,0,1:T(8,128)}, f32[6,8,128,127]{3,2,0,1:T(8,128)}) fusion(f32[6,8,128,128]{3,2,0,1:T(8,128)} %copy-done.1), kind=kLoop, calls=%fused_computation.167 | loop fusion | bytes 12484608 | tf_op jit(solution)/shard_map/slice | solution.py:26
  124.5 2.9 %copy.52 = f32[6,8,128,1]{3,2,0,1:T(8,128)} copy(f32[6,8,128,1]{2,1,3,0:T(8,128)} %collective-permute-done.4) | data formatting | bytes 49152 | tf_op jit(solution)/shard_map/ppermute | solution.py:18
  127.5 3.0 %copy.54 = f32[6,8,128,1]{3,2,0,1:T(8,128)} copy(f32[6,8,128,1]{2,1,3,0:T(8,128)} %collective-permute-done.5) | data formatting | bytes 49152 | tf_op jit(solution)/shard_map/ppermute | solution.py:17
  130.6 9.4 %multiply_add_fusion.1 = f32[6,8,128,128]{3,2,0,1:T(8,128)S(1)} fusion(f32[6,8,128,128]{3,2,0,1:T(8,128)} %copy-done.1, f32[6,8,1,128]{3,2,0,1:T(1,128)} %collective-permute-done.6, f32[6,8,1,128]{3,2,0,1:T(1,128)} %collective-permute-done.7, f32[6,8,128,127]{3,2,0,1:T(8,128)} %get-tuple-element.33, f32[6,8,128,1]{3,2,0,1:T(8,128)} %copy.54, ...), kind=kLoop, calls=%fused_computation.13 | loop fusion | flops 14942208 | bytes 13746176 | tf_op jit(solution)/shard_map/add | solution.py:40
  146.8 5.2 %all-to-all-start.2 = ((bf16[16,12,6,128]{3,1,2,0:T(8,128)(2,1)}), bf16[16,12,6,128]{3,1,2,0:T(8,128)(2,1)S(1)}, u32[]{:S(2)}, u32[]{:S(2)}) async-start(bf16[16,12,6,128]{3,1,2,0:T(8,128)(2,1)} %copy.55), calls=%async_computation.2 | async-start | bytes 786432 | tf_op jit(solution)/shard_map/all_to_all | solution.py:152
  152.1 3.9 %copy.59 = f32[6,8,128,128]{3,2,1,0:T(8,128)} copy(f32[6,8,128,128]{3,2,0,1:T(8,128)} %copy-done.4) | data formatting | bytes 6291456
  156.0 8.3 %all-to-all-done.2 = bf16[16,12,6,128]{3,1,2,0:T(8,128)(2,1)S(1)} async-done(((bf16[16,12,6,128]{3,1,2,0:T(8,128)(2,1)}), bf16[16,12,6,128]{3,1,2,0:T(8,128)(2,1)S(1)}, u32[]{:S(2)}, u32[]{:S(2)}) %all-to-all-start.2) | async-done | bytes 294944 | tf_op jit(solution)/shard_map/all_to_all | solution.py:152
  (169 shorter events, 42.4 us)
Async XLA Ops:
  0.6 40.4 %copy-start = (bf16[96,128,128]{2,1,0:T(8,128)(2,1)S(1)}, bf16[96,128,128]{2,1,0:T(8,128)(2,1)}, u32[]{:S(2)}) copy-start(bf16[96,128,128]{2,1,0:T(8,128)(2,1)} %param.12) | copy-start | bytes 9437188
  4.9 51.7 %all-to-all-start.1 = ((s32[16,1,12]{2,1,0:T(1,128)}), s32[16,1,12]{2,1,0:T(1,128)S(1)}, u32[]{:S(2)}, u32[]{:S(2)}) async-start(s32[16,1,12]{2,1,0:T(1,128)} %bitcast.8), calls=%async_computation.1 | async-start | bytes 16384 | tf_op jit(solution)/shard_map/all_to_all | solution.py:119
  18.8 19.1 %copy-start.47 = (s32[48]{0:T(128)S(1)}, s32[48]{0:T(128)}, u32[]{:S(2)}) copy-start(s32[48]{0:T(128)} %param.11) | copy-start | bytes 580
  18.8 19.2 %copy-start.48 = (s32[96]{0:T(128)S(1)}, s32[96]{0:T(128)}, u32[]{:S(2)}) copy-start(s32[96]{0:T(128)} %param.14) | copy-start | bytes 1156
  21.8 18.6 %copy-start.46 = (bf16[48,8,128]{2,1,0:T(8,128)(2,1)S(1)}, bf16[48,8,128]{2,1,0:T(8,128)(2,1)}, u32[]{:S(2)}) copy-start(bf16[48,8,128]{2,1,0:T(8,128)(2,1)} %param.10) | copy-start | bytes 294916
  21.8 47.8 %collective-permute-start = (f32[6,8,128,1]{2,1,3,0:T(8,128)}, f32[6,8,128,1]{2,1,3,0:T(8,128)}, u32[]{:S(2)}, u32[]{:S(2)}) collective-permute-start(f32[6,8,128,1]{2,1,3,0:T(8,128)} %copy.62), channel_id=1, source_target_pairs={{4,0},{8,4},{12,8},{5,1},{9,5},{13,9},{6,2},{10,6},{14,10},{7,3},{... | collective-permute-start | bytes 73736 | tf_op jit(solution)/shard_map/ppermute | solution.py:18
  26.1 46.4 %collective-permute-start.1 = (f32[6,8,128,1]{2,1,3,0:T(8,128)}, f32[6,8,128,1]{2,1,3,0:T(8,128)}, u32[]{:S(2)}, u32[]{:S(2)}) collective-permute-start(f32[6,8,128,1]{2,1,3,0:T(8,128)} %copy.63), channel_id=1, source_target_pairs={{0,4},{4,8},{8,12},{1,5},{5,9},{9,13},{2,6},{6,10},{10,14},{3,7},{... | collective-permute-start | bytes 73736 | tf_op jit(solution)/shard_map/ppermute | solution.py:17
  33.0 42.5 %collective-permute-start.2 = (f32[6,8,1,128]{3,2,0,1:T(1,128)}, f32[6,8,1,128]{3,2,0,1:T(1,128)}, u32[]{:S(2)}, u32[]{:S(2)}) collective-permute-start(f32[6,8,1,128]{3,2,0,1:T(1,128)} %get-tuple-element.43), channel_id=1, source_target_pairs={{1,0},{2,1},{3,2},{5,4},{6,5},{7,6},{9,8},{10,9},{11,10},{13,12},{... | collective-permute-start | bytes 73736 | tf_op jit(solution)/shard_map/ppermute | solution.py:18
  34.3 41.2 %collective-permute-start.3 = (f32[6,8,1,128]{3,2,0,1:T(1,128)}, f32[6,8,1,128]{3,2,0,1:T(1,128)}, u32[]{:S(2)}, u32[]{:S(2)}) collective-permute-start(f32[6,8,1,128]{3,2,0,1:T(1,128)} %get-tuple-element.42), channel_id=1, source_target_pairs={{0,1},{1,2},{2,3},{4,5},{5,6},{6,7},{8,9},{9,10},{10,11},{12,13},{... | collective-permute-start | bytes 73736 | tf_op jit(solution)/shard_map/ppermute | solution.py:17
  56.6 30.0 %all-to-all-start = ((f32[16,12,8,128]{3,2,1,0:T(8,128)}), f32[16,12,8,128]{3,2,1,0:T(8,128)}, u32[]{:S(2)}, u32[]{:S(2)}) async-start(f32[16,12,8,128]{3,2,1,0:T(8,128)} %bitcast.274), calls=%async_computation | async-start | bytes 1572864 | tf_op jit(solution)/shard_map/all_to_all | solution.py:112
  103.7 20.8 %collective-permute-start.4 = (f32[6,8,128,1]{2,1,3,0:T(8,128)}, f32[6,8,128,1]{2,1,3,0:T(8,128)}, u32[]{:S(2)}, u32[]{:S(2)}) collective-permute-start(f32[6,8,128,1]{2,1,3,0:T(8,128)} %copy.51), channel_id=1, source_target_pairs={{4,0},{8,4},{12,8},{5,1},{9,5},{13,9},{6,2},{10,6},{14,10},{7,3},{... | collective-permute-start | bytes 73736 | tf_op jit(solution)/shard_map/ppermute | solution.py:18
  107.9 19.5 %collective-permute-start.5 = (f32[6,8,128,1]{2,1,3,0:T(8,128)}, f32[6,8,128,1]{2,1,3,0:T(8,128)}, u32[]{:S(2)}, u32[]{:S(2)}) collective-permute-start(f32[6,8,128,1]{2,1,3,0:T(8,128)} %copy.53), channel_id=1, source_target_pairs={{0,4},{4,8},{8,12},{1,5},{5,9},{9,13},{2,6},{6,10},{10,14},{3,7},{... | collective-permute-start | bytes 73736 | tf_op jit(solution)/shard_map/ppermute | solution.py:17
  113.1 17.3 %collective-permute-start.6 = (f32[6,8,1,128]{3,2,0,1:T(1,128)}, f32[6,8,1,128]{3,2,0,1:T(1,128)}, u32[]{:S(2)}, u32[]{:S(2)}) collective-permute-start(f32[6,8,1,128]{3,2,0,1:T(1,128)} %get-tuple-element.37), channel_id=1, source_target_pairs={{1,0},{2,1},{3,2},{5,4},{6,5},{7,6},{9,8},{10,9},{11,10},{13,12},{... | collective-permute-start | bytes 73736 | tf_op jit(solution)/shard_map/ppermute | solution.py:18
  114.4 16.1 %collective-permute-start.7 = (f32[6,8,1,128]{3,2,0,1:T(1,128)}, f32[6,8,1,128]{3,2,0,1:T(1,128)}, u32[]{:S(2)}, u32[]{:S(2)}) collective-permute-start(f32[6,8,1,128]{3,2,0,1:T(1,128)} %get-tuple-element.36), channel_id=1, source_target_pairs={{0,1},{1,2},{2,3},{4,5},{5,6},{6,7},{8,9},{9,10},{10,11},{12,13},{... | collective-permute-start | bytes 73736 | tf_op jit(solution)/shard_map/ppermute | solution.py:17
  130.4 9.6 %copy-start.8 = (f32[1,128,128]{2,1,0:T(8,128)S(1)}, f32[1,128,128]{2,1,0:T(8,128)}, u32[]{:S(2)}) copy-start(f32[1,128,128]{2,1,0:T(8,128)} %copy-done.7) | copy-start | bytes 196612
  130.4 9.6 %copy-start.10 = (f32[1,128,128]{2,1,0:T(8,128)S(1)}, f32[1,128,128]{2,1,0:T(8,128)}, u32[]{:S(2)}) copy-start(f32[1,128,128]{2,1,0:T(8,128)} %copy-done.9) | copy-start | bytes 196612
  130.5 9.6 %copy-start.12 = (f32[1,128,128]{2,1,0:T(8,128)S(1)}, f32[1,128,128]{2,1,0:T(8,128)}, u32[]{:S(2)}) copy-start(f32[1,128,128]{2,1,0:T(8,128)} %copy-done.11) | copy-start | bytes 196612
  130.5 9.6 %copy-start.14 = (f32[1,128,128]{2,1,0:T(8,128)S(1)}, f32[1,128,128]{2,1,0:T(8,128)}, u32[]{:S(2)}) copy-start(f32[1,128,128]{2,1,0:T(8,128)} %copy-done.13) | copy-start | bytes 196612
  130.5 9.6 %copy-start.16 = (f32[1,128,128]{2,1,0:T(8,128)S(1)}, f32[1,128,128]{2,1,0:T(8,128)}, u32[]{:S(2)}) copy-start(f32[1,128,128]{2,1,0:T(8,128)} %copy-done.15) | copy-start | bytes 196612
  130.5 9.6 %copy-start.18 = (f32[1,128,128]{2,1,0:T(8,128)S(1)}, f32[1,128,128]{2,1,0:T(8,128)}, u32[]{:S(2)}) copy-start(f32[1,128,128]{2,1,0:T(8,128)} %copy-done.17) | copy-start | bytes 196612
  130.5 9.6 %copy-start.22 = (f32[128,128]{1,0:T(8,128)S(1)}, f32[128,128]{1,0:T(8,128)}, u32[]{:S(2)}) copy-start(f32[128,128]{1,0:T(8,128)} %get-tuple-element.61) | copy-start | bytes 196612
  130.5 9.6 %copy-start.24 = (f32[128,128]{1,0:T(8,128)S(1)}, f32[128,128]{1,0:T(8,128)}, u32[]{:S(2)}) copy-start(f32[128,128]{1,0:T(8,128)} %copy-done.23) | copy-start | bytes 196612
  146.8 17.5 %all-to-all-start.2 = ((bf16[16,12,6,128]{3,1,2,0:T(8,128)(2,1)}), bf16[16,12,6,128]{3,1,2,0:T(8,128)(2,1)S(1)}, u32[]{:S(2)}, u32[]{:S(2)}) async-start(bf16[16,12,6,128]{3,1,2,0:T(8,128)(2,1)} %copy.55), calls=%async_computation.2 | async-start | bytes 786432 | tf_op jit(solution)/shard_map/all_to_all | solution.py:152
  156.0 12.5 %copy-start.49 = (s32[96]{0:T(128)S(1)}, s32[96]{0:T(128)}, u32[]{:S(2)}) copy-start(s32[96]{0:T(128)} %param.14) | copy-start | bytes 1156
  (37 other events, 192.4 us)
where the time goes:
time: 171 us; the launch traced here: 169 us
  local copies, waits for them, and re-layouts  79.1 us (46%)
  starting transfers between devices  40.6 us (24%)
  other arithmetic  32.7 us (19%)
  waiting for transfers between devices  8.3 us (5%)
  matrix products  7.19 us (4%)
    add x2, other arithmetic, advect_rows(): return centre + sea_mask * tendency  20.5 us
    ppermute x4, starting transfers between devices, with_halo(): before = lax.ppermute(last, axis, up)  17.6 us
    slice x4, local copies, waits for them, and re-layouts, column_sides(): edges = jnp.concatenate([centre[..., :1], centre[..., -1:]], axis=-1)  16.4 us
    unnamed x110, local copies, waits for them, and re-layouts  14.7 us
    slice x2, local copies, waits for them, and re-layouts, column_sides(): east_cell = jnp.concatenate([centre[..., 1:], widened[..., 3:]], axis=-1)  13 us
    scatter x1, local copies, waits for them, and re-layouts, on_device(): outgoing = jnp.zeros((node_count * capacity, fields, tile_width), jnp.flo...  10.4 us
    all_to_all x1, waiting for transfers between devices, on_device(): lax.all_to_all(reply_rows, ('tx', 'ty', 'tz'), split_axis=0, concat_axis=...  8.27 us
    all_to_all x1, starting transfers between devices, on_device(): lax.all_to_all(out_rows.reshape(node_count, capacity), ('tx', 'ty', 'tz')...  7.36 us
  transfers between devices with their start and end apart: 11, of which 1 were waited for; matrix products, arithmetic and copies ran while one was open for 45% of the time, Pallas kernels for 0%

commit v1 on v0

v1 whole, which is shorter than its diff:
```python
import functools

import jax
import jax.numpy as jnp
from jax import lax
from jax.experimental import pallas as pl
from jax.experimental.pallas import tpu as pltpu
from jax.sharding import PartitionSpec as P

DIFFUSION = 0.2
FORCING = 0.5
F32 = jnp.float32
BF16 = jnp.bfloat16
AXES = ("tx", "ty", "tz")
PAD = 8
CHUNKS = 4


def vmem():
    return pl.BlockSpec(memory_space=pltpu.VMEM)


def smem():
    return pl.BlockSpec(memory_space=pltpu.SMEM)


def hbm():
    return pl.BlockSpec(memory_space=pl.ANY)


def params():
    return pltpu.CompilerParams(vmem_limit_bytes=44 * 2**20)


def lane_iota(shape):
    return lax.broadcasted_iota(jnp.int32, shape, len(shape) - 1)


def contrib_kernel(
    info_ref, dest_ref, atm_ref, row_ref, rows_ref, flux_ref, weights_ref,
    out_ref, slot_ref, masked, message, count,
    *, nodes, cap, window, per_step, message_rows,
):
    step = pl.program_id(0)
    fields = flux_ref.shape[1]
    lanes = flux_ref.shape[2]

    @pl.when(step == 0)
    def _():
        message[...] = jnp.zeros(message.shape, F32)
        lane = lane_iota((fields, lanes))

        def clear(n, carry):
            count[n] = 0
            return carry

        lax.fori_loop(0, nodes, clear, 0)

        def mask(b, carry):
            masked[b] = jnp.where(lane < rows_ref[b], flux_ref[b].astype(F32), 0.0)
            return carry

        lax.fori_loop(0, flux_ref.shape[0], mask, 0, unroll=8)

        base = lax.rem(info_ref[6], 128 // window) * window
        lane8 = lane_iota((8, 128))

        def place(p, carry):
            d = dest_ref[p]
            s = count[d]
            count[d] = s + 1
            slot_ref[p] = d * cap + s
            start = pl.multiple_of(d * message_rows + cap * fields, 8)
            tile = message[pl.ds(start, 8), :]
            named = (row_ref[p] + 1).astype(F32)
            message[pl.ds(start, 8), :] = jnp.where(lane8 == base + s, named, tile)
            return carry

        lax.fori_loop(0, dest_ref.shape[0], place, 0, unroll=4)

    for j in range(per_step):
        p = step * per_step + j
        slot = slot_ref[p]
        d = slot // cap
        s = slot - d * cap
        lhs = masked[atm_ref[p]].astype(BF16)
        product = jnp.dot(lhs, weights_ref[j], preferred_element_type=F32)
        start = pl.multiple_of(d * message_rows + s * fields, 8)
        message[pl.ds(start, fields), :] = product

    @pl.when(step == pl.num_programs(0) - 1)
    def _():
        for d in range(nodes):
            out_ref[d] = message[d * message_rows : (d + 1) * message_rows, :].astype(BF16)


def contributions(info, dest, atm, row, rows, flux, weights, nodes, cap, window):
    pairs, cells, width = weights.shape
    fields = flux.shape[1]
    message_rows = cap * fields + 8
    steps = 4
    per_step = pairs // steps
    fixed3 = lambda i: (0, 0, 0)
    return pl.pallas_call(
        functools.partial(
            contrib_kernel, nodes=nodes, cap=cap, window=window,
            per_step=per_step, message_rows=message_rows,
        ),
        grid=(steps,),
        out_shape=(
            jax.ShapeDtypeStruct((nodes, message_rows, width), BF16),
            jax.ShapeDtypeStruct((pairs,), jnp.int32),
        ),
        in_specs=[smem()] * 5
        + [
            pl.BlockSpec(flux.shape, fixed3),
            pl.BlockSpec((per_step, cells, width), lambda i: (i, 0, 0)),
        ],
        out_specs=(pl.BlockSpec((nodes, message_rows, width), fixed3), smem()),
        scratch_shapes=[
            pltpu.VMEM(flux.shape, F32),
            pltpu.VMEM((nodes * message_rows, width), F32),
            pltpu.SMEM((nodes,), jnp.int32),
        ],
        compiler_params=params(),
        name="contributions",
    )(info, dest, atm, row, rows, flux, weights)


def column_lines(collected):
    return collected.T


def store_sends(info_ref, lines_ref, row_first, row_last, sends):
    count = sends[0].shape[0]
    east = lines_ref[pl.ds(1, count, stride=2), :]
    west = lines_ref[pl.ds(2, count, stride=2), :]
    tx_even = info_ref[0] == 1
    g_even = info_ref[3] == 1
    sends[0][...] = jnp.where(tx_even, east, west)
    sends[1][...] = jnp.where(tx_even, west, east)
    sends[2][...] = jnp.where(g_even, row_last, row_first)
    sends[3][...] = jnp.where(g_even, row_first, row_last)


def edges_kernel(info_ref, order_ref, c_ref, s0, s1, s2, s3, cols, lines):
    del order_ref
    count, height, width = c_ref.shape
    lane = lane_iota((8, width))

    def body(i, carry):
        r = pl.multiple_of(i * 8, 8)
        acc = jnp.zeros((8, width), F32)
        for tl in range(count):
            moved = pltpu.roll(c_ref[tl, pl.ds(r, 8), :], (2 * tl + 2) % width, 1)
            acc = jnp.where((lane == 2 * tl + 1) | (lane == 2 * tl + 2), moved, acc)
        cols[pl.ds(r, 8), :] = acc
        return carry

    lax.fori_loop(0, height // 8, body, 0)
    lines[...] = cols[...].T
    store_sends(
        info_ref, lines, c_ref[:, 0, :], c_ref[:, height - 1, :], (s0, s1, s2, s3)
    )


def edges(info, order, state):
    count, height, width = state.shape
    line = jax.ShapeDtypeStruct((count, width), F32)
    return pl.pallas_call(
        edges_kernel,
        out_shape=(line,) * 4,
        in_specs=[smem(), hbm(), vmem()],
        out_specs=(vmem(),) * 4,
        scratch_shapes=[pltpu.VMEM((height, width), F32), pltpu.VMEM((width, height), F32)],
        compiler_params=params(),
        name="edges",
    )(info, order, state)


def exchange(lines, mesh_sizes):
    n_tx, n_ty, n_tz = mesh_sizes
    groups = n_ty * n_tz
    perms = [[], [], [], []]
    for x in range(n_tx):
        for g in range(groups):
            here = x * groups + g
            perms[0].append((here, (x ^ 1) * groups + g))
            inner_x = x + 1 if x % 2 == 1 else x - 1
            if 0 <= inner_x < n_tx:
                perms[1].append((here, inner_x * groups + g))
            else:
                perms[1].append((here, x * groups + (g ^ 1)))
            perms[2].append((here, x * groups + (g ^ 1)))
            inner_g = g + 1 if g % 2 == 1 else g - 1
            perms[3].append((here, x * groups + inner_g % groups))
    return [lax.ppermute(line, AXES, perm) for line, perm in zip(lines, perms)]


def place_halos(info_ref, received, padded, lines, sides):
    count = padded.shape[0]
    height = padded.shape[1] - 2 * PAD
    tx_even = info_ref[0] == 1
    g_even = info_ref[3] == 1
    zero = jnp.zeros(received[0].shape, F32)
    r0, r1, r2, r3 = (r[...] for r in received)
    r1 = jnp.where(info_ref[1] == 1, zero, r1)
    r3 = jnp.where(info_ref[4] == 1, zero, r3)
    lines[...] = jnp.zeros(lines.shape, F32)
    lines[pl.ds(1, count, stride=2), :] = jnp.where(tx_even, r0, r1)
    lines[pl.ds(2, count, stride=2), :] = jnp.where(tx_even, r1, r0)
    sides[...] = lines[...].T
    north = jnp.where(g_even, r2, r3)
    south = jnp.where(g_even, r3, r2)
    for tl in range(count):
        padded[tl, PAD + height : PAD + height + 1, :] = north[tl : tl + 1, :]
        padded[tl, PAD - 1 : PAD, :] = south[tl : tl + 1, :]


def shift_matrix(width):
    k = lax.broadcasted_iota(jnp.int32, (2 * width, 2 * width), 0) % width
    n = lax.broadcasted_iota(jnp.int32, (2 * width, 2 * width), 1)
    j = n % width
    east = jnp.where(k == j + 1, 1.0, 0.0)
    west = jnp.where(k == j - 1, 1.0, 0.0)
    here = jnp.where(k == j, 4.0, 0.0)
    return jnp.where(n < width, east - west, east + west - here).astype(BF16)


def sweep(padded, u_ref, v_ref, k_ref, land_ref, ip_ref, sides, shifted, matrix, wait, finish, levels):
    count, padded_height, width = padded.shape
    height = padded_height - 2 * PAD
    tracers = count // levels
    rows = height // CHUNKS
    lane = lane_iota((8, width))
    matrix[...] = shift_matrix(width)
    wait(0)
    for chunk in range(CHUNKS):
        if chunk + 1 < CHUNKS:
            wait(chunk + 1)
        first = chunk * rows
        x = padded[:, PAD + first : PAD + first + rows, :].reshape(count * rows, width)
        high = x.astype(BF16)
        low = (x - high.astype(F32)).astype(BF16)
        both = jnp.concatenate([high, low], axis=1)
        shifted[...] = jnp.dot(both, matrix[...], preferred_element_type=F32).reshape(
            count, rows, 2 * width
        )

        def block(i, carry):
            r = pl.multiple_of(first + i * 8, 8)
            local = pl.multiple_of(i * 8, 8)
            sea = land_ref[pl.ds(r, 8), :].astype(F32)
            side = sides[pl.ds(r, 8), :]
            diffuse = DIFFUSION * sea
            q = [None] * tracers
            for level in range(levels - 1, -1, -1):
                half_u = 0.5 * sea * u_ref[level, pl.ds(r, 8), :]
                half_v = 0.5 * sea * v_ref[level, pl.ds(r, 8), :]
                c_north = diffuse - half_v
                c_south = diffuse + half_v
                c_side = jnp.where(
                    lane == 0,
                    diffuse + half_u,
                    jnp.where(lane == width - 1, diffuse - half_u, 0.0),
                )
                if level >= 1 and level < levels - 1:
                    link = k_ref[level, pl.ds(r, 8), :] * sea
                if level >= 2:
                    inverse = ip_ref[level, pl.ds(r, 8), :]
                tops = []
                for t in range(tracers):
                    tl = t * levels + level
                    c = padded[tl, pl.ds(PAD + r, 8), :]
                    north = padded[tl, pl.ds(PAD + r + 1, 8), :]
                    south = padded[tl, pl.ds(PAD + r - 1, 8), :]
                    odd = shifted[tl, pl.ds(local, 8), :width]
                    even = shifted[tl, pl.ds(local, 8), width:]
                    halo = pltpu.roll(side, (width - (2 * tl + 2)) % width, 1)
                    rhs = (c - half_u * odd) + diffuse * even
                    rhs = rhs + (c_north * north + c_south * south) + c_side * halo
                    if level == levels - 1:
                        q[t] = rhs * inverse
                    elif level >= 2:
                        q[t] = (rhs + link * q[t]) * inverse
                    elif level == 1:
                        q[t] = rhs + link * q[t]
                    tops.append(rhs)
                if level >= 1:
                    finish(level, r, q, None)
                else:
                    finish(0, r, q, tops)
            return carry

        lax.fori_loop(0, rows // 8, block, 0)


def load_padded(source, padded, sems):
    height = source.shape[1]
    rows = height // CHUNKS
    copies = [
        pltpu.make_async_copy(
            source.at[:, pl.ds(n * rows, rows), :],
            padded.at[:, pl.ds(PAD + n * rows, rows), :],
            sems.at[n],
        )
        for n in range(CHUNKS)
    ]
    for copy in copies:
        copy.start()
    return lambda n: copies[n].wait()


def first_kernel(
    info_ref, c_hbm, r0, r1, r2, r3, u_ref, v_ref, k_ref, land_ref,
    q_ref, ip_ref, padded, shifted, matrix, lines, sides, sems, *, levels,
):
    wait = load_padded(c_hbm, padded, sems)
    place_halos(info_ref, (r0, r1, r2, r3), padded, lines, sides)
    sea = land_ref[...].astype(F32)
    below = None
    for level in range(levels - 1, 1, -1):
        upper = k_ref[level - 1] * sea
        if below is None:
            pivot = 1.0 + upper
        else:
            lower = k_ref[level] * sea
            pivot = 1.0 + upper + lower - lower * lower * below
        below = 1.0 / pivot
        ip_ref[level] = below
    lower = k_ref[1] * sea
    ip_ref[1] = 1.0 + lower - lower * lower * below
    ip_ref[0] = k_ref[0] * sea

    def finish(level, r, q, tops):
        values = q if level > 0 else tops
        for t, value in enumerate(values):
            q_ref[t * levels + level, pl.ds(r, 8), :] = value

    sweep(padded, u_ref, v_ref, k_ref, land_ref, ip_ref, sides, shifted, matrix, wait, finish, levels)


def sweep_scratch(count, height, width):
    return [
        pltpu.VMEM((count, height + 2 * PAD, width), F32),
        pltpu.VMEM((count, height // CHUNKS, 2 * width), F32),
        pltpu.VMEM((2 * width, 2 * width), BF16),
        pltpu.VMEM((width, height), F32),
        pltpu.VMEM((height, width), F32),
        pltpu.SemaphoreType.DMA((CHUNKS,)),
    ]


def first_part(info, state, received, velocity, mixing, land, levels):
    count, height, width = state.shape
    return pl.pallas_call(
        functools.partial(first_kernel, levels=levels),
        out_shape=(
            jax.ShapeDtypeStruct((count, height, width), F32),
            jax.ShapeDtypeStruct((levels, height, width), F32),
        ),
        in_specs=[smem(), hbm()] + [vmem()] * 8,
        out_specs=(vmem(), vmem()),
        scratch_shapes=sweep_scratch(count, height, width),
        compiler_params=params(),
        name="first_part",
    )(info, state, *received, velocity[0], velocity[1], mixing, land)


def middle_kernel(
    info_ref, incoming_ref, q_hbm, ip_ref, k_ref, land_ref,
    x_ref, coef_ref, pick_ref, s0, s1, s2, s3,
    q_ref, wide, flux, cols, lines, sems, *, levels, cap, window,
):
    count, height, width = q_ref.shape
    tracers = count // levels
    nodes, message_rows, _ = incoming_ref.shape
    fields = flux.shape[0]
    rows = height // CHUNKS
    copies = [
        pltpu.make_async_copy(
            q_hbm.at[:, pl.ds(n * rows, rows), :],
            q_ref.at[:, pl.ds(n * rows, rows), :],
            sems.at[n],
        )
        for n in range(CHUNKS)
    ]
    for copy in copies:
        copy.start()
    span = nodes * message_rows
    wide[span:, :] = jnp.zeros((wide.shape[0] - span, width), F32)
    for n in range(nodes):
        wide[n * message_rows : (n + 1) * message_rows, :] = incoming_ref[n].astype(F32)
    per_group = 128 // window
    groups = -(-nodes // per_group)
    row_number = (lax.broadcasted_iota(jnp.int32, (height, 128), 0) + 1).astype(F32)
    selectors = []
    for g in range(groups):
        ids = jnp.zeros((1, 128), F32)
        for n in range(g * per_group, min(nodes, (g + 1) * per_group)):
            at = n * message_rows + cap * fields
            ids = ids + wide[at : at + 1, :]
        chosen = jnp.where(ids == row_number, 1.0, 0.0)
        selectors.append(chosen.astype(BF16))
        pick_ref[g * 128 : (g + 1) * 128, :] = chosen.T.astype(BF16)
    selector = jnp.concatenate(selectors, axis=1)
    for f in range(fields):
        pieces = [
            wide[pl.ds(n * message_rows + f, window, stride=fields), :] for n in range(nodes)
        ]
        for n in range(nodes, groups * per_group):
            pieces.append(jnp.zeros((window, width), F32))
        stacked = jnp.concatenate(pieces, axis=0).astype(BF16)
        flux[f] = jnp.dot(selector, stacked, preferred_element_type=F32)
    sea = land_ref[...].astype(F32)
    stirring = 1.0 + 0.5 * (
        flux[fields - 2] * flux[fields - 2] + flux[fields - 1] * flux[fields - 1]
    )
    top_link = ip_ref[0] * stirring
    inverse1 = 1.0 / (ip_ref[1] + top_link)
    inverse0 = 1.0 / (1.0 + top_link - top_link * top_link * inverse1)
    coef_ref[tracers] = top_link
    coef_ref[tracers + 1] = inverse1
    coef_ref[tracers + 2] = inverse0
    for t in range(tracers):
        coef_ref[t] = FORCING * sea * flux[t]
    lane = lane_iota((8, width))
    for chunk in range(CHUNKS):
        copies[chunk].wait()
        first = chunk * rows

        def block(i, carry):
            r = pl.multiple_of(first + i * 8, 8)
            here = pl.ds(r, 8)
            sea8 = land_ref[here, :].astype(F32)
            link0 = coef_ref[tracers, here, :]
            inv1 = coef_ref[tracers + 1, here, :]
            inv0 = coef_ref[tracers + 2, here, :]
            down = [None, link0 * inv1]
            for level in range(2, levels):
                down.append(k_ref[level - 1, here, :] * sea8 * ip_ref[level, here, :])
            acc = jnp.zeros((8, width), F32)
            for t in range(tracers):
                base = t * levels
                q1 = q_ref[base + 1, here, :] * inv1
                x = (q_ref[base, here, :] + coef_ref[t, here, :] + link0 * q1) * inv0
                for level in range(levels):
                    tl = base + level
                    if level == 1:
                        x = q1 + down[1] * x
                    elif level > 1:
                        x = q_ref[tl, here, :] + down[level] * x
                    x_ref[tl, here, :] = x
                    moved = pltpu.roll(x, (2 * tl + 2) % width, 1)
                    acc = jnp.where((lane == 2 * tl + 1) | (lane == 2 * tl + 2), moved, acc)
            cols[here, :] = acc
            return carry

        lax.fori_loop(0, rows // 8, block, 0)
    lines[...] = cols[...].T
    store_sends(
        info_ref, lines, x_ref[:, 0, :], x_ref[:, height - 1, :], (s0, s1, s2, s3)
    )


def middle_part(info, incoming, q, ip, mixing, land, fields, levels, cap, window):
    count, height, width = q.shape
    nodes, message_rows, _ = incoming.shape
    tracers = count // levels
    groups = -(-nodes // (128 // window))
    line = jax.ShapeDtypeStruct((count, width), F32)
    return pl.pallas_call(
        functools.partial(middle_kernel, levels=levels, cap=cap, window=window),
        out_shape=(
            jax.ShapeDtypeStruct((count, height, width), F32),
            jax.ShapeDtypeStruct((tracers + 3, height, width), F32),
            jax.ShapeDtypeStruct((groups * 128, height), BF16),
            line, line, line, line,
        ),
        in_specs=[smem(), vmem(), hbm(), vmem(), vmem(), vmem()],
        out_specs=(vmem(),) * 7,
        scratch_shapes=[
            pltpu.VMEM((count, height, width), F32),
            pltpu.VMEM((nodes * message_rows + window * fields, width), F32),
            pltpu.VMEM((fields, height, width), F32),
            pltpu.VMEM((height, width), F32),
            pltpu.VMEM((width, height), F32),
            pltpu.SemaphoreType.DMA((CHUNKS,)),
        ],
        compiler_params=params(),
        name="middle_part",
    )(info, incoming, q, ip, mixing, land)


def top_level(coef_ref, here, t, tracers, q1, rhs):
    inv1 = coef_ref[tracers + 1, here, :]
    link0 = coef_ref[tracers, here, :]
    q1 = q1 * inv1
    top = (rhs + coef_ref[t, here, :] + link0 * q1) * coef_ref[tracers + 2, here, :]
    return q1, top


def reply_kernel(
    info_ref, c_hbm, r0, r1, r2, r3, u_ref, v_ref, k_ref, land_ref, ip_ref, coef_ref, pick_ref,
    out_ref, padded, shifted, matrix, lines, sides, sems, top, rows_out,
    *, levels, cap, window,
):
    tracers = top.shape[0]
    height = top.shape[1]
    wait = load_padded(c_hbm, padded, sems)
    place_halos(info_ref, (r0, r1, r2, r3), padded, lines, sides)

    def finish(level, r, q, tops):
        if level == 0:
            here = pl.ds(r, 8)
            sea = land_ref[here, :].astype(F32)
            for t in range(tracers):
                _, x = top_level(coef_ref, here, t, tracers, q[t], tops[t])
                top[t, here, :] = x * sea

    sweep(padded, u_ref, v_ref, k_ref, land_ref, ip_ref, sides, shifted, matrix, wait, finish, levels)
    nodes = out_ref.shape[0]
    per = cap * tracers
    picked = pick_ref[...]
    for t in range(tracers):
        rows = jnp.dot(picked, top[t].astype(BF16), preferred_element_type=F32)
        for n in range(nodes):
            rows_out[pl.ds(n * per + t, cap, stride=tracers), :] = rows[
                n * window : n * window + cap, :
            ]
    for n in range(nodes):
        out_ref[n] = rows_out[n * per : (n + 1) * per, :].astype(BF16)


def replies(info, state, received, velocity, mixing, land, ip, coef, pick, nodes, levels, cap, window):
    count, height, width = state.shape
    tracers = count // levels
    return pl.pallas_call(
        functools.partial(reply_kernel, levels=levels, cap=cap, window=window),
        out_shape=jax.ShapeDtypeStruct((nodes, cap * tracers, width), BF16),
        in_specs=[smem(), hbm()] + [vmem()] * 11,
        out_specs=vmem(),
        scratch_shapes=sweep_scratch(count, height, width)
        + [
            pltpu.VMEM((tracers, height, width), F32),
            pltpu.VMEM((nodes * cap * tracers, width), F32),
        ],
        compiler_params=params(),
        name="replies",
    )(info, state, *received, velocity[0], velocity[1], mixing, land, ip, coef, pick)


def last_kernel(
    info_ref, order_ref, c_hbm, r0, r1, r2, r3, u_ref, v_ref, k_ref, land_ref, ip_ref, coef_ref,
    out_ref, padded, shifted, matrix, lines, sides, sems, *, levels,
):
    del order_ref
    count = out_ref.shape[0]
    tracers = count // levels
    wait = load_padded(c_hbm, padded, sems)
    place_halos(info_ref, (r0, r1, r2, r3), padded, lines, sides)

    def finish(level, r, q, tops):
        here = pl.ds(r, 8)
        if level >= 2:
            for t in range(tracers):
                out_ref[t * levels + level, here, :] = q[t]
        if level == 0:
            sea = land_ref[here, :].astype(F32)
            down = [None, coef_ref[tracers, here, :] * coef_ref[tracers + 1, here, :]]
            for lower in range(2, levels):
                down.append(k_ref[lower - 1, here, :] * sea * ip_ref[lower, here, :])
            for t in range(tracers):
                q1, x = top_level(coef_ref, here, t, tracers, q[t], tops[t])
                out_ref[t * levels, here, :] = x
                x = q1 + down[1] * x
                out_ref[t * levels + 1, here, :] = x
                for lower in range(2, levels):
                    x = out_ref[t * levels + lower, here, :] + down[lower] * x
                    out_ref[t * levels + lower, here, :] = x

    sweep(padded, u_ref, v_ref, k_ref, land_ref, ip_ref, sides, shifted, matrix, wait, finish, levels)


def last_part(info, order, state, received, velocity, mixing, land, ip, coef, levels):
    count, height, width = state.shape
    return pl.pallas_call(
        functools.partial(last_kernel, levels=levels),
        out_shape=jax.ShapeDtypeStruct((count, height, width), F32),
        in_specs=[smem(), hbm(), hbm()] + [vmem()] * 10,
        out_specs=vmem(),
        scratch_shapes=sweep_scratch(count, height, width),
        compiler_params=params(),
        name="last_part",
    )(info, order, state, *received, velocity[0], velocity[1], mixing, land, ip, coef)


def back_kernel(
    slot_ref, atm_ref, rows_ref, returned_ref, weights_ref, out_ref, wide, total,
    *, per_step, tracers, cells,
):
    step = pl.program_id(0)
    nodes, per, width = returned_ref.shape

    @pl.when(step == 0)
    def _():
        total[...] = jnp.zeros(total.shape, F32)
        wide[nodes * per :, :] = jnp.zeros((wide.shape[0] - nodes * per, width), F32)
        for n in range(nodes):
            wide[n * per : (n + 1) * per, :] = returned_ref[n].astype(F32)

    for j in range(per_step):
        p = step * per_step + j
        lhs = wide[pl.ds(slot_ref[p] * tracers, 8), :].astype(BF16)
        product = lax.dot_general(
            lhs, weights_ref[j], (((1,), (1,)), ((), ())), preferred_element_type=F32
        )
        b = atm_ref[p]
        total[b] = total[b] + product

    @pl.when(step == pl.num_programs(0) - 1)
    def _():
        lane = lane_iota((tracers, cells))

        def write(b, carry):
            out_ref[b] = jnp.where(lane < rows_ref[b], total[b][:tracers], 0.0)
            return carry

        lax.fori_loop(0, out_ref.shape[0], write, 0, unroll=8)


def back(slots, atm, rows, returned, weights, tracers):
    pairs, cells, width = weights.shape
    nodes, per, _ = returned.shape
    blocks = rows.shape[0]
    steps = 4
    per_step = pairs // steps
    fixed3 = lambda i: (0, 0, 0)
    return pl.pallas_call(
        functools.partial(back_kernel, per_step=per_step, tracers=tracers, cells=cells),
        grid=(steps,),
        out_shape=jax.ShapeDtypeStruct((blocks, tracers, cells), F32),
        in_specs=[smem()] * 3
        + [
            pl.BlockSpec(returned.shape, fixed3),
            pl.BlockSpec((per_step, cells, width), lambda i: (i, 0, 0)),
        ],
        out_specs=pl.BlockSpec((blocks, tracers, cells), fixed3),
        scratch_shapes=[
            pltpu.VMEM((nodes * per + 8, width), F32),
            pltpu.VMEM((blocks, 8, cells), F32),
        ],
        compiler_params=params(),
        name="back",
    )(slots, atm, rows, returned, weights)


def all_to_all(x):
    return lax.all_to_all(x, AXES, split_axis=0, concat_axis=0, tiled=True)


def on_device(
    atm_flux,
    atm_rows,
    regrid_weights,
    pair_dest,
    pair_atm,
    pair_row,
    tracers,
    velocity,
    mixing,
    land,
    *,
    mesh_sizes,
):
    n_tx, n_ty, n_tz = mesh_sizes
    groups = n_ty * n_tz
    nodes = n_tx * groups
    pairs = pair_atm.shape[0]
    cap = max(2, (2 * pairs + nodes - 1) // nodes)
    window = -(-cap // 8) * 8
    fields = atm_flux.shape[1]
    tracer_count, levels, height, width = tracers.shape
    tx = lax.axis_index("tx")
    group = lax.axis_index("ty") * n_tz + lax.axis_index("tz")
    info = jnp.stack(
        [
            (tx % 2 == 0),
            (tx == 0) | (tx == n_tx - 1),
            tx == n_tx - 1,
            (group % 2 == 0),
            (group == 0) | (group == groups - 1),
            group == groups - 1,
            tx * groups + group,
            0,
        ]
    ).astype(jnp.int32)
    state = tracers.reshape(tracer_count * levels, height, width)
    message, slots = contributions(
        info, pair_dest[:, 0], pair_atm, pair_row, atm_rows, atm_flux, regrid_weights,
        nodes, cap, window,
    )
    incoming = all_to_all(message)
    received = exchange(edges(info, slots, state), mesh_sizes)
    q, ip = first_part(info, state, received, velocity, mixing, land, levels)
    state, coef, pick, *lines = middle_part(
        info, incoming, q, ip, mixing, land, fields, levels, cap, window
    )
    received = exchange(lines, mesh_sizes)
    answer = replies(
        info, state, received, velocity, mixing, land, ip, coef, pick, nodes, levels, cap, window
    )
    returned = all_to_all(answer)
    out = last_part(info, answer, state, received, velocity, mixing, land, ip, coef, levels)
    atm_surface = back(slots, pair_atm, atm_rows, returned, regrid_weights, tracer_count)
    return (out.reshape(tracers.shape), atm_surface)


def solution(mesh):
    in_specs = (
        P(("ens", "tx", "ty", "tz"), None, None),
        P(("tx", "ty", "tz")),
        P(("tx", "ty", "tz"), None, None),
        P(("tx", "ty", "tz"), None),
        P(("tx", "ty", "tz")),
        P(("tx", "ty", "tz")),
        P("ens", None, ("ty", "tz"), "tx"),
        P("ens", None, ("ty", "tz"), "tx"),
        P("ens", ("ty", "tz"), "tx"),
        P(("ty", "tz"), "tx"),
    )
    out_specs = (P("ens", None, ("ty", "tz"), "tx"), P(("ens", "tx", "ty", "tz"), None, None))
    mesh_sizes = tuple(mesh.shape[name] for name in AXES)
    return jax.shard_map(
        functools.partial(on_device, mesh_sizes=mesh_sizes),
        mesh=mesh, in_specs=in_specs, out_specs=out_specs, check_vma=False,
    )
```

time: 171 us -> 91.4 us (0.53)
  local copies, waits for them, and re-layouts: 79.1 us -> 30.2 us
  Pallas kernels: 0 us -> 32.7 us
  other arithmetic: 32.7 us -> 0 us
  starting transfers between devices: 40.6 us -> 22 us
  matrix products: 7.19 us -> 0 us
  waiting for transfers between devices: 8.3 us -> 4.71 us
    pallas_call x0 -> x7, Pallas kernels: none -> 32.7 us  [the longest x1 7.72 us: last_part(): pl.pallas_call(functools.partial(last_kernel, levels=levels), out_shape=j...]
    slice x8 -> x0, local copies, waits for them, and re-layouts: 31.7 us -> none  [the longest x4 16.4 us: column_sides(): edges = jnp.concatenate([centre[..., :1], centre[..., -1:]], axis=-1)]
    add x4 -> x0, other arithmetic: 21.9 us -> none  [the longest x2 20.5 us: advect_rows(): return centre + sea_mask * tendency]
    unnamed x110 -> x79, local copies, waits for them, and re-layouts: 14.7 us -> 30 us
    ppermute x8, starting transfers between devices: 22.8 us -> 10.7 us  [exchange(): return [lax.ppermute(line, AXES, perm) for line, perm in zip(lines, perms)]]
    ppermute x4 -> x0, local copies, waits for them, and re-layouts: 11.8 us -> none  [the longest x2 5.92 us: with_halo(): after = lax.ppermute(leading, axis, down)]
    scatter x2 -> x0, local copies, waits for them, and re-layouts: 11.4 us -> none  [the longest x1 10.4 us: on_device(): outgoing = jnp.zeros((node_count * capacity, fields, tile_width), jnp.flo...]
    all_to_all x3 -> x2, waiting for transfers between devices: 8.28 us -> 0.01 us  [all_to_all(): return lax.all_to_all(x, AXES, split_axis=0, concat_axis=0, tiled=True)]
  transfers between devices with their start and end apart: 11 -> 10, of which waited for: 1 -> 3; matrix products, arithmetic and copies ran while one was open for 45% -> 0% of each run, Pallas kernels for 0% -> 17%
where the time goes in v1:
time: 91.4 us; the launch traced here: 90.5 us
  Pallas kernels  32.7 us (36%)
  local copies, waits for them, and re-layouts  30.2 us (33%)
  starting transfers between devices  22 us (24%)
  waiting for transfers between devices  4.71 us (5%)
    unnamed x79, local copies, waits for them, and re-layouts  30 us
    all_to_all x2, starting transfers between devices, all_to_all(): return lax.all_to_all(x, AXES, split_axis=0, concat_axis=0, tiled=True)  11.3 us
    ppermute x8, starting transfers between devices, exchange(): return [lax.ppermute(line, AXES, perm) for line, perm in zip(lines, perms)]  10.7 us
    pallas_call x1, Pallas kernels, last_part(): pl.pallas_call(functools.partial(last_kernel, levels=levels), out_shape=j...  7.72 us
    pallas_call x1, Pallas kernels, replies(): pl.pallas_call(functools.partial(reply_kernel, levels=levels, cap=cap, wi...  6.66 us
    pallas_call x1, Pallas kernels, first_part(): pl.pallas_call(functools.partial(first_kernel, levels=levels), out_shape=...  5.53 us
    ppermute x8, waiting for transfers between devices, exchange(): return [lax.ppermute(line, AXES, perm) for line, perm in zip(lines, perms)]  4.7 us
    pallas_call x1, Pallas kernels, middle_part(): pl.pallas_call(functools.partial(middle_kernel, levels=levels, cap=cap, w...  4.01 us
  transfers between devices with their start and end apart: 10, of which 3 were waited for; matrix products, arithmetic and copies ran while one was open for 0% of the time, Pallas kernels for 17%

profile of v1, /device:TPU:0, one launch (start us, length us, event | category | flops | bytes accessed | tf_op | source)
XLA Modules:
  0.0 90.5 jit_solution(3112965971866561451)
XLA Ops:
  0.8 2.0 %copy-done.1 = bf16[96,128,128]{2,1,0:T(8,128)(2,1)S(1)} copy-done((bf16[96,128,128]{2,1,0:T(8,128)(2,1)S(1)}, bf16[96,128,128]{2,1,0:T(8,128)(2,1)}, u32[]{:S(2)}) %copy-start.1) | copy-done | bytes 3145752
  6.3 3.4 %contributions.1 = (bf16[16,104,128]{2,1,0:T(8,128)(2,1)S(1)}, s32[96]{0:T(128)S(1)}) custom-call(s32[8]{0:T(128)S(1)} %stack.55.info_ref, s32[96]{0:T(128)S(1)} %bitcast.16, s32[96]{0:T(128)S(1)} %copy-done.30, s32[96]{0:T(128)S(1)} %copy-done.37, s32[48]{0:T(128)S(1)} %copy-done.32, bf16[48,8,128]{2,1,0:T(8,128)(2,1)S(1)} %copy-done.27, ...), custom_call_target="tpu_custom_call" | custom-call | tf_op jit(solution)/shard_map/contributions/pallas_call | solution.py:104
  10.6 7.5 %all-to-all-start = ((bf16[16,104,128]{2,1,0:T(8,128)(2,1)}), bf16[16,104,128]{2,1,0:T(8,128)(2,1)}, u32[]{:S(2)}, u32[]{:S(2)}) async-start(bf16[16,104,128]{2,1,0:T(8,128)(2,1)} %copy-done.22), calls=%async_computation | async-start | bytes 851968 | tf_op jit(solution)/shard_map/all_to_all | solution.py:659
  18.1 2.5 %edges.1 = (f32[48,128]{1,0:T(8,128)S(1)}, f32[48,128]{1,0:T(8,128)S(1)}, f32[48,128]{1,0:T(8,128)S(1)}, f32[48,128]{1,0:T(8,128)S(1)}) custom-call(s32[8]{0:T(128)S(1)} %stack.55.info_ref, s32[96]{0:T(128)S(1)} %get-tuple-element.18.order_ref.slot_ref, f32[48,128,128]{2,1,0:T(8,128)S(1)} %bitcast.14), custom_call_target="tpu_custom_call" | custom-call | tf_op jit(solution)/shard_map/edges/pallas_call | solution.py:170
  20.7 1.9 %collective-permute-start = (f32[48,128]{1,0:T(8,128)S(1)}, f32[48,128]{1,0:T(8,128)S(1)}, u32[]{:S(2)}, u32[]{:S(2)}) collective-permute-start(f32[48,128]{1,0:T(8,128)S(1)} %get-tuple-element.19), channel_id=1, source_target_pairs={{0,4},{1,5},{2,6},{3,7},{4,0},{5,1},{6,2},{7,3},{8,12},{9,13},{10,... | collective-permute-start | bytes 73736 | tf_op jit(solution)/shard_map/ppermute | solution.py:197
  23.1 1.1 %collective-permute-start.3 = (f32[48,128]{1,0:T(8,128)S(1)}, f32[48,128]{1,0:T(8,128)S(1)}, u32[]{:S(2)}, u32[]{:S(2)}) collective-permute-start(f32[48,128]{1,0:T(8,128)S(1)} %get-tuple-element.22), channel_id=1, source_target_pairs={{0,3},{1,2},{2,1},{3,0},{4,7},{5,6},{6,5},{7,4},{8,11},{9,10},{10,... | collective-permute-start | bytes 73736 | tf_op jit(solution)/shard_map/ppermute | solution.py:197
  24.3 2.4 %collective-permute-done.r0 = f32[48,128]{1,0:T(8,128)S(1)} collective-permute-done((f32[48,128]{1,0:T(8,128)S(1)}, f32[48,128]{1,0:T(8,128)S(1)}, u32[]{:S(2)}, u32[]{:S(2)}) %collective-permute-start) | collective-permute-done | bytes 24608 | tf_op jit(solution)/shard_map/ppermute | solution.py:197
  26.8 5.5 %first_part.1 = (f32[48,128,128]{2,1,0:T(8,128)S(1)}, f32[8,128,128]{2,1,0:T(8,128)S(1)}) custom-call(s32[8]{0:T(128)S(1)} %stack.55.info_ref, f32[48,128,128]{2,1,0:T(8,128)S(1)} %bitcast.15, f32[48,128]{1,0:T(8,128)S(1)} %collective-permute-done.r0, f32[48,128]{1,0:T(8,128)S(1)} %collective-permute-done.1.r1, f32[48,128]{1,0:T(8,128)S(1)} %collective-permute-done.2.r2, ...), custom_call_target="tpu_custom_call" | custom-call | tf_op jit(solution)/shard_map/first_part/pallas_call | solution.py:356
  34.7 1.7 %copy-done.17 = f32[48,128,128]{2,1,0:T(8,128)} copy-done((f32[48,128,128]{2,1,0:T(8,128)}, f32[48,128,128]{2,1,0:T(8,128)S(1)}, u32[]{:S(2)}) %copy-start.17) | copy-done | bytes 3145752
  36.4 1.1 %copy-done.12 = f32[7,128,128]{2,1,0:T(8,128)S(1)} copy-done((f32[7,128,128]{2,1,0:T(8,128)S(1)}, f32[7,128,128]{2,1,0:T(8,128)}, u32[]{:S(2)}) %copy-start.12) | copy-done | bytes 458776
  37.5 1.0 %copy-done.15 = f32[8,128,128]{2,1,0:T(8,128)S(1)} copy-done((f32[8,128,128]{2,1,0:T(8,128)S(1)}, f32[8,128,128]{2,1,0:T(8,128)}, u32[]{:S(2)}) %copy-start.15) | copy-done | bytes 524312
  38.5 1.9 %copy-done.18 = f32[48,128,128]{2,1,0:T(8,128)S(1)} copy-done((f32[48,128,128]{2,1,0:T(8,128)S(1)}, f32[48,128,128]{2,1,0:T(8,128)}, u32[]{:S(2)}) %copy-start.18) | copy-done | bytes 3145752
  40.4 4.0 %middle_part.1 = (f32[48,128,128]{2,1,0:T(8,128)S(1)}, f32[9,128,128]{2,1,0:T(8,128)S(1)}, bf16[256,128]{1,0:T(8,128)(2,1)S(1)}, f32[48,128]{1,0:T(8,128)S(1)}, ...) custom-call(s32[8]{0:T(128)S(1)} %stack.55.info_ref, ...), custom_call_target="tpu_custom_call" | custom-call | tf_op jit(solution)/shard_map/middle_part/pallas_call | solution.py:472
  44.4 5.6 %collective-permute-start.4 = (f32[48,128]{1,0:T(8,128)S(1)}, f32[48,128]{1,0:T(8,128)S(1)}, u32[]{:S(2)}, u32[]{:S(2)}) collective-permute-start(f32[48,128]{1,0:T(8,128)S(1)} %get-tuple-element.26), channel_id=1, source_target_pairs={{0,4},{1,5},{2,6},{3,7},{4,0},{5,1},{6,2},{7,3},{8,12},{9,13},{10,... | collective-permute-start | bytes 73736 | tf_op jit(solution)/shard_map/ppermute | solution.py:197
  50.6 1.1 %collective-permute-start.7 = (f32[48,128]{1,0:T(8,128)S(1)}, f32[48,128]{1,0:T(8,128)S(1)}, u32[]{:S(2)}, u32[]{:S(2)}) collective-permute-start(f32[48,128]{1,0:T(8,128)S(1)} %get-tuple-element.29), channel_id=1, source_target_pairs={{0,3},{1,2},{2,1},{3,0},{4,7},{5,6},{6,5},{7,4},{8,11},{9,10},{10,... | collective-permute-start | bytes 73736 | tf_op jit(solution)/shard_map/ppermute | solution.py:197
  51.9 2.0 %collective-permute-done.7.r3 = f32[48,128]{1,0:T(8,128)S(1)} collective-permute-done((f32[48,128]{1,0:T(8,128)S(1)}, f32[48,128]{1,0:T(8,128)S(1)}, u32[]{:S(2)}, u32[]{:S(2)}) %collective-permute-start.7) | collective-permute-done | bytes 24608 | tf_op jit(solution)/shard_map/ppermute | solution.py:197
  53.9 6.7 %replies.1.order_ref = bf16[16,72,128]{2,1,0:T(8,128)(2,1)} custom-call(s32[8]{0:T(128)S(1)} %stack.55.info_ref, f32[48,128,128]{2,1,0:T(8,128)S(1)} %get-tuple-element.25.c_hbm, f32[48,128]{1,0:T(8,128)S(1)} %collective-permute-done.4.r0, f32[48,128]{1,0:T(8,128)S(1)} %collective-permute-done.5.r1, f32[48,128]{1,0:T(8,128)S(1)} %collective-permute-done.6.r2, ...), custom_call_target="tpu_custom_call" | custom-call | tf_op jit(solution)/shard_map/replies/pallas_call | solution.py:538
  60.6 1.7 %copy-done.3 = f32[48,128,128]{2,1,0:T(8,128)} copy-done((f32[48,128,128]{2,1,0:T(8,128)}, f32[48,128,128]{2,1,0:T(8,128)S(1)}, u32[]{:S(2)}) %copy-start.3) | copy-done | bytes 3145752
  64.3 3.8 %all-to-all-start.1 = ((bf16[16,72,128]{2,1,0:T(8,128)(2,1)}), bf16[16,72,128]{2,1,0:T(8,128)(2,1)S(1)}, u32[]{:S(2)}, u32[]{:S(2)}) async-start(bf16[16,72,128]{2,1,0:T(8,128)(2,1)} %replies.1.order_ref), calls=%async_computation.1 | async-start | bytes 589824 | tf_op jit(solution)/shard_map/all_to_all | solution.py:659
  68.1 1.9 %copy-done.4 = f32[48,128,128]{2,1,0:T(8,128)S(1)} copy-done((f32[48,128,128]{2,1,0:T(8,128)S(1)}, f32[48,128,128]{2,1,0:T(8,128)}, u32[]{:S(2)}) %copy-start.4) | copy-done | bytes 3145752
  73.0 1.0 %copy-done.16 = f32[8,128,128]{2,1,0:T(8,128)S(1)} copy-done((f32[8,128,128]{2,1,0:T(8,128)S(1)}, f32[8,128,128]{2,1,0:T(8,128)}, u32[]{:S(2)}) %copy-start.16) | copy-done | bytes 524312
  74.1 1.1 %copy-done.20 = f32[9,128,128]{2,1,0:T(8,128)S(1)} copy-done((f32[9,128,128]{2,1,0:T(8,128)S(1)}, f32[9,128,128]{2,1,0:T(8,128)}, u32[]{:S(2)}) %copy-start.20) | copy-done | bytes 589848
  77.3 7.7 %last_part.1 = f32[48,128,128]{2,1,0:T(8,128)} custom-call(s32[8]{0:T(128)S(1)} %copy-done.29, bf16[16,72,128]{2,1,0:T(8,128)(2,1)} %replies.1.order_ref, f32[48,128,128]{2,1,0:T(8,128)S(1)} %copy-done.4, f32[48,128]{1,0:T(8,128)S(1)} %collective-permute-done.4.r0, f32[48,128]{1,0:T(8,128)S(1)} %collective-permute-done.5.r1, f32[48,128]{1,0:T(8,128)S(1)} %copy-done.24, ...), custom_call_target="tpu_custom_call" | custom-call | tf_op jit(solution)/shard_map/last_part/pallas_call | solution.py:587
  87.0 2.8 %back.1 = f32[48,6,128]{2,1,0:T(8,128)S(1)} custom-call(s32[96]{0:T(128)S(1)} %copy-done.35, s32[96]{0:T(128)S(1)} %copy-done.31, s32[48]{0:T(128)S(1)} %copy-done.33, bf16[16,72,128]{2,1,0:T(8,128)(2,1)S(1)} %all-to-all-done.1.returned_ref, bf16[96,128,128]{2,1,0:T(8,128)(2,1)S(1)} %copy-done.2), custom_call_target="tpu_custom_call" | custom-call | tf_op jit(solution)/shard_map/back/pallas_call | solution.py:639
  (84 shorter events, 18.0 us)
Async XLA Ops:
  0.6 17.5 %copy-start = (f32[6,8,128,128]{3,2,1,0:T(8,128)S(1)}, f32[6,8,128,128]{3,2,1,0:T(8,128)}, u32[]{:S(2)}) copy-start(f32[6,8,128,128]{3,2,1,0:T(8,128)} %param.16) | copy-start | bytes 9437188
  0.8 53.1 %copy-start.28 = (s32[8]{0:T(128)}, s32[8]{0:T(128)S(1)}, u32[]{:S(2)}) copy-start(s32[8]{0:T(128)S(1)} %stack.55.info_ref) | copy-start | bytes 100
  0.8 2.0 %copy-start.1 = (bf16[96,128,128]{2,1,0:T(8,128)(2,1)S(1)}, bf16[96,128,128]{2,1,0:T(8,128)(2,1)}, u32[]{:S(2)}) copy-start(bf16[96,128,128]{2,1,0:T(8,128)(2,1)} %weights_ref.3) | copy-start | bytes 9437188
  10.5 12.1 %copy-start.34 = (s32[96]{0:T(128)}, s32[96]{0:T(128)S(1)}, u32[]{:S(2)}) copy-start(s32[96]{0:T(128)S(1)} %get-tuple-element.18.order_ref.slot_ref) | copy-start | bytes 1156
  10.6 16.2 %copy-start.21 = (s32[128,128]{1,0:T(8,128)S(1)}, s32[128,128]{1,0:T(8,128)}, u32[]{:S(2)}) copy-start(s32[128,128]{1,0:T(8,128)} %land_ref.7) | copy-start | bytes 196612
  10.6 25.8 %all-to-all-start = ((bf16[16,104,128]{2,1,0:T(8,128)(2,1)}), bf16[16,104,128]{2,1,0:T(8,128)(2,1)}, u32[]{:S(2)}, u32[]{:S(2)}) async-start(bf16[16,104,128]{2,1,0:T(8,128)(2,1)} %copy-done.22), calls=%async_computation | async-start | bytes 851968 | tf_op jit(solution)/shard_map/all_to_all | solution.py:659
  18.1 6.1 %copy-start.38 = (f32[2,8,128,128]{3,2,1,0:T(8,128)S(1)}, f32[2,8,128,128]{3,2,1,0:T(8,128)}, u32[]{:S(2)}) copy-start(f32[2,8,128,128]{3,2,1,0:T(8,128)} %param.17) | copy-start | bytes 3145732
  18.1 8.7 %copy-start.11 = (f32[7,128,128]{2,1,0:T(8,128)S(1)}, f32[7,128,128]{2,1,0:T(8,128)}, u32[]{:S(2)}) copy-start(f32[7,128,128]{2,1,0:T(8,128)} %k_ref.7) | copy-start | bytes 1376260
  20.7 6.1 %collective-permute-start = (f32[48,128]{1,0:T(8,128)S(1)}, f32[48,128]{1,0:T(8,128)S(1)}, u32[]{:S(2)}, u32[]{:S(2)}) collective-permute-start(f32[48,128]{1,0:T(8,128)S(1)} %get-tuple-element.19), channel_id=1, source_target_pairs={{0,4},{1,5},{2,6},{3,7},{4,0},{5,1},{6,2},{7,3},{8,12},{9,13},{10,... | collective-permute-start | bytes 73736 | tf_op jit(solution)/shard_map/ppermute | solution.py:197
  22.6 4.1 %collective-permute-start.1 = (f32[48,128]{1,0:T(8,128)S(1)}, f32[48,128]{1,0:T(8,128)S(1)}, u32[]{:S(2)}, u32[]{:S(2)}) collective-permute-start(f32[48,128]{1,0:T(8,128)S(1)} %get-tuple-element.20), channel_id=1, source_target_pairs={{0,1},{1,0},{2,3},{3,2},{4,8},{5,9},{6,10},{7,11},{8,4},{9,5},{10,... | collective-permute-start | bytes 73736 | tf_op jit(solution)/shard_map/ppermute | solution.py:197
  22.6 4.1 %collective-permute-start.2 = (f32[48,128]{1,0:T(8,128)S(1)}, f32[48,128]{1,0:T(8,128)S(1)}, u32[]{:S(2)}, u32[]{:S(2)}) collective-permute-start(f32[48,128]{1,0:T(8,128)S(1)} %get-tuple-element.21), channel_id=1, source_target_pairs={{0,1},{1,0},{2,3},{3,2},{4,5},{5,4},{6,7},{7,6},{8,9},{9,8},{10,11... | collective-permute-start | bytes 73736 | tf_op jit(solution)/shard_map/ppermute | solution.py:197
  23.1 3.6 %collective-permute-start.3 = (f32[48,128]{1,0:T(8,128)S(1)}, f32[48,128]{1,0:T(8,128)S(1)}, u32[]{:S(2)}, u32[]{:S(2)}) collective-permute-start(f32[48,128]{1,0:T(8,128)S(1)} %get-tuple-element.22), channel_id=1, source_target_pairs={{0,3},{1,2},{2,1},{3,0},{4,7},{5,6},{6,5},{7,4},{8,11},{9,10},{10,... | collective-permute-start | bytes 73736 | tf_op jit(solution)/shard_map/ppermute | solution.py:197
  34.7 1.7 %copy-start.17 = (f32[48,128,128]{2,1,0:T(8,128)}, f32[48,128,128]{2,1,0:T(8,128)S(1)}, u32[]{:S(2)}) copy-start(f32[48,128,128]{2,1,0:T(8,128)S(1)} %get-tuple-element.23.q_hbm) | copy-start | bytes 9437188
  36.4 17.5 %copy-start.6 = (f32[8,128,128]{2,1,0:T(8,128)S(1)}, f32[8,128,128]{2,1,0:T(8,128)}, u32[]{:S(2)}) copy-start(f32[8,128,128]{2,1,0:T(8,128)} %copy-done.5) | copy-start | bytes 1572868
  36.4 17.5 %copy-start.9 = (f32[8,128,128]{2,1,0:T(8,128)S(1)}, f32[8,128,128]{2,1,0:T(8,128)}, u32[]{:S(2)}) copy-start(f32[8,128,128]{2,1,0:T(8,128)} %copy-done.8) | copy-start | bytes 1572868
  38.5 1.9 %copy-start.18 = (f32[48,128,128]{2,1,0:T(8,128)S(1)}, f32[48,128,128]{2,1,0:T(8,128)}, u32[]{:S(2)}) copy-start(f32[48,128,128]{2,1,0:T(8,128)} %copy-done.17) | copy-start | bytes 9437188
  44.4 7.4 %collective-permute-start.4 = (f32[48,128]{1,0:T(8,128)S(1)}, f32[48,128]{1,0:T(8,128)S(1)}, u32[]{:S(2)}, u32[]{:S(2)}) collective-permute-start(f32[48,128]{1,0:T(8,128)S(1)} %get-tuple-element.26), channel_id=1, source_target_pairs={{0,4},{1,5},{2,6},{3,7},{4,0},{5,1},{6,2},{7,3},{8,12},{9,13},{10,... | collective-permute-start | bytes 73736 | tf_op jit(solution)/shard_map/ppermute | solution.py:197
  50.0 1.8 %collective-permute-start.5 = (f32[48,128]{1,0:T(8,128)S(1)}, f32[48,128]{1,0:T(8,128)S(1)}, u32[]{:S(2)}, u32[]{:S(2)}) collective-permute-start(f32[48,128]{1,0:T(8,128)S(1)} %get-tuple-element.27), channel_id=1, source_target_pairs={{0,1},{1,0},{2,3},{3,2},{4,8},{5,9},{6,10},{7,11},{8,4},{9,5},{10,... | collective-permute-start | bytes 73736 | tf_op jit(solution)/shard_map/ppermute | solution.py:197
  50.1 1.8 %collective-permute-start.6 = (f32[48,128]{1,0:T(8,128)S(1)}, f32[48,128]{1,0:T(8,128)S(1)}, u32[]{:S(2)}, u32[]{:S(2)}) collective-permute-start(f32[48,128]{1,0:T(8,128)S(1)} %get-tuple-element.28), channel_id=1, source_target_pairs={{0,1},{1,0},{2,3},{3,2},{4,5},{5,4},{6,7},{7,6},{8,9},{9,8},{10,11... | collective-permute-start | bytes 73736 | tf_op jit(solution)/shard_map/ppermute | solution.py:197
  50.6 3.3 %collective-permute-start.7 = (f32[48,128]{1,0:T(8,128)S(1)}, f32[48,128]{1,0:T(8,128)S(1)}, u32[]{:S(2)}, u32[]{:S(2)}) collective-permute-start(f32[48,128]{1,0:T(8,128)S(1)} %get-tuple-element.29), channel_id=1, source_target_pairs={{0,3},{1,2},{2,1},{3,0},{4,7},{5,6},{6,5},{7,4},{8,11},{9,10},{10,... | collective-permute-start | bytes 73736 | tf_op jit(solution)/shard_map/ppermute | solution.py:197
  60.6 1.7 %copy-start.3 = (f32[48,128,128]{2,1,0:T(8,128)}, f32[48,128,128]{2,1,0:T(8,128)S(1)}, u32[]{:S(2)}) copy-start(f32[48,128,128]{2,1,0:T(8,128)S(1)} %get-tuple-element.25.c_hbm) | copy-start | bytes 9437188
  64.3 20.7 %all-to-all-start.1 = ((bf16[16,72,128]{2,1,0:T(8,128)(2,1)}), bf16[16,72,128]{2,1,0:T(8,128)(2,1)S(1)}, u32[]{:S(2)}, u32[]{:S(2)}) async-start(bf16[16,72,128]{2,1,0:T(8,128)(2,1)} %replies.1.order_ref), calls=%async_computation.1 | async-start | bytes 589824 | tf_op jit(solution)/shard_map/all_to_all | solution.py:659
  68.0 1.9 %copy-start.4 = (f32[48,128,128]{2,1,0:T(8,128)S(1)}, f32[48,128,128]{2,1,0:T(8,128)}, u32[]{:S(2)}) copy-start(f32[48,128,128]{2,1,0:T(8,128)} %copy-done.3) | copy-start | bytes 9437188
  77.3 7.7 %copy-start.2 = (bf16[96,128,128]{2,1,0:T(8,128)(2,1)S(1)}, bf16[96,128,128]{2,1,0:T(8,128)(2,1)}, u32[]{:S(2)}) copy-start(bf16[96,128,128]{2,1,0:T(8,128)(2,1)} %weights_ref.3) | copy-start | bytes 9437188
  (25 other events, 20.2 us)

commit v2 on v1

v2 whole, which is shorter than its diff:
```python
import functools

import jax
import jax.numpy as jnp
from jax import lax
from jax.experimental import pallas as pl
from jax.experimental.pallas import tpu as pltpu
from jax.sharding import PartitionSpec as P

DIFFUSION = 0.2
FORCING = 0.5
F32 = jnp.float32
BF16 = jnp.bfloat16
AXES = ("tx", "ty", "tz")
PAD = 8
CHUNKS = 4


def vmem():
    return pl.BlockSpec(memory_space=pltpu.VMEM)


def smem():
    return pl.BlockSpec(memory_space=pltpu.SMEM)


def hbm():
    return pl.BlockSpec(memory_space=pltpu.HBM)


def pin(*arrays):
    return tuple(pltpu.with_memory_space_constraint(x, pltpu.HBM) for x in arrays)


def copies_of(pairs, sems, base=0):
    copies = [
        pltpu.make_async_copy(src, dst, sems.at[base + n]) for n, (src, dst) in enumerate(pairs)
    ]
    for copy in copies:
        copy.start()
    return copies


def chunk_copies(src, src_pad, dst, dst_pad, height, sems, base=0):
    rows = height // CHUNKS
    return copies_of(
        [
            (
                src.at[:, pl.ds(src_pad + n * rows, rows), :],
                dst.at[:, pl.ds(dst_pad + n * rows, rows), :],
            )
            for n in range(CHUNKS)
        ],
        sems,
        base,
    )


def params(mib):
    return pltpu.CompilerParams(vmem_limit_bytes=mib * 2**20)


def place_of(sizes):
    tx = lax.axis_index("tx")
    group = lax.axis_index("ty") * sizes[2] + lax.axis_index("tz")
    return tx, group, sizes[1] * sizes[2]


def lane_iota(shape):
    return lax.broadcasted_iota(jnp.int32, shape, len(shape) - 1)


def contrib_kernel(
    dest_hbm, atm_hbm, row_hbm, rows_hbm, flux_hbm, weights_hbm,
    out_hbm, slot_hbm,
    dest_ref, atm_ref, row_ref, rows_ref, slot_ref, count, flux_ref, weights_ref,
    masked, message, packed, sems, out_sems,
    *, sizes, nodes, cap, window, steps, message_rows,
):
    pairs = weights_ref.shape[0]
    per_step = pairs // steps
    fields = flux_ref.shape[1]
    lanes = flux_ref.shape[2]
    small = [
        pltpu.make_async_copy(src, dst, sems.at[n])
        for n, (src, dst) in enumerate(
            [
                (dest_hbm, dest_ref), (row_hbm, row_ref), (atm_hbm, atm_ref),
                (rows_hbm, rows_ref), (flux_hbm, flux_ref),
            ]
        )
    ]
    parts = [
        pltpu.make_async_copy(
            weights_hbm.at[pl.ds(n * per_step, per_step)],
            weights_ref.at[pl.ds(n * per_step, per_step)],
            sems.at[len(small) + n],
        )
        for n in range(steps)
    ]
    for copy in small + parts:
        copy.start()
    message[...] = jnp.zeros(message.shape, F32)

    def clear(n, carry):
        count[n] = 0
        return carry

    lax.fori_loop(0, nodes, clear, 0, unroll=8)
    tx, group, groups = place_of(sizes)
    base = lax.rem(tx * groups + group, 128 // window) * window
    lane8 = lane_iota((8, 128))
    small[0].wait()
    small[1].wait()

    def place(p, carry):
        d = dest_ref[p]
        s = count[d]
        count[d] = s + 1
        slot_ref[p] = d * cap + s
        start = pl.multiple_of(d * message_rows + cap * fields, 8)
        tile = message[pl.ds(start, 8), :]
        named = (row_ref[p] + 1).astype(F32)
        message[pl.ds(start, 8), :] = jnp.where(lane8 == base + s, named, tile)
        return carry

    lax.fori_loop(0, pairs, place, 0, unroll=4)
    slots_out = pltpu.make_async_copy(slot_ref, slot_hbm, sems.at[0])
    slots_out.start()
    small[2].wait()
    small[3].wait()
    small[4].wait()
    lane = lane_iota((fields, lanes))

    def mask(b, carry):
        masked[b] = jnp.where(lane < rows_ref[b], flux_ref[b].astype(F32), 0.0)
        return carry

    lax.fori_loop(0, flux_ref.shape[0], mask, 0, unroll=8)
    for n in range(steps):
        parts[n].wait()
        for p in range(n * per_step, (n + 1) * per_step):
            slot = slot_ref[p]
            d = slot // cap
            s = slot - d * cap
            lhs = masked[atm_ref[p]].astype(BF16)
            product = jnp.dot(lhs, weights_ref[p], preferred_element_type=F32)
            start = pl.multiple_of(d * message_rows + s * fields, 8)
            message[pl.ds(start, fields), :] = product
    per_part = nodes // steps
    outs = []
    for n in range(steps):
        for d in range(n * per_part, (n + 1) * per_part):
            packed[d] = message[d * message_rows : (d + 1) * message_rows, :].astype(BF16)
        here = pl.ds(n * per_part, per_part)
        copy = pltpu.make_async_copy(packed.at[here], out_hbm.at[here], out_sems.at[n])
        copy.start()
        outs.append(copy)
    for copy in outs:
        copy.wait()
    slots_out.wait()


def contributions(sizes, dest, atm, row, rows, flux, weights, nodes, cap, window):
    pairs, cells, width = weights.shape
    fields = flux.shape[1]
    message_rows = cap * fields + 8
    steps = 4
    ints = jnp.int32
    return pl.pallas_call(
        functools.partial(
            contrib_kernel, sizes=sizes, nodes=nodes, cap=cap, window=window,
            steps=steps, message_rows=message_rows,
        ),
        out_shape=(
            pltpu.HBM((nodes, message_rows, width), BF16),
            pltpu.HBM((pairs,), ints),
        ),
        in_specs=[hbm()] * 6,
        out_specs=(hbm(), hbm()),
        scratch_shapes=[
            pltpu.SMEM((pairs,), ints),
            pltpu.SMEM((pairs,), ints),
            pltpu.SMEM((pairs,), ints),
            pltpu.SMEM(rows.shape, ints),
            pltpu.SMEM((pairs,), ints),
            pltpu.SMEM((nodes,), ints),
            pltpu.VMEM(flux.shape, BF16),
            pltpu.VMEM(weights.shape, BF16),
            pltpu.VMEM(flux.shape, F32),
            pltpu.VMEM((nodes * message_rows, width), F32),
            pltpu.VMEM((nodes, message_rows, width), BF16),
            pltpu.SemaphoreType.DMA((5 + steps,)),
            pltpu.SemaphoreType.DMA((steps,)),
        ],
        compiler_params=params(10),
        name="contributions",
    )(*pin(dest, atm, row, rows, flux, weights))


def column_lines(collected):
    return collected.T


def store_sends(sizes, lines_ref, row_first, row_last, sends):
    count = sends[0].shape[0]
    east = lines_ref[pl.ds(1, count, stride=2), :]
    west = lines_ref[pl.ds(2, count, stride=2), :]
    tx, group, _ = place_of(sizes)
    tx_even = lax.rem(tx, 2) == 0
    g_even = lax.rem(group, 2) == 0
    sends[0][...] = jnp.where(tx_even, east, west)
    sends[1][...] = jnp.where(tx_even, west, east)
    sends[2][...] = jnp.where(g_even, row_last, row_first)
    sends[3][...] = jnp.where(g_even, row_first, row_last)


def edges_kernel(order, c_hbm, padded, s0, s1, s2, s3, cols, lines, sems, *, sizes):
    del order
    count, height, width = c_hbm.shape
    lane = lane_iota((8, width))
    rows = height // CHUNKS
    copies = chunk_copies(c_hbm, 0, padded, PAD, height, sems)
    for chunk in range(CHUNKS):
        copies[chunk].wait()

        def body(i, carry):
            r = pl.multiple_of(chunk * rows + i * 8, 8)
            acc = jnp.zeros((8, width), F32)
            for tl in range(count):
                moved = pltpu.roll(padded[tl, pl.ds(PAD + r, 8), :], (2 * tl + 2) % width, 1)
                acc = jnp.where((lane == 2 * tl + 1) | (lane == 2 * tl + 2), moved, acc)
            cols[pl.ds(r, 8), :] = acc
            return carry

        lax.fori_loop(0, rows // 8, body, 0)
    lines[...] = cols[...].T
    store_sends(
        sizes, lines, padded[:, PAD, :], padded[:, PAD + height - 1, :], (s0, s1, s2, s3)
    )


def edges(sizes, order, state):
    count, height, width = state.shape
    line = jax.ShapeDtypeStruct((count, width), F32)
    return pl.pallas_call(
        functools.partial(edges_kernel, sizes=sizes),
        out_shape=(jax.ShapeDtypeStruct((count, height + 2 * PAD, width), F32),) + (line,) * 4,
        in_specs=[hbm(), hbm()],
        out_specs=(vmem(),) * 5,
        scratch_shapes=[
            pltpu.VMEM((height, width), F32),
            pltpu.VMEM((width, height), F32),
            pltpu.SemaphoreType.DMA((CHUNKS,)),
        ],
        compiler_params=params(4),
        name="edges",
    )(*pin(order, state))


def exchange(lines, mesh_sizes):
    n_tx, n_ty, n_tz = mesh_sizes
    groups = n_ty * n_tz
    perms = [[], [], [], []]
    for x in range(n_tx):
        for g in range(groups):
            here = x * groups + g
            perms[0].append((here, (x ^ 1) * groups + g))
            inner_x = x + 1 if x % 2 == 1 else x - 1
            if 0 <= inner_x < n_tx:
                perms[1].append((here, inner_x * groups + g))
            else:
                perms[1].append((here, x * groups + (g ^ 1)))
            perms[2].append((here, x * groups + (g ^ 1)))
            inner_g = g + 1 if g % 2 == 1 else g - 1
            perms[3].append((here, x * groups + inner_g % groups))
    return [lax.ppermute(line, AXES, perm) for line, perm in zip(lines, perms)]


def place_sides(sizes, received, lines, sides):
    count = received[0].shape[0]
    tx, _, _ = place_of(sizes)
    tx_even = lax.rem(tx, 2) == 0
    zero = jnp.zeros(received[0].shape, F32)
    r0, r1 = (r[...] for r in received)
    r1 = jnp.where((tx == 0) | (tx == sizes[0] - 1), zero, r1)
    lines[...] = jnp.zeros(lines.shape, F32)
    lines[pl.ds(1, count, stride=2), :] = jnp.where(tx_even, r0, r1)
    lines[pl.ds(2, count, stride=2), :] = jnp.where(tx_even, r1, r0)
    sides[...] = lines[...].T


def place_rows(sizes, received, padded):
    count = padded.shape[0]
    height = padded.shape[1] - 2 * PAD
    _, group, groups = place_of(sizes)
    g_even = lax.rem(group, 2) == 0
    r2, r3 = (r[...] for r in received)
    r3 = jnp.where((group == 0) | (group == groups - 1), jnp.zeros(r3.shape, F32), r3)
    north = jnp.where(g_even, r2, r3)
    south = jnp.where(g_even, r3, r2)
    for tl in range(count):
        padded[tl, PAD + height : PAD + height + 1, :] = north[tl : tl + 1, :]
        padded[tl, PAD - 1 : PAD, :] = south[tl : tl + 1, :]


def shift_matrix(width):
    k = lax.broadcasted_iota(jnp.int32, (2 * width, 2 * width), 0) % width
    n = lax.broadcasted_iota(jnp.int32, (2 * width, 2 * width), 1)
    j = n % width
    east = jnp.where(k == j + 1, 1.0, 0.0)
    west = jnp.where(k == j - 1, 1.0, 0.0)
    here = jnp.where(k == j, 4.0, 0.0)
    return jnp.where(n < width, east - west, east + west - here).astype(BF16)


def sweep(padded, vel_ref, k_ref, land_ref, ip_ref, sides, shifted, matrix, finish, levels, wait=None, done=None):
    count, padded_height, width = padded.shape
    height = padded_height - 2 * PAD
    tracers = count // levels
    rows = height // CHUNKS
    lane = lane_iota((8, width))
    matrix[...] = shift_matrix(width)
    for chunk in range(CHUNKS):
        if wait is not None:
            wait(chunk)
        first = chunk * rows
        x = padded[:, PAD + first : PAD + first + rows, :].reshape(count * rows, width)
        high = x.astype(BF16)
        low = (x - high.astype(F32)).astype(BF16)
        both = jnp.concatenate([high, low], axis=1)
        shifted[...] = jnp.dot(both, matrix[...], preferred_element_type=F32).reshape(
            count, rows, 2 * width
        )

        def block(i, carry):
            r = pl.multiple_of(first + i * 8, 8)
            local = pl.multiple_of(i * 8, 8)
            sea = land_ref[pl.ds(r, 8), :].astype(F32)
            side = sides[pl.ds(r, 8), :]
            diffuse = DIFFUSION * sea
            q = [None] * tracers
            for level in range(levels - 1, -1, -1):
                half_u = 0.5 * sea * vel_ref[0, level, pl.ds(r, 8), :]
                half_v = 0.5 * sea * vel_ref[1, level, pl.ds(r, 8), :]
                c_north = diffuse - half_v
                c_south = diffuse + half_v
                c_side = jnp.where(
                    lane == 0,
                    diffuse + half_u,
                    jnp.where(lane == width - 1, diffuse - half_u, 0.0),
                )
                if level >= 1 and level < levels - 1:
                    link = k_ref[level, pl.ds(r, 8), :] * sea
                if level >= 2:
                    inverse = ip_ref[level, pl.ds(r, 8), :]
                tops = []
                for t in range(tracers):
                    tl = t * levels + level
                    c = padded[tl, pl.ds(PAD + r, 8), :]
                    north = padded[tl, pl.ds(PAD + r + 1, 8), :]
                    south = padded[tl, pl.ds(PAD + r - 1, 8), :]
                    odd = shifted[tl, pl.ds(local, 8), :width]
                    even = shifted[tl, pl.ds(local, 8), width:]
                    halo = pltpu.roll(side, (width - (2 * tl + 2)) % width, 1)
                    rhs = (c - half_u * odd) + diffuse * even
                    rhs = rhs + (c_north * north + c_south * south) + c_side * halo
                    if level == levels - 1:
                        q[t] = rhs * inverse
                    elif level >= 2:
                        q[t] = (rhs + link * q[t]) * inverse
                    elif level == 1:
                        q[t] = rhs + link * q[t]
                    tops.append(rhs)
                if level >= 1:
                    finish(level, r, q, None)
                else:
                    finish(0, r, q, tops)
            return carry

        lax.fori_loop(0, rows // 8, block, 0)
        if done is not None:
            done(chunk)


def first_kernel(
    padded_in, r0, r1, r2, r3, vel_ref, k_ref, land_ref,
    padded, q_hbm, ip_hbm, shifted, matrix, lines, sides, q_ref, ip_ref, sems, *, sizes, levels,
):
    del padded_in
    height = q_ref.shape[1]
    rows = height // CHUNKS
    place_sides(sizes, (r0, r1), lines, sides)
    place_rows(sizes, (r2, r3), padded)
    sea = land_ref[...].astype(F32)
    below = None
    for level in range(levels - 1, 1, -1):
        upper = k_ref[level - 1] * sea
        if below is None:
            pivot = 1.0 + upper
        else:
            lower = k_ref[level] * sea
            pivot = 1.0 + upper + lower - lower * lower * below
        below = 1.0 / pivot
        ip_ref[level] = below
    lower = k_ref[1] * sea
    ip_ref[1] = 1.0 + lower - lower * lower * below
    ip_ref[0] = k_ref[0] * sea
    outs = copies_of([(ip_ref, ip_hbm)], sems, CHUNKS)

    def done(chunk):
        here = pl.ds(chunk * rows, rows)
        outs.extend(copies_of([(q_ref.at[:, here, :], q_hbm.at[:, here, :])], sems, chunk))

    def finish(level, r, q, tops):
        values = q if level > 0 else tops
        for t, value in enumerate(values):
            q_ref[t * levels + level, pl.ds(r, 8), :] = value

    sweep(
        padded, vel_ref, k_ref, land_ref, ip_ref, sides, shifted, matrix, finish, levels,
        done=done,
    )
    for copy in outs:
        copy.wait()


def sweep_scratch(count, height, width):
    return [
        pltpu.VMEM((count, height // CHUNKS, 2 * width), F32),
        pltpu.VMEM((2 * width, 2 * width), BF16),
        pltpu.VMEM((width, height), F32),
        pltpu.VMEM((height, width), F32),
    ]


def first_part(sizes, padded, received, velocity, mixing, land, levels):
    count, height, width = padded.shape
    height -= 2 * PAD
    return pl.pallas_call(
        functools.partial(first_kernel, sizes=sizes, levels=levels),
        out_shape=(
            jax.ShapeDtypeStruct(padded.shape, F32),
            pltpu.HBM((count, height, width), F32),
            pltpu.HBM((levels, height, width), F32),
        ),
        in_specs=[vmem()] * 8,
        out_specs=(vmem(), hbm(), hbm()),
        input_output_aliases={0: 0},
        scratch_shapes=sweep_scratch(count, height, width)
        + [
            pltpu.VMEM((count, height, width), F32),
            pltpu.VMEM((levels, height, width), F32),
            pltpu.SemaphoreType.DMA((CHUNKS + 1,)),
        ],
        compiler_params=params(12),
        name="first_part",
    )(padded, *received, velocity, mixing, land)


def middle_kernel(
    incoming_hbm, q_hbm, ip_hbm, k_hbm, land_hbm, vel_hbm,
    x_ref, coef_ref, pick_ref, ip_ref, k_ref, land_ref, vel_ref, s0, s1, s2, s3,
    incoming_ref, q_ref, wide, flux, cols, lines, sems, *, sizes, levels, cap, window,
):
    count, height, width = q_ref.shape
    tracers = count // levels
    nodes, message_rows, _ = incoming_ref.shape
    fields = flux.shape[0]
    rows = height // CHUNKS
    early = copies_of(
        [
            (incoming_hbm, incoming_ref), (ip_hbm, ip_ref), (land_hbm, land_ref), (k_hbm, k_ref),
            (vel_hbm, vel_ref),
        ],
        sems,
    )
    arrivals = chunk_copies(q_hbm, 0, q_ref, 0, height, sems, len(early))
    early[0].wait()
    span = nodes * message_rows
    wide[span:, :] = jnp.zeros((wide.shape[0] - span, width), F32)
    for n in range(nodes):
        wide[n * message_rows : (n + 1) * message_rows, :] = incoming_ref[n].astype(F32)
    per_group = 128 // window
    groups = -(-nodes // per_group)
    row_number = (lax.broadcasted_iota(jnp.int32, (height, 128), 0) + 1).astype(F32)
    selectors = []
    for g in range(groups):
        ids = jnp.zeros((1, 128), F32)
        for n in range(g * per_group, min(nodes, (g + 1) * per_group)):
            at = n * message_rows + cap * fields
            ids = ids + wide[at : at + 1, :]
        chosen = jnp.where(ids == row_number, 1.0, 0.0)
        selectors.append(chosen.astype(BF16))
        pick_ref[g * 128 : (g + 1) * 128, :] = chosen.T.astype(BF16)
    selector = jnp.concatenate(selectors, axis=1)
    for f in range(fields):
        pieces = [
            wide[pl.ds(n * message_rows + f, window, stride=fields), :] for n in range(nodes)
        ]
        for n in range(nodes, groups * per_group):
            pieces.append(jnp.zeros((window, width), F32))
        stacked = jnp.concatenate(pieces, axis=0).astype(BF16)
        flux[f] = jnp.dot(selector, stacked, preferred_element_type=F32)
    for copy in early[1:4]:
        copy.wait()
    sea = land_ref[...].astype(F32)
    stirring = 1.0 + 0.5 * (
        flux[fields - 2] * flux[fields - 2] + flux[fields - 1] * flux[fields - 1]
    )
    top_link = ip_ref[0] * stirring
    inverse1 = 1.0 / (ip_ref[1] + top_link)
    inverse0 = 1.0 / (1.0 + top_link - top_link * top_link * inverse1)
    coef_ref[tracers] = top_link
    coef_ref[tracers + 1] = inverse1
    coef_ref[tracers + 2] = inverse0
    for t in range(tracers):
        coef_ref[t] = FORCING * sea * flux[t]
    lane = lane_iota((8, width))
    for chunk in range(CHUNKS):
        arrivals[chunk].wait()
        first = chunk * rows

        def block(i, carry):
            r = pl.multiple_of(first + i * 8, 8)
            here = pl.ds(r, 8)
            sea8 = land_ref[here, :].astype(F32)
            link0 = coef_ref[tracers, here, :]
            inv1 = coef_ref[tracers + 1, here, :]
            inv0 = coef_ref[tracers + 2, here, :]
            down = [None, link0 * inv1]
            for level in range(2, levels):
                down.append(k_ref[level - 1, here, :] * sea8 * ip_ref[level, here, :])
            acc = jnp.zeros((8, width), F32)
            for t in range(tracers):
                base = t * levels
                q1 = q_ref[base + 1, here, :] * inv1
                x = (q_ref[base, here, :] + coef_ref[t, here, :] + link0 * q1) * inv0
                for level in range(levels):
                    tl = base + level
                    if level == 1:
                        x = q1 + down[1] * x
                    elif level > 1:
                        x = q_ref[tl, here, :] + down[level] * x
                    x_ref[tl, pl.ds(PAD + r, 8), :] = x
                    moved = pltpu.roll(x, (2 * tl + 2) % width, 1)
                    acc = jnp.where((lane == 2 * tl + 1) | (lane == 2 * tl + 2), moved, acc)
            cols[here, :] = acc
            return carry

        lax.fori_loop(0, rows // 8, block, 0)
    lines[...] = cols[...].T
    store_sends(
        sizes, lines, x_ref[:, PAD, :], x_ref[:, PAD + height - 1, :], (s0, s1, s2, s3)
    )
    early[4].wait()


def middle_part(sizes, incoming, q, ip, mixing, land, velocity, fields, levels, cap, window):
    count, height, width = q.shape
    nodes, message_rows, _ = incoming.shape
    tracers = count // levels
    groups = -(-nodes // (128 // window))
    line = jax.ShapeDtypeStruct((count, width), F32)
    return pl.pallas_call(
        functools.partial(middle_kernel, sizes=sizes, levels=levels, cap=cap, window=window),
        out_shape=(
            jax.ShapeDtypeStruct((count, height + 2 * PAD, width), F32),
            jax.ShapeDtypeStruct((tracers + 3, height, width), F32),
            jax.ShapeDtypeStruct((groups * 128, height), BF16),
            jax.ShapeDtypeStruct(ip.shape, F32),
            jax.ShapeDtypeStruct(mixing.shape, F32),
            jax.ShapeDtypeStruct(land.shape, land.dtype),
            jax.ShapeDtypeStruct(velocity.shape, F32),
            line, line, line, line,
        ),
        in_specs=[hbm()] * 6,
        out_specs=(vmem(),) * 11,
        scratch_shapes=[
            pltpu.VMEM(incoming.shape, BF16),
            pltpu.VMEM(q.shape, F32),
            pltpu.VMEM((nodes * message_rows + window * fields, width), F32),
            pltpu.VMEM((fields, height, width), F32),
            pltpu.VMEM((height, width), F32),
            pltpu.VMEM((width, height), F32),
            pltpu.SemaphoreType.DMA((5 + CHUNKS,)),
        ],
        compiler_params=params(10),
        name="middle_part",
    )(*pin(incoming, q, ip, mixing, land, velocity))


def top_level(coef_ref, here, t, tracers, q1, rhs):
    inv1 = coef_ref[tracers + 1, here, :]
    link0 = coef_ref[tracers, here, :]
    q1 = q1 * inv1
    top = (rhs + coef_ref[t, here, :] + link0 * q1) * coef_ref[tracers + 2, here, :]
    return q1, top


def reply_kernel(
    padded_in, r0, r1, r2, r3, vel_ref, k_ref, land_ref, ip_ref, coef_ref, pick_ref,
    padded, state_hbm, sides_hbm, coef_hbm, out_hbm,
    shifted, matrix, lines, sides, top, rows_out, packed, sems,
    *, sizes, levels, cap, window,
):
    tracers = top.shape[0]
    height = top.shape[1]
    del padded_in
    place_sides(sizes, (r0, r1), lines, sides)
    place_rows(sizes, (r2, r3), padded)
    kept = copies_of(
        [(padded, state_hbm), (sides, sides_hbm), (coef_ref, coef_hbm)], sems, 2
    )

    def finish(level, r, q, tops):
        if level == 0:
            here = pl.ds(r, 8)
            sea = land_ref[here, :].astype(F32)
            for t in range(tracers):
                _, x = top_level(coef_ref, here, t, tracers, q[t], tops[t])
                top[t, here, :] = x * sea

    sweep(padded, vel_ref, k_ref, land_ref, ip_ref, sides, shifted, matrix, finish, levels)
    nodes = out_hbm.shape[0]
    per = cap * tracers
    picked = pick_ref[...]
    for t in range(tracers):
        rows = jnp.dot(picked, top[t].astype(BF16), preferred_element_type=F32)
        for n in range(nodes):
            rows_out[pl.ds(n * per + t, cap, stride=tracers), :] = rows[
                n * window : n * window + cap, :
            ]
    parts = 2
    share = nodes // parts
    copies = []
    for part in range(parts):
        for n in range(part * share, (part + 1) * share):
            packed[n] = rows_out[n * per : (n + 1) * per, :].astype(BF16)
        here = pl.ds(part * share, share)
        copy = pltpu.make_async_copy(packed.at[here], out_hbm.at[here], sems.at[part])
        copy.start()
        copies.append(copy)
    for copy in copies + kept:
        copy.wait()


def replies(sizes, padded, received, velocity, mixing, land, ip, coef, pick, nodes, levels, cap, window):
    count, height, width = padded.shape
    height -= 2 * PAD
    tracers = count // levels
    scratch = sweep_scratch(count, height, width)
    return pl.pallas_call(
        functools.partial(reply_kernel, sizes=sizes, levels=levels, cap=cap, window=window),
        out_shape=(
            jax.ShapeDtypeStruct(padded.shape, F32),
            pltpu.HBM(padded.shape, F32),
            pltpu.HBM((height, width), F32),
            pltpu.HBM(coef.shape, F32),
            pltpu.HBM((nodes, cap * tracers, width), BF16),
        ),
        in_specs=[vmem()] * 11,
        out_specs=(vmem(),) + (hbm(),) * 4,
        input_output_aliases={0: 0},
        scratch_shapes=scratch
        + [
            pltpu.VMEM((tracers, height, width), F32),
            pltpu.VMEM((nodes * cap * tracers, width), F32),
            pltpu.VMEM((nodes, cap * tracers, width), BF16),
            pltpu.SemaphoreType.DMA((5,)),
        ],
        compiler_params=params(12),
        name="replies",
    )(padded, *received, velocity, mixing, land, ip, coef, pick)


def last_kernel(
    padded_hbm, sides_hbm, vel_hbm, k_hbm, land_hbm, ip_hbm, coef_hbm,
    out_hbm, shifted, matrix, padded, sides, vel_ref, k_ref, land_ref, ip_ref, coef_ref, out_ref,
    sems, *, levels,
):
    height = out_ref.shape[1]
    rows = height // CHUNKS
    early = copies_of(
        [
            (sides_hbm, sides), (vel_hbm, vel_ref), (k_hbm, k_ref), (land_hbm, land_ref),
            (ip_hbm, ip_ref), (coef_hbm, coef_ref), (padded_hbm, padded),
        ],
        sems,
    )
    for copy in early:
        copy.wait()
    outs = []

    def done(chunk):
        here = pl.ds(chunk * rows, rows)
        outs.extend(copies_of([(out_ref.at[:, here, :], out_hbm.at[:, here, :])], sems, chunk))

    count = out_ref.shape[0]
    tracers = count // levels

    def finish(level, r, q, tops):
        here = pl.ds(r, 8)
        if level >= 2:
            for t in range(tracers):
                out_ref[t * levels + level, here, :] = q[t]
        if level == 0:
            sea = land_ref[here, :].astype(F32)
            down = [None, coef_ref[tracers, here, :] * coef_ref[tracers + 1, here, :]]
            for lower in range(2, levels):
                down.append(k_ref[lower - 1, here, :] * sea * ip_ref[lower, here, :])
            for t in range(tracers):
                q1, x = top_level(coef_ref, here, t, tracers, q[t], tops[t])
                out_ref[t * levels, here, :] = x
                x = q1 + down[1] * x
                out_ref[t * levels + 1, here, :] = x
                for lower in range(2, levels):
                    x = out_ref[t * levels + lower, here, :] + down[lower] * x
                    out_ref[t * levels + lower, here, :] = x

    sweep(
        padded, vel_ref, k_ref, land_ref, ip_ref, sides, shifted, matrix, finish, levels,
        done=done,
    )
    for copy in outs:
        copy.wait()


def last_part(padded, sides, velocity, mixing, land, ip, coef, levels):
    count, height, width = padded.shape
    height -= 2 * PAD
    return pl.pallas_call(
        functools.partial(last_kernel, levels=levels),
        out_shape=pltpu.HBM((count, height, width), F32),
        in_specs=[hbm()] * 7,
        out_specs=hbm(),
        scratch_shapes=sweep_scratch(count, height, width)[:2]
        + [
            pltpu.VMEM(padded.shape, F32),
            pltpu.VMEM(sides.shape, F32),
            pltpu.VMEM(velocity.shape, F32),
            pltpu.VMEM(mixing.shape, F32),
            pltpu.VMEM(land.shape, land.dtype),
            pltpu.VMEM(ip.shape, F32),
            pltpu.VMEM(coef.shape, F32),
            pltpu.VMEM((count, height, width), F32),
            pltpu.SemaphoreType.DMA((7,)),
        ],
        compiler_params=params(20),
        name="last_part",
    )(*pin(padded, sides, velocity, mixing, land, ip, coef))


def back_kernel(
    slot_hbm, atm_hbm, rows_hbm, returned_hbm, weights_hbm, out_hbm,
    slot_ref, atm_ref, rows_ref, returned_ref, weights_ref, out_ref, wide, total, sems,
    *, tracers, cells, steps,
):
    nodes, per, width = returned_ref.shape
    pairs = weights_ref.shape[0]
    per_step = pairs // steps
    copies = copies_of(
        [
            (returned_hbm, returned_ref), (slot_hbm, slot_ref), (atm_hbm, atm_ref),
            (rows_hbm, rows_ref),
        ],
        sems,
    )
    parts = copies_of(
        [
            (
                weights_hbm.at[pl.ds(n * per_step, per_step)],
                weights_ref.at[pl.ds(n * per_step, per_step)],
            )
            for n in range(steps)
        ],
        sems,
        len(copies),
    )
    total[...] = jnp.zeros(total.shape, F32)
    wide[nodes * per :, :] = jnp.zeros((wide.shape[0] - nodes * per, width), F32)
    copies[0].wait()
    for n in range(nodes):
        wide[n * per : (n + 1) * per, :] = returned_ref[n].astype(F32)
    for copy in copies[1:]:
        copy.wait()
    for p in range(pairs):
        if p % per_step == 0:
            parts[p // per_step].wait()
        lhs = wide[pl.ds(slot_ref[p] * tracers, 8), :].astype(BF16)
        product = lax.dot_general(
            lhs, weights_ref[p], (((1,), (1,)), ((), ())), preferred_element_type=F32
        )
        b = atm_ref[p]
        total[b] = total[b] + product
    lane = lane_iota((tracers, cells))

    def write(b, carry):
        out_ref[b] = jnp.where(lane < rows_ref[b], total[b][:tracers], 0.0)
        return carry

    lax.fori_loop(0, out_ref.shape[0], write, 0, unroll=8)
    for copy in copies_of([(out_ref, out_hbm)], sems):
        copy.wait()


def back(slots, atm, rows, returned, weights, tracers):
    pairs, cells, width = weights.shape
    nodes, per, _ = returned.shape
    blocks = rows.shape[0]
    ints = jnp.int32
    steps = 4
    return pl.pallas_call(
        functools.partial(back_kernel, tracers=tracers, cells=cells, steps=steps),
        out_shape=pltpu.HBM((blocks, tracers, cells), F32),
        in_specs=[hbm()] * 5,
        out_specs=hbm(),
        scratch_shapes=[
            pltpu.SMEM((pairs,), ints),
            pltpu.SMEM((pairs,), ints),
            pltpu.SMEM((blocks,), ints),
            pltpu.VMEM(returned.shape, BF16),
            pltpu.VMEM(weights.shape, BF16),
            pltpu.VMEM((blocks, tracers, cells), F32),
            pltpu.VMEM((nodes * per + 8, width), F32),
            pltpu.VMEM((blocks, 8, cells), F32),
            pltpu.SemaphoreType.DMA((4 + steps,)),
        ],
        compiler_params=params(8),
        name="back",
    )(*pin(slots, atm, rows, returned, weights))


def all_to_all(x):
    return lax.all_to_all(x, AXES, split_axis=0, concat_axis=0, tiled=True)


def on_device(
    atm_flux,
    atm_rows,
    regrid_weights,
    pair_dest,
    pair_atm,
    pair_row,
    tracers,
    velocity,
    mixing,
    land,
    *,
    mesh_sizes,
):
    n_tx, n_ty, n_tz = mesh_sizes
    groups = n_ty * n_tz
    nodes = n_tx * groups
    pairs = pair_atm.shape[0]
    cap = max(2, (2 * pairs + nodes - 1) // nodes)
    window = -(-cap // 8) * 8
    fields = atm_flux.shape[1]
    tracer_count, levels, height, width = tracers.shape
    state = tracers.reshape(tracer_count * levels, height, width)
    message, slots = contributions(
        mesh_sizes, pair_dest[:, 0], pair_atm, pair_row, atm_rows, atm_flux, regrid_weights,
        nodes, cap, window,
    )
    incoming = all_to_all(message)
    padded, *lines = edges(mesh_sizes, slots, state)
    received = exchange(lines, mesh_sizes)
    _, q, ip = first_part(mesh_sizes, padded, received, velocity, mixing, land, levels)
    padded, coef, pick, ip_near, mixing_near, land_near, velocity_near, *lines = middle_part(
        mesh_sizes, incoming, q, ip, mixing, land, velocity, fields, levels, cap, window
    )
    received = exchange(lines, mesh_sizes)
    _, state, sides, coef, answer = replies(
        mesh_sizes, padded, received, velocity_near, mixing_near, land_near, ip_near, coef, pick,
        nodes, levels, cap, window,
    )
    returned = all_to_all(answer)
    out = last_part(state, sides, velocity, mixing, land, ip, coef, levels)
    atm_surface = back(slots, pair_atm, atm_rows, returned, regrid_weights, tracer_count)
    return (out.reshape(tracers.shape), atm_surface)


def solution(mesh):
    in_specs = (
        P(("ens", "tx", "ty", "tz"), None, None),
        P(("tx", "ty", "tz")),
        P(("tx", "ty", "tz"), None, None),
        P(("tx", "ty", "tz"), None),
        P(("tx", "ty", "tz")),
        P(("tx", "ty", "tz")),
        P("ens", None, ("ty", "tz"), "tx"),
        P("ens", None, ("ty", "tz"), "tx"),
        P("ens", ("ty", "tz"), "tx"),
        P(("ty", "tz"), "tx"),
    )
    out_specs = (P("ens", None, ("ty", "tz"), "tx"), P(("ens", "tx", "ty", "tz"), None, None))
    mesh_sizes = tuple(mesh.shape[name] for name in AXES)
    return jax.shard_map(
        functools.partial(on_device, mesh_sizes=mesh_sizes),
        mesh=mesh, in_specs=in_specs, out_specs=out_specs, check_vma=False,
    )
```

time: 91.4 us -> 66.9 us (0.73)
  local copies, waits for them, and re-layouts: 30.2 us -> 3.1 us
  Pallas kernels: 32.7 us -> 34.9 us
  waiting for transfers between devices: 4.71 us -> 6.59 us
    unnamed x79 -> x11, local copies, waits for them, and re-layouts: 30 us -> 3.1 us
    pallas_call x7, Pallas kernels: 32.7 us -> 34.9 us  [the longest x1 8.86 us: last_part(): pl.pallas_call(functools.partial(last_kernel, levels=levels), out_shape=p...]
    all_to_all x2, waiting for transfers between devices: 0.01 us -> 1.69 us  [all_to_all(): return lax.all_to_all(x, AXES, split_axis=0, concat_axis=0, tiled=True)]
  transfers between devices with their start and end apart: 10 -> 10, of which waited for: 3 -> 5; matrix products, arithmetic and copies ran while one was open for 0% -> 0% of each run, Pallas kernels for 17% -> 26%
where the time goes in v2:
time: 66.9 us; the launch traced here: 66.5 us
  Pallas kernels  34.9 us (52%)
  starting transfers between devices  21.2 us (32%)
  waiting for transfers between devices  6.59 us (10%)
  local copies, waits for them, and re-layouts  3.1 us (5%)
  between operations  0.76 us (1%)
    all_to_all x2, starting transfers between devices, all_to_all(): return lax.all_to_all(x, AXES, split_axis=0, concat_axis=0, tiled=True)  11.1 us
    ppermute x8, starting transfers between devices, exchange(): return [lax.ppermute(line, AXES, perm) for line, perm in zip(lines, perms)]  10.1 us
    pallas_call x1, Pallas kernels, last_part(): pl.pallas_call(functools.partial(last_kernel, levels=levels), out_shape=p...  8.86 us
    pallas_call x1, Pallas kernels, replies(): pl.pallas_call(functools.partial(reply_kernel, sizes=sizes, levels=levels...  5.56 us
    pallas_call x1, Pallas kernels, first_part(): pl.pallas_call(functools.partial(first_kernel, sizes=sizes, levels=levels...  5.34 us
    ppermute x8, waiting for transfers between devices, exchange(): return [lax.ppermute(line, AXES, perm) for line, perm in zip(lines, perms)]  4.9 us
    pallas_call x1, Pallas kernels, middle_part(): pl.pallas_call(functools.partial(middle_kernel, sizes=sizes, levels=level...  4.19 us
    pallas_call x1, Pallas kernels, back(): pl.pallas_call(functools.partial(back_kernel, tracers=tracers, cells=cell...  4.11 us
  transfers between devices with their start and end apart: 10, of which 5 were waited for; matrix products, arithmetic and copies ran while one was open for 0% of the time, Pallas kernels for 26%

profile of v2, /device:TPU:0, one launch (start us, length us, event | category | flops | bytes accessed | tf_op | source)
XLA Modules:
  0.0 66.5 jit_solution(16841432382633707235)
XLA Ops:
  0.6 0.0 copy-start
  0.7 3.6 %contributions.1 = (bf16[16,104,128]{2,1,0:T(8,128)(2,1)}, s32[96]{0:T(128)}) custom-call(s32[96]{0:T(128)} %bitcast.5, s32[96]{0:T(128)} %atm_hbm.3, s32[96]{0:T(128)} %row_hbm.1, s32[48]{0:T(128)} %rows_hbm.3, bf16[48,8,128]{2,1,0:T(8,128)(2,1)} %flux_hbm.1, bf16[96,128,128]{2,1,0:T(8,128)(2,1)} %weights_hbm.3), custom_call_target="tpu_custom_call" | custom-call | tf_op jit(solution)/shard_map/contributions/pallas_call | solution.py:170
  4.3 7.4 %all-to-all-start = ((bf16[16,104,128]{2,1,0:T(8,128)(2,1)}), bf16[16,104,128]{2,1,0:T(8,128)(2,1)S(1)}, u32[]{:S(2)}, u32[]{:S(2)}) async-start(bf16[16,104,128]{2,1,0:T(8,128)(2,1)} %get-tuple-element.26), calls=%async_computation | async-start | bytes 851968 | tf_op jit(solution)/shard_map/all_to_all | solution.py:835
  11.7 3.2 %edges.1 = (f32[48,144,128]{2,1,0:T(8,128)S(1)}, f32[48,128]{1,0:T(8,128)S(1)}, f32[48,128]{1,0:T(8,128)S(1)}, f32[48,128]{1,0:T(8,128)S(1)}, f32[48,128]{1,0:T(8,128)S(1)}) custom-call(s32[96]{0:T(128)} %get-tuple-element.27.order.slot_hbm, f32[48,128,128]{2,1,0:T(8,128)} %bitcast.3), custom_call_target="tpu_custom_call" | custom-call | tf_op jit(solution)/shard_map/edges/pallas_call | solution.py:246
  14.9 2.0 %collective-permute-start = (f32[48,128]{1,0:T(8,128)S(1)}, f32[48,128]{1,0:T(8,128)S(1)}, u32[]{:S(2)}, u32[]{:S(2)}) collective-permute-start(f32[48,128]{1,0:T(8,128)S(1)} %get-tuple-element.29), channel_id=1, source_target_pairs={{0,4},{1,5},{2,6},{3,7},{4,0},{5,1},{6,2},{7,3},{8,12},{9,13},{10,... | collective-permute-start | bytes 73736 | tf_op jit(solution)/shard_map/ppermute | solution.py:277
  16.9 0.5 collective-permute-start.2
  17.4 1.1 %collective-permute-start.3 = (f32[48,128]{1,0:T(8,128)S(1)}, f32[48,128]{1,0:T(8,128)S(1)}, u32[]{:S(2)}, u32[]{:S(2)}) collective-permute-start(f32[48,128]{1,0:T(8,128)S(1)} %get-tuple-element.32), channel_id=1, source_target_pairs={{0,3},{1,2},{2,1},{3,0},{4,7},{5,6},{6,5},{7,4},{8,11},{9,10},{10,... | collective-permute-start | bytes 73736 | tf_op jit(solution)/shard_map/ppermute | solution.py:277
  18.5 1.9 %collective-permute-done.r0 = f32[48,128]{1,0:T(8,128)S(1)} collective-permute-done((f32[48,128]{1,0:T(8,128)S(1)}, f32[48,128]{1,0:T(8,128)S(1)}, u32[]{:S(2)}, u32[]{:S(2)}) %collective-permute-start) | collective-permute-done | bytes 24608 | tf_op jit(solution)/shard_map/ppermute | solution.py:277
  20.4 0.7 %collective-permute-done.3.r3 = f32[48,128]{1,0:T(8,128)S(1)} collective-permute-done((f32[48,128]{1,0:T(8,128)S(1)}, f32[48,128]{1,0:T(8,128)S(1)}, u32[]{:S(2)}, u32[]{:S(2)}) %collective-permute-start.3) | collective-permute-done | bytes 24608 | tf_op jit(solution)/shard_map/ppermute | solution.py:277
  21.1 5.3 %first_part.1 = (f32[48,144,128]{2,1,0:T(8,128)S(1)}, f32[48,128,128]{2,1,0:T(8,128)}, f32[8,128,128]{2,1,0:T(8,128)}) custom-call(f32[48,144,128]{2,1,0:T(8,128)S(1)} %get-tuple-element.28.padded_in, f32[48,128]{1,0:T(8,128)S(1)} %collective-permute-done.r0, f32[48,128]{1,0:T(8,128)S(1)} %collective-permute-done.1.r1, ...), custom_call_target="tpu_custom_call", output_to_operand_aliasing={{0}: (0, {})} | custom-call | tf_op jit(solution)/shard_map/first_part/pallas_call | solution.py:440
  26.5 0.7 %copy-done.3 = bf16[16,104,128]{2,1,0:T(8,128)(2,1)} copy-done((bf16[16,104,128]{2,1,0:T(8,128)(2,1)}, bf16[16,104,128]{2,1,0:T(8,128)(2,1)S(1)}, u32[]{:S(2)}) %copy-start.3) | copy-done | bytes 426008
  27.2 4.2 %middle_part.1 = (f32[48,144,128]{2,1,0:T(8,128)S(1)}, f32[9,128,128]{2,1,0:T(8,128)S(1)}, bf16[256,128]{1,0:T(8,128)(2,1)S(1)}, f32[8,128,128]{2,1,0:T(8,128)S(...) custom-call(bf16[16,104,128]{2,1,0:T(8,128)(2,1)} %copy-done.3, ...), custom_call_target="tpu_custom_call" | custom-call | tf_op jit(solution)/shard_map/middle_part/pallas_call | solution.py:565
  31.4 4.9 %collective-permute-start.4 = (f32[48,128]{1,0:T(8,128)S(1)}, f32[48,128]{1,0:T(8,128)S(1)}, u32[]{:S(2)}, u32[]{:S(2)}) collective-permute-start(f32[48,128]{1,0:T(8,128)S(1)} %get-tuple-element.36), channel_id=1, source_target_pairs={{0,4},{1,5},{2,6},{3,7},{4,0},{5,1},{6,2},{7,3},{8,12},{9,13},{10,... | collective-permute-start | bytes 73736 | tf_op jit(solution)/shard_map/ppermute | solution.py:277
  36.3 0.5 collective-permute-start.6
  36.8 1.1 %collective-permute-start.7 = (f32[48,128]{1,0:T(8,128)S(1)}, f32[48,128]{1,0:T(8,128)S(1)}, u32[]{:S(2)}, u32[]{:S(2)}) collective-permute-start(f32[48,128]{1,0:T(8,128)S(1)} %get-tuple-element.39), channel_id=1, source_target_pairs={{0,3},{1,2},{2,1},{3,0},{4,7},{5,6},{6,5},{7,4},{8,11},{9,10},{10,... | collective-permute-start | bytes 73736 | tf_op jit(solution)/shard_map/ppermute | solution.py:277
  37.9 0.2 collective-permute-done.4.r0
  38.2 2.0 %collective-permute-done.7.r3 = f32[48,128]{1,0:T(8,128)S(1)} collective-permute-done((f32[48,128]{1,0:T(8,128)S(1)}, f32[48,128]{1,0:T(8,128)S(1)}, u32[]{:S(2)}, u32[]{:S(2)}) %collective-permute-start.7) | collective-permute-done | bytes 24608 | tf_op jit(solution)/shard_map/ppermute | solution.py:277
  40.2 5.6 %replies.1 = (f32[48,144,128]{2,1,0:T(8,128)S(1)}, f32[48,144,128]{2,1,0:T(8,128)}, f32[128,128]{1,0:T(8,128)}, f32[9,128,128]{2,1,0:T(8,128)}, bf16[16,72,128]{2,1,0:T(8,128)(2,1)}) custom-call(f32[48,144,128]{2,1,0:T(8,128)S(1)} %get-tuple-element.35.padded_in, f32[48,128]{1,0:T(8,128)S(1)} %collective-permute-done.4.r0, ...), custom_call_target="tpu_custom_call", output_to_operand_aliasing={{0}: (0, {})} | custom-call | tf_op jit(solution)/shard_map/replies/pallas_call | solution.py:653
  45.8 3.8 %all-to-all-start.1 = ((bf16[16,72,128]{2,1,0:T(8,128)(2,1)}), bf16[16,72,128]{2,1,0:T(8,128)(2,1)S(1)}, u32[]{:S(2)}, u32[]{:S(2)}) async-start(bf16[16,72,128]{2,1,0:T(8,128)(2,1)} %get-tuple-element.49), calls=%async_computation.1 | async-start | bytes 589824 | tf_op jit(solution)/shard_map/all_to_all | solution.py:835
  49.5 8.9 %last_part.1 = f32[48,128,128]{2,1,0:T(8,128)} custom-call(f32[48,144,128]{2,1,0:T(8,128)} %get-tuple-element.46.padded_hbm, f32[128,128]{1,0:T(8,128)} %get-tuple-element.47.sides_hbm, f32[2,8,128,128]{3,2,1,0:T(8,128)} %vel_hbm.3, f32[7,128,128]{2,1,0:T(8,128)} %k_hbm.3, s32[128,128]{1,0:T(8,128)} %land_hbm.3, f32[8,128,128]{2,1,0:T(8,128)} %get-tuple-element.34.ip_hbm, ...), custom_call_target="tpu_custom_call" | custom-call | tf_op jit(solution)/shard_map/last_part/pallas_call | solution.py:732
  58.4 1.7 %all-to-all-done.1.returned_hbm = bf16[16,72,128]{2,1,0:T(8,128)(2,1)S(1)} async-done(((bf16[16,72,128]{2,1,0:T(8,128)(2,1)}), bf16[16,72,128]{2,1,0:T(8,128)(2,1)S(1)}, u32[]{:S(2)}, u32[]{:S(2)}) %all-to-all-start.1) | async-done | bytes 294944 | tf_op jit(solution)/shard_map/all_to_all | solution.py:835
  60.1 0.7 %copy-done.4 = bf16[16,72,128]{2,1,0:T(8,128)(2,1)} copy-done((bf16[16,72,128]{2,1,0:T(8,128)(2,1)}, bf16[16,72,128]{2,1,0:T(8,128)(2,1)S(1)}, u32[]{:S(2)}) %copy-start.4) | copy-done | bytes 294936
  60.8 4.1 %back.1 = f32[48,6,128]{2,1,0:T(8,128)} custom-call(s32[96]{0:T(128)} %get-tuple-element.27.order.slot_hbm, s32[96]{0:T(128)} %atm_hbm.3, s32[48]{0:T(128)} %rows_hbm.3, bf16[16,72,128]{2,1,0:T(8,128)(2,1)} %copy-done.4, bf16[96,128,128]{2,1,0:T(8,128)(2,1)} %weights_hbm.3), custom_call_target="tpu_custom_call" | custom-call | tf_op jit(solution)/shard_map/back/pallas_call | solution.py:813
  64.9 1.6 %copy.14 = f32[48,6,128]{2,0,1:T(8,128)} copy(f32[48,6,128]{2,1,0:T(8,128)} %back.1) | data formatting | bytes 294912
  (14 shorter events, 0.0 us)
Async XLA Ops:
  0.6 20.5 %copy-start = (f32[2,8,128,128]{3,2,1,0:T(8,128)S(1)}, f32[2,8,128,128]{3,2,1,0:T(8,128)}, u32[]{:S(2)}) copy-start(f32[2,8,128,128]{3,2,1,0:T(8,128)} %vel_hbm.3) | copy-start | bytes 3145732
  0.6 20.5 %copy-start.1 = (f32[7,128,128]{2,1,0:T(8,128)S(1)}, f32[7,128,128]{2,1,0:T(8,128)}, u32[]{:S(2)}) copy-start(f32[7,128,128]{2,1,0:T(8,128)} %k_hbm.3) | copy-start | bytes 1376260
  0.7 20.5 %copy-start.2 = (s32[128,128]{1,0:T(8,128)S(1)}, s32[128,128]{1,0:T(8,128)}, u32[]{:S(2)}) copy-start(s32[128,128]{1,0:T(8,128)} %land_hbm.3) | copy-start | bytes 196612
  4.3 22.2 %all-to-all-start = ((bf16[16,104,128]{2,1,0:T(8,128)(2,1)}), bf16[16,104,128]{2,1,0:T(8,128)(2,1)S(1)}, u32[]{:S(2)}, u32[]{:S(2)}) async-start(bf16[16,104,128]{2,1,0:T(8,128)(2,1)} %get-tuple-element.26), calls=%async_computation | async-start | bytes 851968 | tf_op jit(solution)/shard_map/all_to_all | solution.py:835
  14.9 5.5 %collective-permute-start = (f32[48,128]{1,0:T(8,128)S(1)}, f32[48,128]{1,0:T(8,128)S(1)}, u32[]{:S(2)}, u32[]{:S(2)}) collective-permute-start(f32[48,128]{1,0:T(8,128)S(1)} %get-tuple-element.29), channel_id=1, source_target_pairs={{0,4},{1,5},{2,6},{3,7},{4,0},{5,1},{6,2},{7,3},{8,12},{9,13},{10,... | collective-permute-start | bytes 73736 | tf_op jit(solution)/shard_map/ppermute | solution.py:277
  16.9 3.5 %collective-permute-start.1 = (f32[48,128]{1,0:T(8,128)S(1)}, f32[48,128]{1,0:T(8,128)S(1)}, u32[]{:S(2)}, u32[]{:S(2)}) collective-permute-start(f32[48,128]{1,0:T(8,128)S(1)} %get-tuple-element.30), channel_id=1, source_target_pairs={{0,1},{1,0},{2,3},{3,2},{4,8},{5,9},{6,10},{7,11},{8,4},{9,5},{10,... | collective-permute-start | bytes 73736 | tf_op jit(solution)/shard_map/ppermute | solution.py:277
  16.9 3.5 %collective-permute-start.2 = (f32[48,128]{1,0:T(8,128)S(1)}, f32[48,128]{1,0:T(8,128)S(1)}, u32[]{:S(2)}, u32[]{:S(2)}) collective-permute-start(f32[48,128]{1,0:T(8,128)S(1)} %get-tuple-element.31), channel_id=1, source_target_pairs={{0,1},{1,0},{2,3},{3,2},{4,5},{5,4},{6,7},{7,6},{8,9},{9,8},{10,11... | collective-permute-start | bytes 73736 | tf_op jit(solution)/shard_map/ppermute | solution.py:277
  17.4 3.7 %collective-permute-start.3 = (f32[48,128]{1,0:T(8,128)S(1)}, f32[48,128]{1,0:T(8,128)S(1)}, u32[]{:S(2)}, u32[]{:S(2)}) collective-permute-start(f32[48,128]{1,0:T(8,128)S(1)} %get-tuple-element.32), channel_id=1, source_target_pairs={{0,3},{1,2},{2,1},{3,0},{4,7},{5,6},{6,5},{7,4},{8,11},{9,10},{10,... | collective-permute-start | bytes 73736 | tf_op jit(solution)/shard_map/ppermute | solution.py:277
  26.5 0.8 %copy-start.3 = (bf16[16,104,128]{2,1,0:T(8,128)(2,1)}, bf16[16,104,128]{2,1,0:T(8,128)(2,1)S(1)}, u32[]{:S(2)}) copy-start(bf16[16,104,128]{2,1,0:T(8,128)(2,1)S(1)} %all-to-all-done.incoming_hbm) | copy-start | bytes 1277956
  31.4 6.7 %collective-permute-start.4 = (f32[48,128]{1,0:T(8,128)S(1)}, f32[48,128]{1,0:T(8,128)S(1)}, u32[]{:S(2)}, u32[]{:S(2)}) collective-permute-start(f32[48,128]{1,0:T(8,128)S(1)} %get-tuple-element.36), channel_id=1, source_target_pairs={{0,4},{1,5},{2,6},{3,7},{4,0},{5,1},{6,2},{7,3},{8,12},{9,13},{10,... | collective-permute-start | bytes 73736 | tf_op jit(solution)/shard_map/ppermute | solution.py:277
  36.3 1.8 %collective-permute-start.5 = (f32[48,128]{1,0:T(8,128)S(1)}, f32[48,128]{1,0:T(8,128)S(1)}, u32[]{:S(2)}, u32[]{:S(2)}) collective-permute-start(f32[48,128]{1,0:T(8,128)S(1)} %get-tuple-element.37), channel_id=1, source_target_pairs={{0,1},{1,0},{2,3},{3,2},{4,8},{5,9},{6,10},{7,11},{8,4},{9,5},{10,... | collective-permute-start | bytes 73736 | tf_op jit(solution)/shard_map/ppermute | solution.py:277
  36.3 1.8 %collective-permute-start.6 = (f32[48,128]{1,0:T(8,128)S(1)}, f32[48,128]{1,0:T(8,128)S(1)}, u32[]{:S(2)}, u32[]{:S(2)}) collective-permute-start(f32[48,128]{1,0:T(8,128)S(1)} %get-tuple-element.38), channel_id=1, source_target_pairs={{0,1},{1,0},{2,3},{3,2},{4,5},{5,4},{6,7},{7,6},{8,9},{9,8},{10,11... | collective-permute-start | bytes 73736 | tf_op jit(solution)/shard_map/ppermute | solution.py:277
  36.8 3.3 %collective-permute-start.7 = (f32[48,128]{1,0:T(8,128)S(1)}, f32[48,128]{1,0:T(8,128)S(1)}, u32[]{:S(2)}, u32[]{:S(2)}) collective-permute-start(f32[48,128]{1,0:T(8,128)S(1)} %get-tuple-element.39), channel_id=1, source_target_pairs={{0,3},{1,2},{2,1},{3,0},{4,7},{5,6},{6,5},{7,4},{8,11},{9,10},{10,... | collective-permute-start | bytes 73736 | tf_op jit(solution)/shard_map/ppermute | solution.py:277
  45.8 14.3 %all-to-all-start.1 = ((bf16[16,72,128]{2,1,0:T(8,128)(2,1)}), bf16[16,72,128]{2,1,0:T(8,128)(2,1)S(1)}, u32[]{:S(2)}, u32[]{:S(2)}) async-start(bf16[16,72,128]{2,1,0:T(8,128)(2,1)} %get-tuple-element.49), calls=%async_computation.1 | async-start | bytes 589824 | tf_op jit(solution)/shard_map/all_to_all | solution.py:835
  60.1 0.7 %copy-start.4 = (bf16[16,72,128]{2,1,0:T(8,128)(2,1)}, bf16[16,72,128]{2,1,0:T(8,128)(2,1)S(1)}, u32[]{:S(2)}) copy-start(bf16[16,72,128]{2,1,0:T(8,128)(2,1)S(1)} %all-to-all-done.1.returned_hbm) | copy-start | bytes 884740

commit v3 on v2

--- a/solution.py
+++ b/solution.py
@@ -198,8 +198,16 @@
     )(*pin(dest, atm, row, rows, flux, weights))
 
 
-def column_lines(collected):
-    return collected.T
+def gather_columns(acc, lane, tile, n):
+    width = tile.shape[1]
+    moved = pltpu.roll(tile, (2 * n + 2) % width, 1)
+    return jnp.where((lane == 2 * n + 1) | (lane == 2 * n + 2), moved, acc)
+
+
+def scatter_columns(lane, lines, n):
+    width = lines.shape[1]
+    moved = pltpu.roll(lines, (width - (2 * n + 2)) % width, 1)
+    return jnp.where((lane == 0) | (lane == width - 1), moved, 0.0)
 
 
 def store_sends(sizes, lines_ref, row_first, row_last, sends):
@@ -215,47 +223,18 @@
     sends[3][...] = jnp.where(g_even, row_first, row_last)
 
 
-def edges_kernel(order, c_hbm, padded, s0, s1, s2, s3, cols, lines, sems, *, sizes):
-    del order
-    count, height, width = c_hbm.shape
-    lane = lane_iota((8, width))
-    rows = height // CHUNKS
-    copies = chunk_copies(c_hbm, 0, padded, PAD, height, sems)
-    for chunk in range(CHUNKS):
-        copies[chunk].wait()
-
-        def body(i, carry):
-            r = pl.multiple_of(chunk * rows + i * 8, 8)
-            acc = jnp.zeros((8, width), F32)
-            for tl in range(count):
-                moved = pltpu.roll(padded[tl, pl.ds(PAD + r, 8), :], (2 * tl + 2) % width, 1)
-                acc = jnp.where((lane == 2 * tl + 1) | (lane == 2 * tl + 2), moved, acc)
-            cols[pl.ds(r, 8), :] = acc
-            return carry
-
-        lax.fori_loop(0, rows // 8, body, 0)
-    lines[...] = cols[...].T
-    store_sends(
-        sizes, lines, padded[:, PAD, :], padded[:, PAD + height - 1, :], (s0, s1, s2, s3)
-    )
-
-
-def edges(sizes, order, state):
-    count, height, width = state.shape
-    line = jax.ShapeDtypeStruct((count, width), F32)
-    return pl.pallas_call(
-        functools.partial(edges_kernel, sizes=sizes),
-        out_shape=(jax.ShapeDtypeStruct((count, height + 2 * PAD, width), F32),) + (line,) * 4,
-        in_specs=[hbm(), hbm()],
-        out_specs=(vmem(),) * 5,
-        scratch_shapes=[
-            pltpu.VMEM((height, width), F32),
-            pltpu.VMEM((width, height), F32),
-            pltpu.SemaphoreType.DMA((CHUNKS,)),
-        ],
-        compiler_params=params(4),
-        name="edges",
-    )(*pin(order, state))
+def sort_halos(sizes, received, halos):
+    tx, group, groups = place_of(sizes)
+    tx_even = lax.rem(tx, 2) == 0
+    g_even = lax.rem(group, 2) == 0
+    r0, r1, r2, r3 = (r[...] for r in received)
+    zero = jnp.zeros(r0.shape, F32)
+    r1 = jnp.where((tx == 0) | (tx == sizes[0] - 1), zero, r1)
+    r3 = jnp.where((group == 0) | (group == groups - 1), zero, r3)
+    halos[0] = jnp.where(tx_even, r0, r1)
+    halos[1] = jnp.where(tx_even, r1, r0)
+    halos[2] = jnp.where(g_even, r2, r3)
+    halos[3] = jnp.where(g_even, r3, r2)
 
 
 def exchange(lines, mesh_sizes):
@@ -277,79 +256,83 @@
     return [lax.ppermute(line, AXES, perm) for line, perm in zip(lines, perms)]
 
 
-def place_sides(sizes, received, lines, sides):
-    count = received[0].shape[0]
-    tx, _, _ = place_of(sizes)
-    tx_even = lax.rem(tx, 2) == 0
-    zero = jnp.zeros(received[0].shape, F32)
-    r0, r1 = (r[...] for r in received)
-    r1 = jnp.where((tx == 0) | (tx == sizes[0] - 1), zero, r1)
-    lines[...] = jnp.zeros(lines.shape, F32)
-    lines[pl.ds(1, count, stride=2), :] = jnp.where(tx_even, r0, r1)
-    lines[pl.ds(2, count, stride=2), :] = jnp.where(tx_even, r1, r0)
-    sides[...] = lines[...].T
-
-
-def place_rows(sizes, received, padded):
-    count = padded.shape[0]
-    height = padded.shape[1] - 2 * PAD
-    _, group, groups = place_of(sizes)
-    g_even = lax.rem(group, 2) == 0
-    r2, r3 = (r[...] for r in received)
-    r3 = jnp.where((group == 0) | (group == groups - 1), jnp.zeros(r3.shape, F32), r3)
-    north = jnp.where(g_even, r2, r3)
-    south = jnp.where(g_even, r3, r2)
-    for tl in range(count):
-        padded[tl, PAD + height : PAD + height + 1, :] = north[tl : tl + 1, :]
-        padded[tl, PAD - 1 : PAD, :] = south[tl : tl + 1, :]
-
-
-def shift_matrix(width):
-    k = lax.broadcasted_iota(jnp.int32, (2 * width, 2 * width), 0) % width
-    n = lax.broadcasted_iota(jnp.int32, (2 * width, 2 * width), 1)
-    j = n % width
-    east = jnp.where(k == j + 1, 1.0, 0.0)
-    west = jnp.where(k == j - 1, 1.0, 0.0)
-    here = jnp.where(k == j, 4.0, 0.0)
-    return jnp.where(n < width, east - west, east + west - here).astype(BF16)
-
-
-def sweep(padded, vel_ref, k_ref, land_ref, ip_ref, sides, shifted, matrix, finish, levels, wait=None, done=None):
+def clear_pads(padded):
+    count, padded_height, width = padded.shape
+    zero = jnp.zeros((count, PAD, width), F32)
+    padded[:, :PAD, :] = zero
+    padded[:, padded_height - PAD :, :] = zero
+
+
+def edges_kernel(order, c_hbm, padded, s0, s1, s2, s3, cols, lines, sems, *, sizes):
+    del order
+    count, height, width = c_hbm.shape
+    lane = lane_iota((8, width))
+    rows = height // CHUNKS
+    copies = chunk_copies(c_hbm, 0, padded, PAD, height, sems)
+    clear_pads(padded)
+    for chunk in range(CHUNKS):
+        copies[chunk].wait()
+
+        def body(i, carry):
+            r = pl.multiple_of(chunk * rows + i * 8, 8)
+            acc = jnp.zeros((8, width), F32)
+            for tl in range(count):
+                acc = gather_columns(acc, lane, padded[tl, pl.ds(PAD + r, 8), :], tl)
+            cols[pl.ds(r, 8), :] = acc
+            return carry
+
+        lax.fori_loop(0, rows // 8, body, 0, unroll=2)
+    lines[...] = cols[...].T
+    store_sends(
+        sizes, lines, padded[:, PAD, :], padded[:, PAD + height - 1, :], (s0, s1, s2, s3)
+    )
+
+
+def edges(sizes, order, state):
+    count, height, width = state.shape
+    line = jax.ShapeDtypeStruct((count, width), F32)
+    return pl.pallas_call(
+        functools.partial(edges_kernel, sizes=sizes),
+        out_shape=(jax.ShapeDtypeStruct((count, height + 2 * PAD, width), F32),) + (line,) * 4,
+        in_specs=[hbm(), hbm()],
+        out_specs=(vmem(),) * 5,
+        scratch_shapes=[
+            pltpu.VMEM((height, width), F32),
+            pltpu.VMEM((width, height), F32),
+            pltpu.SemaphoreType.DMA((CHUNKS,)),
+        ],
+        compiler_params=params(4),
+        name="edges",
+    )(*pin(order, state))
+
+
+def sweep(padded, vel_ref, k_ref, land_ref, ip_ref, sides, finish, levels, done=None):
     count, padded_height, width = padded.shape
     height = padded_height - 2 * PAD
     tracers = count // levels
     rows = height // CHUNKS
     lane = lane_iota((8, width))
-    matrix[...] = shift_matrix(width)
     for chunk in range(CHUNKS):
-        if wait is not None:
-            wait(chunk)
         first = chunk * rows
-        x = padded[:, PAD + first : PAD + first + rows, :].reshape(count * rows, width)
-        high = x.astype(BF16)
-        low = (x - high.astype(F32)).astype(BF16)
-        both = jnp.concatenate([high, low], axis=1)
-        shifted[...] = jnp.dot(both, matrix[...], preferred_element_type=F32).reshape(
-            count, rows, 2 * width
-        )
 
         def block(i, carry):
             r = pl.multiple_of(first + i * 8, 8)
-            local = pl.multiple_of(i * 8, 8)
             sea = land_ref[pl.ds(r, 8), :].astype(F32)
-            side = sides[pl.ds(r, 8), :]
+            if sides is not None:
+                side = sides[pl.ds(r, 8), :]
             diffuse = DIFFUSION * sea
+            c_here = 1.0 - 4.0 * diffuse
             q = [None] * tracers
             for level in range(levels - 1, -1, -1):
                 half_u = 0.5 * sea * vel_ref[0, level, pl.ds(r, 8), :]
                 half_v = 0.5 * sea * vel_ref[1, level, pl.ds(r, 8), :]
                 c_north = diffuse - half_v
                 c_south = diffuse + half_v
-                c_side = jnp.where(
-                    lane == 0,
-                    diffuse + half_u,
-                    jnp.where(lane == width - 1, diffuse - half_u, 0.0),
-                )
+                c_east = diffuse - half_u
+                c_west = diffuse + half_u
+                c_side = jnp.where(lane == 0, c_west, c_east)
+                c_east = jnp.where(lane == width - 1, 0.0, c_east)
+                c_west = jnp.where(lane == 0, 0.0, c_west)
                 if level >= 1 and level < levels - 1:
                     link = k_ref[level, pl.ds(r, 8), :] * sea
                 if level >= 2:
@@ -360,11 +343,12 @@
                     c = padded[tl, pl.ds(PAD + r, 8), :]
                     north = padded[tl, pl.ds(PAD + r + 1, 8), :]
                     south = padded[tl, pl.ds(PAD + r - 1, 8), :]
-                    odd = shifted[tl, pl.ds(local, 8), :width]
-                    even = shifted[tl, pl.ds(local, 8), width:]
-                    halo = pltpu.roll(side, (width - (2 * tl + 2)) % width, 1)
-                    rhs = (c - half_u * odd) + diffuse * even
-                    rhs = rhs + (c_north * north + c_south * south) + c_side * halo
+                    east = pltpu.roll(c, width - 1, 1)
+                    west = pltpu.roll(c, 1, 1)
+                    rhs = c_here * c + (c_east * east + c_west * west)
+                    rhs = rhs + (c_north * north + c_south * south)
+                    if sides is not None:
+                        rhs = rhs + c_side * scatter_columns(lane, side, tl)
                     if level == levels - 1:
                         q[t] = rhs * inverse
                     elif level >= 2:
@@ -372,26 +356,37 @@
                     elif level == 1:
                         q[t] = rhs + link * q[t]
                     tops.append(rhs)
-                if level >= 1:
-                    finish(level, r, q, None)
-                else:
-                    finish(0, r, q, tops)
+                finish(level, r, q, tops)
             return carry
 
-        lax.fori_loop(0, rows // 8, block, 0)
+        lax.fori_loop(0, rows // 8, block, 0, unroll=2)
         if done is not None:
             done(chunk)
 
 
+def correct(edge_ref, halos, level_done, levels):
+    tracers = halos.shape[1] // levels
+    for side in range(4):
+        q = None
+        for level in range(levels - 1, -1, -1):
+            halo = halos[side, pl.ds(level, tracers, stride=levels), :]
+            rhs = edge_ref[side, 0, level : level + 1, :] * halo
+            link = edge_ref[side, 1, level : level + 1, :]
+            inverse = edge_ref[side, 2, level : level + 1, :]
+            if level == levels - 1:
+                q = rhs * inverse
+            elif level >= 2:
+                q = (rhs + link * q) * inverse
+            elif level == 1:
+                q = rhs + link * q
+            level_done(side, level, q, rhs)
+
+
 def first_kernel(
-    padded_in, r0, r1, r2, r3, vel_ref, k_ref, land_ref,
-    padded, q_hbm, ip_hbm, shifted, matrix, lines, sides, q_ref, ip_ref, sems, *, sizes, levels,
+    padded, vel_ref, k_ref, land_ref, q_ref, edge_ref, ip_hbm, edge_hbm,
+    ip_ref, cols, lines, sems, *, levels,
 ):
-    del padded_in
-    height = q_ref.shape[1]
-    rows = height // CHUNKS
-    place_sides(sizes, (r0, r1), lines, sides)
-    place_rows(sizes, (r2, r3), padded)
+    height, width = land_ref.shape
     sea = land_ref[...].astype(F32)
     below = None
     for level in range(levels - 1, 1, -1):
@@ -406,62 +401,137 @@
     lower = k_ref[1] * sea
     ip_ref[1] = 1.0 + lower - lower * lower * below
     ip_ref[0] = k_ref[0] * sea
-    outs = copies_of([(ip_ref, ip_hbm)], sems, CHUNKS)
-
-    def done(chunk):
-        here = pl.ds(chunk * rows, rows)
-        outs.extend(copies_of([(q_ref.at[:, here, :], q_hbm.at[:, here, :])], sems, chunk))
+    outs = copies_of([(ip_ref, ip_hbm)], sems)
+    lane = lane_iota((8, width))
+
+    def coefficients(i, carry):
+        here = pl.ds(pl.multiple_of(i * 8, 8), 8)
+        sea8 = land_ref[here, :].astype(F32)
+        acc = jnp.zeros((8, width), F32)
+        for level in range(levels):
+            half_u = 0.5 * sea8 * vel_ref[0, level, here, :]
+            side = DIFFUSION * sea8 + jnp.where(lane == 0, half_u, -half_u)
+            acc = gather_columns(acc, lane, side, level)
+            if level >= 1 and level < levels - 1:
+                acc = gather_columns(acc, lane, k_ref[level, here, :] * sea8, levels + level)
+            if level >= 2:
+                acc = gather_columns(acc, lane, ip_ref[level, here, :], 2 * levels + level)
+        cols[here, :] = acc
+        return carry
+
+    lax.fori_loop(0, height // 8, coefficients, 0, unroll=2)
+    lines[...] = cols[...].T
+    for side in range(2):
+        for part in range(3):
+            edge_ref[side, part] = lines[
+                pl.ds(2 * levels * part + 1 + side, levels, stride=2), :
+            ]
+    for side, row, sign in ((2, height - 1, -0.5), (3, 0, 0.5)):
+        sea1 = land_ref[row : row + 1, :].astype(F32)
+        edge_ref[side, 0] = DIFFUSION * sea1 + sign * sea1 * vel_ref[1, :, row, :]
+        edge_ref[side, 1, : levels - 1, :] = k_ref[:, row, :] * sea1
+        edge_ref[side, 1, levels - 1 :, :] = jnp.zeros((1, width), F32)
+        edge_ref[side, 2] = ip_ref[:, row, :]
+    outs.extend(copies_of([(edge_ref, edge_hbm)], sems, 1))
 
     def finish(level, r, q, tops):
         values = q if level > 0 else tops
         for t, value in enumerate(values):
             q_ref[t * levels + level, pl.ds(r, 8), :] = value
 
-    sweep(
-        padded, vel_ref, k_ref, land_ref, ip_ref, sides, shifted, matrix, finish, levels,
-        done=done,
-    )
+    sweep(padded, vel_ref, k_ref, land_ref, ip_ref, None, finish, levels)
     for copy in outs:
         copy.wait()
 
 
-def sweep_scratch(count, height, width):
-    return [
-        pltpu.VMEM((count, height // CHUNKS, 2 * width), F32),
-        pltpu.VMEM((2 * width, 2 * width), BF16),
-        pltpu.VMEM((width, height), F32),
-        pltpu.VMEM((height, width), F32),
-    ]
-
-
-def first_part(sizes, padded, received, velocity, mixing, land, levels):
+def first_part(padded, velocity, mixing, land, levels):
     count, height, width = padded.shape
     height -= 2 * PAD
+    edge = (4, 3, levels, width)
     return pl.pallas_call(
-        functools.partial(first_kernel, sizes=sizes, levels=levels),
+        functools.partial(first_kernel, levels=levels),
         out_shape=(
-            jax.ShapeDtypeStruct(padded.shape, F32),
-            pltpu.HBM((count, height, width), F32),
+            jax.ShapeDtypeStruct((count, height, width), F32),
+            jax.ShapeDtypeStruct(edge, F32),
             pltpu.HBM((levels, height, width), F32),
+            pltpu.HBM(edge, F32),
         ),
-        in_specs=[vmem()] * 8,
-        out_specs=(vmem(), hbm(), hbm()),
+        in_specs=[vmem()] * 4,
+        out_specs=(vmem(), vmem(), hbm(), hbm()),
+        scratch_shapes=[
+            pltpu.VMEM((levels, height, width), F32),
+            pltpu.VMEM((height, width), F32),
+            pltpu.VMEM((width, height), F32),
+            pltpu.SemaphoreType.DMA((2,)),
+        ],
+        compiler_params=params(6),
+        name="first_part",
+    )(padded, velocity, mixing, land)
+
+
+def fix_kernel(
+    q_in, edge_ref, r0, r1, r2, r3, q_ref, q_hbm, halos, added, lines, sides, sems, *, sizes, levels
+):
+    del q_in
+    count, height, width = q_ref.shape
+    tracers = count // levels
+    rows = height // CHUNKS
+    lane = lane_iota((8, width))
+    sort_halos(sizes, (r0, r1, r2, r3), halos)
+
+    def level_done(side, level, q, rhs):
+        value = rhs if level == 0 else q
+        added[side, pl.ds(level, tracers, stride=levels), :] = value
+
+    correct(edge_ref, halos, level_done, levels)
+    lines[...] = jnp.zeros(lines.shape, F32)
+    lines[pl.ds(1, count, stride=2), :] = added[0]
+    lines[pl.ds(2, count, stride=2), :] = added[1]
+    sides[...] = lines[...].T
+    q_ref[:, height - 1, :] = q_ref[:, height - 1, :] + added[2]
+    q_ref[:, 0, :] = q_ref[:, 0, :] + added[3]
+    outs = []
+    for chunk in range(CHUNKS):
+
+        def block(i, carry):
+            here = pl.ds(pl.multiple_of(chunk * rows + i * 8, 8), 8)
+            side = sides[here, :]
+            for tl in range(count):
+                q_ref[tl, here, :] = q_ref[tl, here, :] + scatter_columns(lane, side, tl)
+            return carry
+
+        lax.fori_loop(0, rows // 8, block, 0, unroll=2)
+        here = pl.ds(chunk * rows, rows)
+        outs.extend(copies_of([(q_ref.at[:, here, :], q_hbm.at[:, here, :])], sems, chunk))
+    for copy in outs:
+        copy.wait()
+
+
+def fix_part(sizes, q, edge, received, levels):
+    count, height, width = q.shape
+    return pl.pallas_call(
+        functools.partial(fix_kernel, sizes=sizes, levels=levels),
+        out_shape=(jax.ShapeDtypeStruct(q.shape, F32), pltpu.HBM(q.shape, F32)),
+        in_specs=[vmem()] * 6,
+        out_specs=(vmem(), hbm()),
         input_output_aliases={0: 0},
-        scratch_shapes=sweep_scratch(count, height, width)
-        + [
-            pltpu.VMEM((count, height, width), F32),
-            pltpu.VMEM((levels, height, width), F32),
-            pltpu.SemaphoreType.DMA((CHUNKS + 1,)),
+        scratch_shapes=[
+            pltpu.VMEM((4, count, width), F32),
+            pltpu.VMEM((4, count, width), F32),
+            pltpu.VMEM((width, height), F32),
+            pltpu.VMEM((height, width), F32),
+            pltpu.SemaphoreType.DMA((CHUNKS,)),
         ],
-        compiler_params=params(12),
-        name="first_part",
-    )(padded, *received, velocity, mixing, land)
+        compiler_params=params(4),
+        name="fix_part",
+    )(q, edge, *received)
 
 
 def middle_kernel(
-    incoming_hbm, q_hbm, ip_hbm, k_hbm, land_hbm, vel_hbm,
-    x_ref, coef_ref, pick_ref, ip_ref, k_ref, land_ref, vel_ref, s0, s1, s2, s3,
-    incoming_ref, q_ref, wide, flux, cols, lines, sems, *, sizes, levels, cap, window,
+    incoming_ref, q_hbm, ip_hbm, k_hbm, land_hbm, vel_hbm, edge_hbm,
+    x_ref, coef_ref, pick_ref, ip_ref, k_ref, land_ref, vel_ref, edge_ref, top_edge_ref,
+    s0, s1, s2, s3, coef_hbm,
+    q_ref, wide, flux, cols, lines, sems, *, sizes, levels, cap, window,
 ):
     count, height, width = q_ref.shape
     tracers = count // levels
@@ -469,14 +539,11 @@
     fields = flux.shape[0]
     rows = height // CHUNKS
     early = copies_of(
-        [
-            (incoming_hbm, incoming_ref), (ip_hbm, ip_ref), (land_hbm, land_ref), (k_hbm, k_ref),
-            (vel_hbm, vel_ref),
-        ],
-        sems,
-    )
-    arrivals = chunk_copies(q_hbm, 0, q_ref, 0, height, sems, len(early))
-    early[0].wait()
+        [(ip_hbm, ip_ref), (land_hbm, land_ref), (k_hbm, k_ref)], sems
+    )
+    arrivals = chunk_copies(q_hbm, 0, q_ref, 0, height, sems, 5)
+    late = copies_of([(vel_hbm, vel_ref), (edge_hbm, edge_ref)], sems, 3)
+    clear_pads(x_ref)
     span = nodes * message_rows
     wide[span:, :] = jnp.zeros((wide.shape[0] - span, width), F32)
     for n in range(nodes):
@@ -502,7 +569,7 @@
             pieces.append(jnp.zeros((window, width), F32))
         stacked = jnp.concatenate(pieces, axis=0).astype(BF16)
         flux[f] = jnp.dot(selector, stacked, preferred_element_type=F32)
-    for copy in early[1:4]:
+    for copy in early:
         copy.wait()
     sea = land_ref[...].astype(F32)
     stirring = 1.0 + 0.5 * (
@@ -516,6 +583,7 @@
     coef_ref[tracers + 2] = inverse0
     for t in range(tracers):
         coef_ref[t] = FORCING * sea * flux[t]
+    kept = copies_of([(coef_ref, coef_hbm)], sems, 5 + CHUNKS)
     lane = lane_iota((8, width))
     for chunk in range(CHUNKS):
         arrivals[chunk].wait()
@@ -543,51 +611,58 @@
                     elif level > 1:
                         x = q_ref[tl, here, :] + down[level] * x
                     x_ref[tl, pl.ds(PAD + r, 8), :] = x
-                    moved = pltpu.roll(x, (2 * tl + 2) % width, 1)
-                    acc = jnp.where((lane == 2 * tl + 1) | (lane == 2 * tl + 2), moved, acc)
+                    acc = gather_columns(acc, lane, x, tl)
+            for n, value in enumerate((link0, inv1, inv0)):
+                acc = gather_columns(acc, lane, value, count + n)
             cols[here, :] = acc
             return carry
 
-        lax.fori_loop(0, rows // 8, block, 0)
+        lax.fori_loop(0, rows // 8, block, 0, unroll=2)
     lines[...] = cols[...].T
     store_sends(
         sizes, lines, x_ref[:, PAD, :], x_ref[:, PAD + height - 1, :], (s0, s1, s2, s3)
     )
-    early[4].wait()
-
-
-def middle_part(sizes, incoming, q, ip, mixing, land, velocity, fields, levels, cap, window):
+    for n in range(3):
+        for side in range(2):
+            at = 2 * (count + n) + 1 + side
+            top_edge_ref[side, n : n + 1, :] = lines[at : at + 1, :]
+        for side, row in ((2, height - 1), (3, 0)):
+            top_edge_ref[side, n : n + 1, :] = coef_ref[tracers + n, row : row + 1, :]
+    for copy in late + kept:
+        copy.wait()
+
+
+def middle_part(sizes, incoming, q, ip, mixing, land, velocity, edge, fields, levels, cap, window):
     count, height, width = q.shape
     nodes, message_rows, _ = incoming.shape
     tracers = count // levels
     groups = -(-nodes // (128 // window))
     line = jax.ShapeDtypeStruct((count, width), F32)
+    near = [jax.ShapeDtypeStruct(x.shape, x.dtype) for x in (ip, mixing, land, velocity, edge)]
     return pl.pallas_call(
         functools.partial(middle_kernel, sizes=sizes, levels=levels, cap=cap, window=window),
         out_shape=(
             jax.ShapeDtypeStruct((count, height + 2 * PAD, width), F32),
             jax.ShapeDtypeStruct((tracers + 3, height, width), F32),
             jax.ShapeDtypeStruct((groups * 128, height), BF16),
-            jax.ShapeDtypeStruct(ip.shape, F32),
-            jax.ShapeDtypeStruct(mixing.shape, F32),
-            jax.ShapeDtypeStruct(land.shape, land.dtype),
-            jax.ShapeDtypeStruct(velocity.shape, F32),
+            *near,
+            jax.ShapeDtypeStruct((4, 8, width), F32),
             line, line, line, line,
+            pltpu.HBM((tracers + 3, height, width), F32),
         ),
-        in_specs=[hbm()] * 6,
-        out_specs=(vmem(),) * 11,
+        in_specs=[vmem()] + [hbm()] * 6,
+        out_specs=(vmem(),) * 13 + (hbm(),),
         scratch_shapes=[
-            pltpu.VMEM(incoming.shape, BF16),
             pltpu.VMEM(q.shape, F32),
             pltpu.VMEM((nodes * message_rows + window * fields, width), F32),
             pltpu.VMEM((fields, height, width), F32),
             pltpu.VMEM((height, width), F32),
             pltpu.VMEM((width, height), F32),
-            pltpu.SemaphoreType.DMA((5 + CHUNKS,)),
+            pltpu.SemaphoreType.DMA((6 + CHUNKS,)),
         ],
         compiler_params=params(10),
         name="middle_part",
-    )(*pin(incoming, q, ip, mixing, land, velocity))
+    )(incoming, *pin(q, ip, mixing, land, velocity, edge))
 
 
 def top_level(coef_ref, here, t, tracers, q1, rhs):
@@ -598,35 +673,76 @@
     return q1, top
 
 
-def reply_kernel(
-    padded_in, r0, r1, r2, r3, vel_ref, k_ref, land_ref, ip_ref, coef_ref, pick_ref,
-    padded, state_hbm, sides_hbm, coef_hbm, out_hbm,
-    shifted, matrix, lines, sides, top, rows_out, packed, sems,
-    *, sizes, levels, cap, window,
+def inner_kernel(
+    padded, vel_ref, k_ref, land_ref, ip_ref, coef_ref, top_ref, state_hbm, sems, *, levels
 ):
-    tracers = top.shape[0]
-    height = top.shape[1]
-    del padded_in
-    place_sides(sizes, (r0, r1), lines, sides)
-    place_rows(sizes, (r2, r3), padded)
-    kept = copies_of(
-        [(padded, state_hbm), (sides, sides_hbm), (coef_ref, coef_hbm)], sems, 2
-    )
+    tracers = top_ref.shape[0]
+    kept = copies_of([(padded, state_hbm)], sems)
 
     def finish(level, r, q, tops):
         if level == 0:
             here = pl.ds(r, 8)
-            sea = land_ref[here, :].astype(F32)
             for t in range(tracers):
                 _, x = top_level(coef_ref, here, t, tracers, q[t], tops[t])
-                top[t, here, :] = x * sea
-
-    sweep(padded, vel_ref, k_ref, land_ref, ip_ref, sides, shifted, matrix, finish, levels)
+                top_ref[t, here, :] = x
+
+    sweep(padded, vel_ref, k_ref, land_ref, ip_ref, None, finish, levels)
+    kept[0].wait()
+
+
+def inner_part(padded, velocity, mixing, land, ip, coef, levels):
+    count, height, width = padded.shape
+    height -= 2 * PAD
+    return pl.pallas_call(
+        functools.partial(inner_kernel, levels=levels),
+        out_shape=(
+            jax.ShapeDtypeStruct((count // levels, height, width), F32),
+            pltpu.HBM(padded.shape, F32),
+        ),
+        in_specs=[vmem()] * 6,
+        out_specs=(vmem(), hbm()),
+        scratch_shapes=[pltpu.SemaphoreType.DMA((1,))],
+        compiler_params=params(4),
+        name="inner_part",
+    )(padded, velocity, mixing, land, ip, coef)
+
+
+def reply_kernel(
+    top_in, r0, r1, r2, r3, edge_ref, top_edge_ref, land_ref, pick_ref,
+    top, halo_hbm, out_hbm, halos, added, lines, sides, rows_out, packed, sems,
+    *, sizes, levels, cap, window,
+):
+    del top_in
+    tracers, height, width = top.shape
+    sort_halos(sizes, (r0, r1, r2, r3), halos)
+    kept = copies_of([(halos, halo_hbm)], sems, 2)
+    below = [None] * 4
+
+    def level_done(side, level, q, rhs):
+        if level == 1:
+            below[side] = q
+        if level == 0:
+            link0 = top_edge_ref[side, 0:1, :]
+            inv1 = top_edge_ref[side, 1:2, :]
+            inv0 = top_edge_ref[side, 2:3, :]
+            added[side, :tracers, :] = (rhs + link0 * (below[side] * inv1)) * inv0
+
+    correct(edge_ref, halos, level_done, levels)
+    lines[...] = jnp.zeros(lines.shape, F32)
+    lines[pl.ds(1, tracers, stride=2), :] = added[0, :tracers, :]
+    lines[pl.ds(2, tracers, stride=2), :] = added[1, :tracers, :]
+    sides[...] = lines[...].T
+    top[:, height - 1, :] = top[:, height - 1, :] + added[2, :tracers, :]
+    top[:, 0, :] = top[:, 0, :] + added[3, :tracers, :]
+    lane = lane_iota((height, width))
+    side = sides[...]
+    sea = land_ref[...].astype(F32)
     nodes = out_hbm.shape[0]
     per = cap * tracers
     picked = pick_ref[...]
     for t in range(tracers):
-        rows = jnp.dot(picked, top[t].astype(BF16), preferred_element_type=F32)
+        surface = (top[t] + scatter_columns(lane, side, t)) * sea
+        rows = jnp.dot(picked, surface.astype(BF16), preferred_element_type=F32)
         for n in range(nodes):
             rows_out[pl.ds(n * per + t, cap, stride=tracers), :] = rows[
                 n * window : n * window + cap, :
@@ -638,66 +754,67 @@
         for n in range(part * share, (part + 1) * share):
             packed[n] = rows_out[n * per : (n + 1) * per, :].astype(BF16)
         here = pl.ds(part * share, share)
-        copy = pltpu.make_async_copy(packed.at[here], out_hbm.at[here], sems.at[part])
-        copy.start()
-        copies.append(copy)
+        copies.extend(copies_of([(packed.at[here], out_hbm.at[here])], sems, part))
     for copy in copies + kept:
         copy.wait()
 
 
-def replies(sizes, padded, received, velocity, mixing, land, ip, coef, pick, nodes, levels, cap, window):
-    count, height, width = padded.shape
-    height -= 2 * PAD
-    tracers = count // levels
-    scratch = sweep_scratch(count, height, width)
+def replies(sizes, top, received, edge, top_edge, land, pick, nodes, levels, cap, window):
+    tracers, height, width = top.shape
+    count = tracers * levels
     return pl.pallas_call(
         functools.partial(reply_kernel, sizes=sizes, levels=levels, cap=cap, window=window),
         out_shape=(
-            jax.ShapeDtypeStruct(padded.shape, F32),
-            pltpu.HBM(padded.shape, F32),
-            pltpu.HBM((height, width), F32),
-            pltpu.HBM(coef.shape, F32),
+            jax.ShapeDtypeStruct(top.shape, F32),
+            pltpu.HBM((4, count, width), F32),
             pltpu.HBM((nodes, cap * tracers, width), BF16),
         ),
-        in_specs=[vmem()] * 11,
-        out_specs=(vmem(),) + (hbm(),) * 4,
+        in_specs=[vmem()] * 9,
+        out_specs=(vmem(), hbm(), hbm()),
         input_output_aliases={0: 0},
-        scratch_shapes=scratch
-        + [
-            pltpu.VMEM((tracers, height, width), F32),
+        scratch_shapes=[
+            pltpu.VMEM((4, count, width), F32),
+            pltpu.VMEM((4, 8, width), F32),
+            pltpu.VMEM((width, height), F32),
+            pltpu.VMEM((height, width), F32),
             pltpu.VMEM((nodes * cap * tracers, width), F32),
             pltpu.VMEM((nodes, cap * tracers, width), BF16),
-            pltpu.SemaphoreType.DMA((5,)),
+            pltpu.SemaphoreType.DMA((3,)),
         ],
-        compiler_params=params(12),
+        compiler_params=params(6),
         name="replies",
-    )(padded, *received, velocity, mixing, land, ip, coef, pick)
+    )(top, *received, edge, top_edge, land, pick)
 
 
 def last_kernel(
-    padded_hbm, sides_hbm, vel_hbm, k_hbm, land_hbm, ip_hbm, coef_hbm,
-    out_hbm, shifted, matrix, padded, sides, vel_ref, k_ref, land_ref, ip_ref, coef_ref, out_ref,
+    padded_hbm, halo_hbm, vel_hbm, k_hbm, land_hbm, ip_hbm, coef_hbm,
+    out_hbm, padded, halos, lines, sides, vel_ref, k_ref, land_ref, ip_ref, coef_ref, out_ref,
     sems, *, levels,
 ):
-    height = out_ref.shape[1]
+    count, height, width = out_ref.shape
+    tracers = count // levels
     rows = height // CHUNKS
     early = copies_of(
         [
-            (sides_hbm, sides), (vel_hbm, vel_ref), (k_hbm, k_ref), (land_hbm, land_ref),
+            (halo_hbm, halos), (vel_hbm, vel_ref), (k_hbm, k_ref), (land_hbm, land_ref),
             (ip_hbm, ip_ref), (coef_hbm, coef_ref), (padded_hbm, padded),
         ],
         sems,
     )
-    for copy in early:
+    early[0].wait()
+    lines[...] = jnp.zeros(lines.shape, F32)
+    lines[pl.ds(1, count, stride=2), :] = halos[0]
+    lines[pl.ds(2, count, stride=2), :] = halos[1]
+    sides[...] = lines[...].T
+    for copy in early[1:]:
         copy.wait()
+    padded[:, PAD + height, :] = halos[2]
+    padded[:, PAD - 1, :] = halos[3]
     outs = []
 
     def done(chunk):
         here = pl.ds(chunk * rows, rows)
         outs.extend(copies_of([(out_ref.at[:, here, :], out_hbm.at[:, here, :])], sems, chunk))
-
-    count = out_ref.shape[0]
-    tracers = count // levels
 
     def finish(level, r, q, tops):
         here = pl.ds(r, 8)
@@ -718,15 +835,12 @@
                     x = out_ref[t * levels + lower, here, :] + down[lower] * x
                     out_ref[t * levels + lower, here, :] = x
 
-    sweep(
-        padded, vel_ref, k_ref, land_ref, ip_ref, sides, shifted, matrix, finish, levels,
-        done=done,
-    )
+    sweep(padded, vel_ref, k_ref, land_ref, ip_ref, sides, finish, levels, done)
     for copy in outs:
         copy.wait()
 
 
-def last_part(padded, sides, velocity, mixing, land, ip, coef, levels):
+def last_part(padded, halos, velocity, mixing, land, ip, coef, levels):
     count, height, width = padded.shape
     height -= 2 * PAD
     return pl.pallas_call(
@@ -734,10 +848,11 @@
         out_shape=pltpu.HBM((count, height, width), F32),
         in_specs=[hbm()] * 7,
         out_specs=hbm(),
-        scratch_shapes=sweep_scratch(count, height, width)[:2]
-        + [
+        scratch_shapes=[
             pltpu.VMEM(padded.shape, F32),
-            pltpu.VMEM(sides.shape, F32),
+            pltpu.VMEM(halos.shape, F32),
+            pltpu.VMEM((width, height), F32),
+            pltpu.VMEM((height, width), F32),
             pltpu.VMEM(velocity.shape, F32),
             pltpu.VMEM(mixing.shape, F32),
             pltpu.VMEM(land.shape, land.dtype),
@@ -746,25 +861,22 @@
             pltpu.VMEM((count, height, width), F32),
             pltpu.SemaphoreType.DMA((7,)),
         ],
-        compiler_params=params(20),
+        compiler_params=params(16),
         name="last_part",
-    )(*pin(padded, sides, velocity, mixing, land, ip, coef))
+    )(*pin(padded, halos, velocity, mixing, land, ip, coef))
 
 
 def back_kernel(
-    slot_hbm, atm_hbm, rows_hbm, returned_hbm, weights_hbm, out_hbm,
-    slot_ref, atm_ref, rows_ref, returned_ref, weights_ref, out_ref, wide, total, sems,
+    slot_hbm, atm_hbm, rows_hbm, returned_ref, weights_hbm, out_hbm,
+    slot_ref, atm_ref, rows_ref, weights_ref, out_ref, wide, total, sems,
     *, tracers, cells, steps,
 ):
     nodes, per, width = returned_ref.shape
     pairs = weights_ref.shape[0]
+    blocks = out_ref.shape[1]
     per_step = pairs // steps
     copies = copies_of(
-        [
-            (returned_hbm, returned_ref), (slot_hbm, slot_ref), (atm_hbm, atm_ref),
-            (rows_hbm, rows_ref),
-        ],
-        sems,
+        [(slot_hbm, slot_ref), (atm_hbm, atm_ref), (rows_hbm, rows_ref)], sems
     )
     parts = copies_of(
         [
@@ -779,10 +891,9 @@
     )
     total[...] = jnp.zeros(total.shape, F32)
     wide[nodes * per :, :] = jnp.zeros((wide.shape[0] - nodes * per, width), F32)
-    copies[0].wait()
     for n in range(nodes):
         wide[n * per : (n + 1) * per, :] = returned_ref[n].astype(F32)
-    for copy in copies[1:]:
+    for copy in copies:
         copy.wait()
     for p in range(pairs):
         if p % per_step == 0:
@@ -791,15 +902,18 @@
         product = lax.dot_general(
             lhs, weights_ref[p], (((1,), (1,)), ((), ())), preferred_element_type=F32
         )
-        b = atm_ref[p]
-        total[b] = total[b] + product
-    lane = lane_iota((tracers, cells))
-
-    def write(b, carry):
-        out_ref[b] = jnp.where(lane < rows_ref[b], total[b][:tracers], 0.0)
+        here = pl.ds(pl.multiple_of(atm_ref[p] * 8, 8), 8)
+        total[here, :] = total[here, :] + product
+    lane = lane_iota((8, cells))
+
+    def mask(b, carry):
+        here = pl.ds(pl.multiple_of(b * 8, 8), 8)
+        total[here, :] = jnp.where(lane < rows_ref[b], total[here, :], 0.0)
         return carry
 
-    lax.fori_loop(0, out_ref.shape[0], write, 0, unroll=8)
+    lax.fori_loop(0, blocks, mask, 0, unroll=8)
+    for t in range(tracers):
+        out_ref[t] = total[pl.ds(t, blocks, stride=8), :]
     for copy in copies_of([(out_ref, out_hbm)], sems):
         copy.wait()
 
@@ -810,25 +924,25 @@
     blocks = rows.shape[0]
     ints = jnp.int32
     steps = 4
-    return pl.pallas_call(
+    by_tracer = pl.pallas_call(
         functools.partial(back_kernel, tracers=tracers, cells=cells, steps=steps),
-        out_shape=pltpu.HBM((blocks, tracers, cells), F32),
-        in_specs=[hbm()] * 5,
+        out_shape=pltpu.HBM((tracers, blocks, cells), F32),
+        in_specs=[hbm()] * 3 + [vmem(), hbm()],
         out_specs=hbm(),
         scratch_shapes=[
             pltpu.SMEM((pairs,), ints),
             pltpu.SMEM((pairs,), ints),
             pltpu.SMEM((blocks,), ints),
-            pltpu.VMEM(returned.shape, BF16),
             pltpu.VMEM(weights.shape, BF16),
-            pltpu.VMEM((blocks, tracers, cells), F32),
+            pltpu.VMEM((tracers, blocks, cells), F32),
             pltpu.VMEM((nodes * per + 8, width), F32),
-            pltpu.VMEM((blocks, 8, cells), F32),
-            pltpu.SemaphoreType.DMA((4 + steps,)),
+            pltpu.VMEM((blocks * 8, cells), F32),
+            pltpu.SemaphoreType.DMA((3 + steps,)),
         ],
         compiler_params=params(8),
         name="back",
-    )(*pin(slots, atm, rows, returned, weights))
+    )(*pin(slots, atm, rows), returned, *pin(weights))
+    return by_tracer.transpose(1, 0, 2)
 
 
 def all_to_all(x):
@@ -865,17 +979,21 @@
     incoming = all_to_all(message)
     padded, *lines = edges(mesh_sizes, slots, state)
     received = exchange(lines, mesh_sizes)
-    _, q, ip = first_part(mesh_sizes, padded, received, velocity, mixing, land, levels)
-    padded, coef, pick, ip_near, mixing_near, land_near, velocity_near, *lines = middle_part(
-        mesh_sizes, incoming, q, ip, mixing, land, velocity, fields, levels, cap, window
+    q, edge, ip, edge_far = first_part(padded, velocity, mixing, land, levels)
+    _, q = fix_part(mesh_sizes, q, edge, received, levels)
+    (
+        padded, coef, pick, ip_near, mixing_near, land_near, velocity_near, edge, top_edge,
+        *lines, coef_far,
+    ) = middle_part(
+        mesh_sizes, incoming, q, ip, mixing, land, velocity, edge_far, fields, levels, cap, window
     )
     received = exchange(lines, mesh_sizes)
-    _, state, sides, coef, answer = replies(
-        mesh_sizes, padded, received, velocity_near, mixing_near, land_near, ip_near, coef, pick,
-        nodes, levels, cap, window,
+    top, state = inner_part(padded, velocity_near, mixing_near, land_near, ip_near, coef, levels)
+    _, halos, answer = replies(
+        mesh_sizes, top, received, edge, top_edge, land_near, pick, nodes, levels, cap, window
     )
     returned = all_to_all(answer)
-    out = last_part(state, sides, velocity, mixing, land, ip, coef, levels)
+    out = last_part(state, halos, velocity, mixing, land, ip, coef_far, levels)
     atm_surface = back(slots, pair_atm, atm_rows, returned, regrid_weights, tracer_count)
     return (out.reshape(tracers.shape), atm_surface)
 

time: 66.9 us -> 55.7 us (0.83)
  Pallas kernels: 34.9 us -> 30.4 us
  local copies, waits for them, and re-layouts: 3.1 us -> 0.02 us
  waiting for transfers between devices: 6.59 us -> 4.11 us
  starting transfers between devices: 21.2 us -> 20 us
    ppermute x8, waiting for transfers between devices: 4.9 us -> 0.02 us  [exchange(): return [lax.ppermute(line, AXES, perm) for line, perm in zip(lines, perms)]]
    pallas_call x1, Pallas kernels: 5.56 us -> 1.26 us  [replies(): pl.pallas_call(functools.partial(reply_kernel, sizes=sizes, levels=levels...]
    unnamed x11 -> x6, local copies, waits for them, and re-layouts: 3.1 us -> 0.02 us
    pallas_call x1 -> x3, Pallas kernels: 5.34 us -> 8.07 us  [the longest x1 3.31 us: first_part(): pl.pallas_call(functools.partial(first_kernel, levels=levels), out_shape=...]
    all_to_all x2, waiting for transfers between devices: 1.69 us -> 4.09 us  [all_to_all(): return lax.all_to_all(x, AXES, split_axis=0, concat_axis=0, tiled=True)]
    pallas_call x1, Pallas kernels: 8.86 us -> 7.37 us  [last_part(): pl.pallas_call(functools.partial(last_kernel, levels=levels), out_shape=p...]
    ppermute x8, starting transfers between devices: 10.1 us -> 9 us  [exchange(): return [lax.ppermute(line, AXES, perm) for line, perm in zip(lines, perms)]]
    pallas_call x1, Pallas kernels: 4.19 us -> 3.36 us  [middle_part(): pl.pallas_call(functools.partial(middle_kernel, sizes=sizes, levels=level...]
  transfers between devices with their start and end apart: 10 -> 10, of which waited for: 5 -> 2; matrix products, arithmetic and copies ran while one was open for 0% -> 0% of each run, Pallas kernels for 26% -> 33%
where the time goes in v3:
time: 55.7 us; the launch traced here: 55.4 us
  Pallas kernels  30.4 us (55%)
  starting transfers between devices  20 us (36%)
  waiting for transfers between devices  4.11 us (7%)
  between operations  0.8 us (1%)
    all_to_all x2, starting transfers between devices, all_to_all(): return lax.all_to_all(x, AXES, split_axis=0, concat_axis=0, tiled=True)  11.1 us
    ppermute x8, starting transfers between devices, exchange(): return [lax.ppermute(line, AXES, perm) for line, perm in zip(lines, perms)]  9 us
    pallas_call x1, Pallas kernels, last_part(): pl.pallas_call(functools.partial(last_kernel, levels=levels), out_shape=p...  7.37 us
    all_to_all x2, waiting for transfers between devices, all_to_all(): return lax.all_to_all(x, AXES, split_axis=0, concat_axis=0, tiled=True)  4.09 us
    pallas_call x1, Pallas kernels, back(): pl.pallas_call(functools.partial(back_kernel, tracers=tracers, cells=cell...  4.04 us
    pallas_call x1, Pallas kernels, contributions(): pl.pallas_call(functools.partial(contrib_kernel, sizes=sizes, nodes=nodes...  3.63 us
    pallas_call x1, Pallas kernels, middle_part(): pl.pallas_call(functools.partial(middle_kernel, sizes=sizes, levels=level...  3.36 us
    pallas_call x1, Pallas kernels, first_part(): pl.pallas_call(functools.partial(first_kernel, levels=levels), out_shape=...  3.31 us
  transfers between devices with their start and end apart: 10, of which 2 were waited for; matrix products, arithmetic and copies ran while one was open for 0% of the time, Pallas kernels for 33%

profile of v3, /device:TPU:0, one launch (start us, length us, event | category | flops | bytes accessed | tf_op | source)
XLA Modules:
  0.0 55.4 jit_solution(5150344175580174066)
XLA Ops:
  0.6 0.0 copy-start
  0.6 0.0 copy-start.1
  0.7 0.0 copy-start.2
  0.7 3.6 %contributions.1 = (bf16[16,104,128]{2,1,0:T(8,128)(2,1)}, s32[96]{0:T(128)}) custom-call(s32[96]{0:T(128)} %bitcast.7, s32[96]{0:T(128)} %atm_hbm.3, s32[96]{0:T(128)} %row_hbm.1, s32[48]{0:T(128)} %rows_hbm.3, bf16[48,8,128]{2,1,0:T(8,128)(2,1)} %flux_hbm.1, bf16[96,128,128]{2,1,0:T(8,128)(2,1)} %weights_hbm.3), custom_call_target="tpu_custom_call" | custom-call | tf_op jit(solution)/shard_map/contributions/pallas_call | solution.py:170
  4.3 7.4 %all-to-all-start = ((bf16[16,104,128]{2,1,0:T(8,128)(2,1)}), bf16[16,104,128]{2,1,0:T(8,128)(2,1)S(1)}, u32[]{:S(2)}, u32[]{:S(2)}) async-start(bf16[16,104,128]{2,1,0:T(8,128)(2,1)} %get-tuple-element.32), calls=%async_computation | async-start | bytes 851968 | tf_op jit(solution)/shard_map/all_to_all | solution.py:949
  11.7 2.6 %edges.1 = (f32[48,144,128]{2,1,0:T(8,128)S(1)}, f32[48,128]{1,0:T(8,128)S(1)}, f32[48,128]{1,0:T(8,128)S(1)}, f32[48,128]{1,0:T(8,128)S(1)}, f32[48,128]{1,0:T(8,128)S(1)}) custom-call(s32[96]{0:T(128)} %get-tuple-element.33.order.slot_hbm, f32[48,128,128]{2,1,0:T(8,128)} %bitcast.4), custom_call_target="tpu_custom_call" | custom-call | tf_op jit(solution)/shard_map/edges/pallas_call | solution.py:294
  14.3 2.0 %collective-permute-start = (f32[48,128]{1,0:T(8,128)S(1)}, f32[48,128]{1,0:T(8,128)S(1)}, u32[]{:S(2)}, u32[]{:S(2)}) collective-permute-start(f32[48,128]{1,0:T(8,128)S(1)} %get-tuple-element.37), channel_id=1, source_target_pairs={{0,4},{1,5},{2,6},{3,7},{4,0},{5,1},{6,2},{7,3},{8,12},{9,13},{10,... | collective-permute-start | bytes 73736 | tf_op jit(solution)/shard_map/ppermute | solution.py:256
  16.3 0.0 collective-permute-start.1
  16.3 0.5 collective-permute-start.2
  16.8 1.1 %collective-permute-start.3 = (f32[48,128]{1,0:T(8,128)S(1)}, f32[48,128]{1,0:T(8,128)S(1)}, u32[]{:S(2)}, u32[]{:S(2)}) collective-permute-start(f32[48,128]{1,0:T(8,128)S(1)} %get-tuple-element.40), channel_id=1, source_target_pairs={{0,3},{1,2},{2,1},{3,0},{4,7},{5,6},{6,5},{7,4},{8,11},{9,10},{10,... | collective-permute-start | bytes 73736 | tf_op jit(solution)/shard_map/ppermute | solution.py:256
  17.9 3.3 %first_part.1 = (f32[48,128,128]{2,1,0:T(8,128)S(1)}, f32[4,3,8,128]{3,2,1,0:T(8,128)S(1)}, f32[8,128,128]{2,1,0:T(8,128)}, f32[4,3,8,128]{3,2,1,0:T(8,128)}) custom-call(f32[48,144,128]{2,1,0:T(8,128)S(1)} %get-tuple-element.34.padded, f32[2,8,128,128]{3,2,1,0:T(8,128)S(1)} %copy-done, f32[7,128,128]{2,1,0:T(8,128)S(1)} %copy-done.1, s32[128,128]{1,0:T(8,128)S(1)} %copy-done.2), custom_call_target="tpu_custom_call" | custom-call | tf_op jit(solution)/shard_map/first_part/pallas_call | solution.py:451
  21.2 0.0 collective-permute-done.r0
  21.3 2.5 %fix_part.1 = (f32[48,128,128]{2,1,0:T(8,128)S(1)}, f32[48,128,128]{2,1,0:T(8,128)}) custom-call(f32[48,128,128]{2,1,0:T(8,128)S(1)} %get-tuple-element.35.q_in, f32[4,3,8,128]{3,2,1,0:T(8,128)S(1)} %get-tuple-element.36.edge_ref, f32[48,128]{1,0:T(8,128)S(1)} %collective-permute-done.r0, ...), custom_call_target="tpu_custom_call", output_to_operand_aliasing={{0}: (0, {})} | custom-call | tf_op jit(solution)/shard_map/fix_part/pallas_call | solution.py:512
  23.8 0.9 %all-to-all-done.incoming_ref = bf16[16,104,128]{2,1,0:T(8,128)(2,1)S(1)} async-done(((bf16[16,104,128]{2,1,0:T(8,128)(2,1)}), bf16[16,104,128]{2,1,0:T(8,128)(2,1)S(1)}, u32[]{:S(2)}, u32[]{:S(2)}) %all-to-all-start) | async-done | bytes 426016 | tf_op jit(solution)/shard_map/all_to_all | solution.py:949
  24.7 3.4 %middle_part.1 = (f32[48,144,128]{2,1,0:T(8,128)S(1)}, f32[9,128,128]{2,1,0:T(8,128)S(1)}, bf16[256,128]{1,0:T(8,128)(2,1)S(1)}, f32[8,128,128]{2,1,0:T(8,128)S(...) custom-call(bf16[16,104,128]{2,1,0:T(8,128)(2,1)S(1)} %all-to-all-do, ...), custom_call_target="tpu_custom_call" | custom-call | tf_op jit(solution)/shard_map/middle_part/pallas_call | solution.py:642
  28.0 3.8 %collective-permute-start.4 = (f32[48,128]{1,0:T(8,128)S(1)}, f32[48,128]{1,0:T(8,128)S(1)}, u32[]{:S(2)}, u32[]{:S(2)}) collective-permute-start(f32[48,128]{1,0:T(8,128)S(1)} %get-tuple-element.52), channel_id=1, source_target_pairs={{0,4},{1,5},{2,6},{3,7},{4,0},{5,1},{6,2},{7,3},{8,12},{9,13},{10,... | collective-permute-start | bytes 73736 | tf_op jit(solution)/shard_map/ppermute | solution.py:256
  31.9 0.5 collective-permute-start.6
  32.4 1.1 %collective-permute-start.7 = (f32[48,128]{1,0:T(8,128)S(1)}, f32[48,128]{1,0:T(8,128)S(1)}, u32[]{:S(2)}, u32[]{:S(2)}) collective-permute-start(f32[48,128]{1,0:T(8,128)S(1)} %get-tuple-element.55), channel_id=1, source_target_pairs={{0,3},{1,2},{2,1},{3,0},{4,7},{5,6},{6,5},{7,4},{8,11},{9,10},{10,... | collective-permute-start | bytes 73736 | tf_op jit(solution)/shard_map/ppermute | solution.py:256
  33.5 2.3 %inner_part.1 = (f32[6,128,128]{2,1,0:T(8,128)S(1)}, f32[48,144,128]{2,1,0:T(8,128)}) custom-call(f32[48,144,128]{2,1,0:T(8,128)S(1)} %get-tuple-element.44.padded, f32[2,8,128,128]{3,2,1,0:T(8,128)S(1)} %get-tuple-element.45.vel_ref, f32[7,128,128]{2,1,0:T(8,128)S(1)} %get-tuple-element.46.k_ref, s32[128,128]{1,0:T(8,128)S(1)} %get-tuple-element.47.land_ref, ...), custom_call_target="tpu_custom_call" | custom-call | tf_op jit(solution)/shard_map/inner_part/pallas_call | solution.py:696
  35.8 1.3 %replies.1 = (f32[6,128,128]{2,1,0:T(8,128)S(1)}, f32[4,48,128]{2,1,0:T(8,128)}, bf16[16,72,128]{2,1,0:T(8,128)(2,1)}) custom-call(f32[6,128,128]{2,1,0:T(8,128)S(1)} %get-tuple-element.51.top_in, f32[48,128]{1,0:T(8,128)S(1)} %collective-permute-done.4.r0, f32[48,128]{1,0:T(8,128)S(1)} %collective-permute-done.5.r1, ...), custom_call_target="tpu_custom_call", output_to_operand_aliasing={{0}: (0, {})} | custom-call | tf_op jit(solution)/shard_map/replies/pallas_call | solution.py:765
  37.1 3.7 %all-to-all-start.1 = ((bf16[16,72,128]{2,1,0:T(8,128)(2,1)}), bf16[16,72,128]{2,1,0:T(8,128)(2,1)S(1)}, u32[]{:S(2)}, u32[]{:S(2)}) async-start(bf16[16,72,128]{2,1,0:T(8,128)(2,1)} %get-tuple-element.61), calls=%async_computation.1 | async-start | bytes 589824 | tf_op jit(solution)/shard_map/all_to_all | solution.py:949
  40.7 7.4 %last_part.1 = f32[48,128,128]{2,1,0:T(8,128)} custom-call(f32[48,144,128]{2,1,0:T(8,128)} %get-tuple-element.50.padded_hbm, f32[4,48,128]{2,1,0:T(8,128)} %get-tuple-element.59.halo_hbm, f32[2,8,128,128]{3,2,1,0:T(8,128)} %vel_hbm.3, f32[7,128,128]{2,1,0:T(8,128)} %k_hbm.3, s32[128,128]{1,0:T(8,128)} %land_hbm.3, f32[8,128,128]{2,1,0:T(8,128)} %get-tuple-element.42.ip_hbm, ...), custom_call_target="tpu_custom_call" | custom-call | tf_op jit(solution)/shard_map/last_part/pallas_call | solution.py:846
  48.1 3.2 %all-to-all-done.1.returned_ref = bf16[16,72,128]{2,1,0:T(8,128)(2,1)S(1)} async-done(((bf16[16,72,128]{2,1,0:T(8,128)(2,1)}), bf16[16,72,128]{2,1,0:T(8,128)(2,1)S(1)}, u32[]{:S(2)}, u32[]{:S(2)}) %all-to-all-start.1) | async-done | bytes 294944 | tf_op jit(solution)/shard_map/all_to_all | solution.py:949
  51.3 4.0 %back.1 = f32[6,48,128]{2,1,0:T(8,128)} custom-call(s32[96]{0:T(128)} %get-tuple-element.33.order.slot_hbm, s32[96]{0:T(128)} %atm_hbm.3, s32[48]{0:T(128)} %rows_hbm.3, bf16[16,72,128]{2,1,0:T(8,128)(2,1)S(1)} %all-to-all-done.1.returned_ref, bf16[96,128,128]{2,1,0:T(8,128)(2,1)} %weights_hbm.3), custom_call_target="tpu_custom_call" | custom-call | tf_op jit(solution)/shard_map/back/pallas_call | solution.py:927
  (11 shorter events, 0.0 us)
Async XLA Ops:
  0.6 17.3 %copy-start = (f32[2,8,128,128]{3,2,1,0:T(8,128)S(1)}, f32[2,8,128,128]{3,2,1,0:T(8,128)}, u32[]{:S(2)}) copy-start(f32[2,8,128,128]{3,2,1,0:T(8,128)} %vel_hbm.3) | copy-start | bytes 3145732
  0.6 17.3 %copy-start.1 = (f32[7,128,128]{2,1,0:T(8,128)S(1)}, f32[7,128,128]{2,1,0:T(8,128)}, u32[]{:S(2)}) copy-start(f32[7,128,128]{2,1,0:T(8,128)} %k_hbm.3) | copy-start | bytes 1376260
  0.7 17.3 %copy-start.2 = (s32[128,128]{1,0:T(8,128)S(1)}, s32[128,128]{1,0:T(8,128)}, u32[]{:S(2)}) copy-start(s32[128,128]{1,0:T(8,128)} %land_hbm.3) | copy-start | bytes 196612
  4.3 20.4 %all-to-all-start = ((bf16[16,104,128]{2,1,0:T(8,128)(2,1)}), bf16[16,104,128]{2,1,0:T(8,128)(2,1)S(1)}, u32[]{:S(2)}, u32[]{:S(2)}) async-start(bf16[16,104,128]{2,1,0:T(8,128)(2,1)} %get-tuple-element.32), calls=%async_computation | async-start | bytes 851968 | tf_op jit(solution)/shard_map/all_to_all | solution.py:949
  14.3 6.9 %collective-permute-start = (f32[48,128]{1,0:T(8,128)S(1)}, f32[48,128]{1,0:T(8,128)S(1)}, u32[]{:S(2)}, u32[]{:S(2)}) collective-permute-start(f32[48,128]{1,0:T(8,128)S(1)} %get-tuple-element.37), channel_id=1, source_target_pairs={{0,4},{1,5},{2,6},{3,7},{4,0},{5,1},{6,2},{7,3},{8,12},{9,13},{10,... | collective-permute-start | bytes 73736 | tf_op jit(solution)/shard_map/ppermute | solution.py:256
  16.3 4.9 %collective-permute-start.1 = (f32[48,128]{1,0:T(8,128)S(1)}, f32[48,128]{1,0:T(8,128)S(1)}, u32[]{:S(2)}, u32[]{:S(2)}) collective-permute-start(f32[48,128]{1,0:T(8,128)S(1)} %get-tuple-element.38), channel_id=1, source_target_pairs={{0,1},{1,0},{2,3},{3,2},{4,8},{5,9},{6,10},{7,11},{8,4},{9,5},{10,... | collective-permute-start | bytes 73736 | tf_op jit(solution)/shard_map/ppermute | solution.py:256
  16.3 4.9 %collective-permute-start.2 = (f32[48,128]{1,0:T(8,128)S(1)}, f32[48,128]{1,0:T(8,128)S(1)}, u32[]{:S(2)}, u32[]{:S(2)}) collective-permute-start(f32[48,128]{1,0:T(8,128)S(1)} %get-tuple-element.39), channel_id=1, source_target_pairs={{0,1},{1,0},{2,3},{3,2},{4,5},{5,4},{6,7},{7,6},{8,9},{9,8},{10,11... | collective-permute-start | bytes 73736 | tf_op jit(solution)/shard_map/ppermute | solution.py:256
  16.8 4.4 %collective-permute-start.3 = (f32[48,128]{1,0:T(8,128)S(1)}, f32[48,128]{1,0:T(8,128)S(1)}, u32[]{:S(2)}, u32[]{:S(2)}) collective-permute-start(f32[48,128]{1,0:T(8,128)S(1)} %get-tuple-element.40), channel_id=1, source_target_pairs={{0,3},{1,2},{2,1},{3,0},{4,7},{5,6},{6,5},{7,4},{8,11},{9,10},{10,... | collective-permute-start | bytes 73736 | tf_op jit(solution)/shard_map/ppermute | solution.py:256
  28.0 7.7 %collective-permute-start.4 = (f32[48,128]{1,0:T(8,128)S(1)}, f32[48,128]{1,0:T(8,128)S(1)}, u32[]{:S(2)}, u32[]{:S(2)}) collective-permute-start(f32[48,128]{1,0:T(8,128)S(1)} %get-tuple-element.52), channel_id=1, source_target_pairs={{0,4},{1,5},{2,6},{3,7},{4,0},{5,1},{6,2},{7,3},{8,12},{9,13},{10,... | collective-permute-start | bytes 73736 | tf_op jit(solution)/shard_map/ppermute | solution.py:256
  31.9 3.9 %collective-permute-start.5 = (f32[48,128]{1,0:T(8,128)S(1)}, f32[48,128]{1,0:T(8,128)S(1)}, u32[]{:S(2)}, u32[]{:S(2)}) collective-permute-start(f32[48,128]{1,0:T(8,128)S(1)} %get-tuple-element.53), channel_id=1, source_target_pairs={{0,1},{1,0},{2,3},{3,2},{4,8},{5,9},{6,10},{7,11},{8,4},{9,5},{10,... | collective-permute-start | bytes 73736 | tf_op jit(solution)/shard_map/ppermute | solution.py:256
  31.9 3.9 %collective-permute-start.6 = (f32[48,128]{1,0:T(8,128)S(1)}, f32[48,128]{1,0:T(8,128)S(1)}, u32[]{:S(2)}, u32[]{:S(2)}) collective-permute-start(f32[48,128]{1,0:T(8,128)S(1)} %get-tuple-element.54), channel_id=1, source_target_pairs={{0,1},{1,0},{2,3},{3,2},{4,5},{5,4},{6,7},{7,6},{8,9},{9,8},{10,11... | collective-permute-start | bytes 73736 | tf_op jit(solution)/shard_map/ppermute | solution.py:256
  32.4 3.4 %collective-permute-start.7 = (f32[48,128]{1,0:T(8,128)S(1)}, f32[48,128]{1,0:T(8,128)S(1)}, u32[]{:S(2)}, u32[]{:S(2)}) collective-permute-start(f32[48,128]{1,0:T(8,128)S(1)} %get-tuple-element.55), channel_id=1, source_target_pairs={{0,3},{1,2},{2,1},{3,0},{4,7},{5,6},{6,5},{7,4},{8,11},{9,10},{10,... | collective-permute-start | bytes 73736 | tf_op jit(solution)/shard_map/ppermute | solution.py:256
  37.1 14.3 %all-to-all-start.1 = ((bf16[16,72,128]{2,1,0:T(8,128)(2,1)}), bf16[16,72,128]{2,1,0:T(8,128)(2,1)S(1)}, u32[]{:S(2)}, u32[]{:S(2)}) async-start(bf16[16,72,128]{2,1,0:T(8,128)(2,1)} %get-tuple-element.61), calls=%async_computation.1 | async-start | bytes 589824 | tf_op jit(solution)/shard_map/all_to_all | solution.py:949

commit v4 on v3

--- a/solution.py
+++ b/solution.py
@@ -73,7 +73,7 @@
 def contrib_kernel(
     dest_hbm, atm_hbm, row_hbm, rows_hbm, flux_hbm, weights_hbm,
     out_hbm, slot_hbm,
-    dest_ref, atm_ref, row_ref, rows_ref, slot_ref, count, flux_ref, weights_ref,
+    dest_ref, atm_ref, row_ref, rows_ref, slot_ref, start_ref, count, flux_ref, weights_ref,
     masked, message, packed, sems, out_sems,
     *, sizes, nodes, cap, window, steps, message_rows,
 ):
@@ -81,6 +81,7 @@
     per_step = pairs // steps
     fields = flux_ref.shape[1]
     lanes = flux_ref.shape[2]
+    width = weights_ref.shape[2]
     small = [
         pltpu.make_async_copy(src, dst, sems.at[n])
         for n, (src, dst) in enumerate(
@@ -118,6 +119,7 @@
         s = count[d]
         count[d] = s + 1
         slot_ref[p] = d * cap + s
+        start_ref[p] = d * message_rows + s * fields
         start = pl.multiple_of(d * message_rows + cap * fields, 8)
         tile = message[pl.ds(start, 8), :]
         named = (row_ref[p] + 1).astype(F32)
@@ -139,14 +141,15 @@
     lax.fori_loop(0, flux_ref.shape[0], mask, 0, unroll=8)
     for n in range(steps):
         parts[n].wait()
-        for p in range(n * per_step, (n + 1) * per_step):
-            slot = slot_ref[p]
-            d = slot // cap
-            s = slot - d * cap
-            lhs = masked[atm_ref[p]].astype(BF16)
-            product = jnp.dot(lhs, weights_ref[p], preferred_element_type=F32)
-            start = pl.multiple_of(d * message_rows + s * fields, 8)
-            message[pl.ds(start, fields), :] = product
+        for p in range(n * per_step, (n + 1) * per_step, 2):
+            lhs = jnp.concatenate([masked[atm_ref[p]], masked[atm_ref[p + 1]]], axis=0)
+            rhs = jnp.concatenate([weights_ref[p], weights_ref[p + 1]], axis=1)
+            both = jnp.dot(lhs.astype(BF16), rhs, preferred_element_type=F32)
+            for k in range(2):
+                start = pl.multiple_of(start_ref[p + k], 8)
+                message[pl.ds(start, fields), :] = both[
+                    k * fields : (k + 1) * fields, k * width : (k + 1) * width
+                ]
     per_part = nodes // steps
     outs = []
     for n in range(steps):
@@ -184,6 +187,7 @@
             pltpu.SMEM((pairs,), ints),
             pltpu.SMEM(rows.shape, ints),
             pltpu.SMEM((pairs,), ints),
+            pltpu.SMEM((pairs,), ints),
             pltpu.SMEM((nodes,), ints),
             pltpu.VMEM(flux.shape, BF16),
             pltpu.VMEM(weights.shape, BF16),
@@ -206,7 +210,7 @@
 
 def scatter_columns(lane, lines, n):
     width = lines.shape[1]
-    moved = pltpu.roll(lines, (width - (2 * n + 2)) % width, 1)
+    moved = pltpu.roll(lines, (width - (2 * n + 2)) % width, 1).astype(F32)
     return jnp.where((lane == 0) | (lane == width - 1), moved, 0.0)
 
 
@@ -266,7 +270,7 @@
 def edges_kernel(order, c_hbm, padded, s0, s1, s2, s3, cols, lines, sems, *, sizes):
     del order
     count, height, width = c_hbm.shape
-    lane = lane_iota((8, width))
+    lane = lane_iota((16, width))
     rows = height // CHUNKS
     copies = chunk_copies(c_hbm, 0, padded, PAD, height, sems)
     clear_pads(padded)
@@ -274,14 +278,15 @@
         copies[chunk].wait()
 
         def body(i, carry):
-            r = pl.multiple_of(chunk * rows + i * 8, 8)
-            acc = jnp.zeros((8, width), F32)
+            r = pl.multiple_of(chunk * rows + i * 16, 16)
+            acc = jnp.zeros((16, width), BF16)
             for tl in range(count):
-                acc = gather_columns(acc, lane, padded[tl, pl.ds(PAD + r, 8), :], tl)
-            cols[pl.ds(r, 8), :] = acc
+                tile = padded[tl, pl.ds(PAD + r, 16), :].astype(BF16)
+                acc = gather_columns(acc, lane, tile, tl)
+            cols[pl.ds(r, 16), :] = acc.astype(F32)
             return carry
 
-        lax.fori_loop(0, rows // 8, body, 0, unroll=2)
+        lax.fori_loop(0, rows // 16, body, 0)
     lines[...] = cols[...].T
     store_sends(
         sizes, lines, padded[:, PAD, :], padded[:, PAD + height - 1, :], (s0, s1, s2, s3)
@@ -306,26 +311,29 @@
     )(*pin(order, state))
 
 
-def sweep(padded, vel_ref, k_ref, land_ref, ip_ref, sides, finish, levels, done=None):
+def sweep(padded, vel_ref, k_ref, land_ref, ip_ref, sides, finish, levels, wait=None, done=None):
     count, padded_height, width = padded.shape
     height = padded_height - 2 * PAD
     tracers = count // levels
-    rows = height // CHUNKS
-    lane = lane_iota((8, width))
-    for chunk in range(CHUNKS):
+    chunks = 1 if wait is None and done is None else CHUNKS
+    rows = height // chunks
+    lane = lane_iota((16, width))
+    for chunk in range(chunks):
+        if wait is not None:
+            wait(chunk)
         first = chunk * rows
 
         def block(i, carry):
-            r = pl.multiple_of(first + i * 8, 8)
-            sea = land_ref[pl.ds(r, 8), :].astype(F32)
+            r = pl.multiple_of(first + i * 16, 16)
+            sea = land_ref[pl.ds(r, 16), :].astype(F32)
             if sides is not None:
-                side = sides[pl.ds(r, 8), :]
+                side = sides[pl.ds(r, 16), :].astype(BF16)
             diffuse = DIFFUSION * sea
             c_here = 1.0 - 4.0 * diffuse
             q = [None] * tracers
             for level in range(levels - 1, -1, -1):
-                half_u = 0.5 * sea * vel_ref[0, level, pl.ds(r, 8), :]
-                half_v = 0.5 * sea * vel_ref[1, level, pl.ds(r, 8), :]
+                half_u = 0.5 * sea * vel_ref[0, level, pl.ds(r, 16), :]
+                half_v = 0.5 * sea * vel_ref[1, level, pl.ds(r, 16), :]
                 c_north = diffuse - half_v
                 c_south = diffuse + half_v
                 c_east = diffuse - half_u
@@ -334,15 +342,15 @@
                 c_east = jnp.where(lane == width - 1, 0.0, c_east)
                 c_west = jnp.where(lane == 0, 0.0, c_west)
                 if level >= 1 and level < levels - 1:
-                    link = k_ref[level, pl.ds(r, 8), :] * sea
+                    link = k_ref[level, pl.ds(r, 16), :] * sea
                 if level >= 2:
-                    inverse = ip_ref[level, pl.ds(r, 8), :]
+                    inverse = ip_ref[level, pl.ds(r, 16), :]
                 tops = []
                 for t in range(tracers):
                     tl = t * levels + level
-                    c = padded[tl, pl.ds(PAD + r, 8), :]
-                    north = padded[tl, pl.ds(PAD + r + 1, 8), :]
-                    south = padded[tl, pl.ds(PAD + r - 1, 8), :]
+                    c = padded[tl, pl.ds(PAD + r, 16), :]
+                    north = padded[tl, pl.ds(PAD + r + 1, 16), :]
+                    south = padded[tl, pl.ds(PAD + r - 1, 16), :]
                     east = pltpu.roll(c, width - 1, 1)
                     west = pltpu.roll(c, 1, 1)
                     rhs = c_here * c + (c_east * east + c_west * west)
@@ -359,7 +367,7 @@
                 finish(level, r, q, tops)
             return carry
 
-        lax.fori_loop(0, rows // 8, block, 0, unroll=2)
+        lax.fori_loop(0, rows // 16, block, 0, unroll=2)
         if done is not None:
             done(chunk)
 
@@ -383,8 +391,8 @@
 
 
 def first_kernel(
-    padded, vel_ref, k_ref, land_ref, q_ref, edge_ref, ip_hbm, edge_hbm,
-    ip_ref, cols, lines, sems, *, levels,
+    padded, vel_ref, k_ref, land_ref, edge_ref, q_hbm, ip_hbm, edge_hbm,
+    q_ref, ip_ref, cols, lines, sems, *, levels,
 ):
     height, width = land_ref.shape
     sea = land_ref[...].astype(F32)
@@ -437,9 +445,10 @@
     def finish(level, r, q, tops):
         values = q if level > 0 else tops
         for t, value in enumerate(values):
-            q_ref[t * levels + level, pl.ds(r, 8), :] = value
+            q_ref[t * levels + level, pl.ds(r, 16), :] = value
 
     sweep(padded, vel_ref, k_ref, land_ref, ip_ref, None, finish, levels)
+    outs.extend(copies_of([(q_ref, q_hbm)], sems, 2))
     for copy in outs:
         copy.wait()
 
@@ -451,32 +460,27 @@
     return pl.pallas_call(
         functools.partial(first_kernel, levels=levels),
         out_shape=(
-            jax.ShapeDtypeStruct((count, height, width), F32),
             jax.ShapeDtypeStruct(edge, F32),
+            pltpu.HBM((count, height, width), F32),
             pltpu.HBM((levels, height, width), F32),
             pltpu.HBM(edge, F32),
         ),
         in_specs=[vmem()] * 4,
-        out_specs=(vmem(), vmem(), hbm(), hbm()),
+        out_specs=(vmem(), hbm(), hbm(), hbm()),
         scratch_shapes=[
+            pltpu.VMEM((count, height, width), F32),
             pltpu.VMEM((levels, height, width), F32),
             pltpu.VMEM((height, width), F32),
             pltpu.VMEM((width, height), F32),
-            pltpu.SemaphoreType.DMA((2,)),
+            pltpu.SemaphoreType.DMA((3,)),
         ],
-        compiler_params=params(6),
+        compiler_params=params(8),
         name="first_part",
     )(padded, velocity, mixing, land)
 
 
-def fix_kernel(
-    q_in, edge_ref, r0, r1, r2, r3, q_ref, q_hbm, halos, added, lines, sides, sems, *, sizes, levels
-):
-    del q_in
-    count, height, width = q_ref.shape
-    tracers = count // levels
-    rows = height // CHUNKS
-    lane = lane_iota((8, width))
+def halo_kernel(edge_ref, r0, r1, r2, r3, added_hbm, halos, added, sems, *, sizes, levels):
+    tracers = halos.shape[1] // levels
     sort_halos(sizes, (r0, r1, r2, r3), halos)
 
     def level_done(side, level, q, rhs):
@@ -484,54 +488,40 @@
         added[side, pl.ds(level, tracers, stride=levels), :] = value
 
     correct(edge_ref, halos, level_done, levels)
+    for copy in copies_of([(added, added_hbm)], sems):
+        copy.wait()
+
+
+def halo_part(sizes, edge, received, levels):
+    shape = (4,) + received[0].shape
+    return pl.pallas_call(
+        functools.partial(halo_kernel, sizes=sizes, levels=levels),
+        out_shape=pltpu.HBM(shape, F32),
+        in_specs=[vmem()] * 5,
+        out_specs=hbm(),
+        scratch_shapes=[
+            pltpu.VMEM(shape, F32),
+            pltpu.VMEM(shape, F32),
+            pltpu.SemaphoreType.DMA((1,)),
+        ],
+        compiler_params=params(4),
+        name="halo_part",
+    )(edge, *received)
+
+
+def place_sides(added, lines, sides):
+    count = added.shape[1]
     lines[...] = jnp.zeros(lines.shape, F32)
     lines[pl.ds(1, count, stride=2), :] = added[0]
     lines[pl.ds(2, count, stride=2), :] = added[1]
     sides[...] = lines[...].T
-    q_ref[:, height - 1, :] = q_ref[:, height - 1, :] + added[2]
-    q_ref[:, 0, :] = q_ref[:, 0, :] + added[3]
-    outs = []
-    for chunk in range(CHUNKS):
-
-        def block(i, carry):
-            here = pl.ds(pl.multiple_of(chunk * rows + i * 8, 8), 8)
-            side = sides[here, :]
-            for tl in range(count):
-                q_ref[tl, here, :] = q_ref[tl, here, :] + scatter_columns(lane, side, tl)
-            return carry
-
-        lax.fori_loop(0, rows // 8, block, 0, unroll=2)
-        here = pl.ds(chunk * rows, rows)
-        outs.extend(copies_of([(q_ref.at[:, here, :], q_hbm.at[:, here, :])], sems, chunk))
-    for copy in outs:
-        copy.wait()
-
-
-def fix_part(sizes, q, edge, received, levels):
-    count, height, width = q.shape
-    return pl.pallas_call(
-        functools.partial(fix_kernel, sizes=sizes, levels=levels),
-        out_shape=(jax.ShapeDtypeStruct(q.shape, F32), pltpu.HBM(q.shape, F32)),
-        in_specs=[vmem()] * 6,
-        out_specs=(vmem(), hbm()),
-        input_output_aliases={0: 0},
-        scratch_shapes=[
-            pltpu.VMEM((4, count, width), F32),
-            pltpu.VMEM((4, count, width), F32),
-            pltpu.VMEM((width, height), F32),
-            pltpu.VMEM((height, width), F32),
-            pltpu.SemaphoreType.DMA((CHUNKS,)),
-        ],
-        compiler_params=params(4),
-        name="fix_part",
-    )(q, edge, *received)
 
 
 def middle_kernel(
-    incoming_ref, q_hbm, ip_hbm, k_hbm, land_hbm, vel_hbm, edge_hbm,
+    incoming_ref, q_hbm, ip_hbm, k_hbm, land_hbm, vel_hbm, edge_hbm, added_hbm,
     x_ref, coef_ref, pick_ref, ip_ref, k_ref, land_ref, vel_ref, edge_ref, top_edge_ref,
     s0, s1, s2, s3, coef_hbm,
-    q_ref, wide, flux, cols, lines, sems, *, sizes, levels, cap, window,
+    q_ref, wide, flux, cols, lines, added, sides, sems, *, sizes, levels, cap, window,
 ):
     count, height, width = q_ref.shape
     tracers = count // levels
@@ -539,10 +529,10 @@
     fields = flux.shape[0]
     rows = height // CHUNKS
     early = copies_of(
-        [(ip_hbm, ip_ref), (land_hbm, land_ref), (k_hbm, k_ref)], sems
-    )
-    arrivals = chunk_copies(q_hbm, 0, q_ref, 0, height, sems, 5)
-    late = copies_of([(vel_hbm, vel_ref), (edge_hbm, edge_ref)], sems, 3)
+        [(added_hbm, added), (ip_hbm, ip_ref), (land_hbm, land_ref), (k_hbm, k_ref)], sems
+    )
+    arrivals = chunk_copies(q_hbm, 0, q_ref, 0, height, sems, 6)
+    late = copies_of([(vel_hbm, vel_ref), (edge_hbm, edge_ref)], sems, 4)
     clear_pads(x_ref)
     span = nodes * message_rows
     wide[span:, :] = jnp.zeros((wide.shape[0] - span, width), F32)
@@ -571,6 +561,7 @@
         flux[f] = jnp.dot(selector, stacked, preferred_element_type=F32)
     for copy in early:
         copy.wait()
+    place_sides(added, lines, sides)
     sea = land_ref[...].astype(F32)
     stirring = 1.0 + 0.5 * (
         flux[fields - 2] * flux[fields - 2] + flux[fields - 1] * flux[fields - 1]
@@ -583,15 +574,20 @@
     coef_ref[tracers + 2] = inverse0
     for t in range(tracers):
         coef_ref[t] = FORCING * sea * flux[t]
-    kept = copies_of([(coef_ref, coef_hbm)], sems, 5 + CHUNKS)
-    lane = lane_iota((8, width))
+    kept = copies_of([(coef_ref, coef_hbm)], sems, 6 + CHUNKS)
+    lane = lane_iota((16, width))
     for chunk in range(CHUNKS):
         arrivals[chunk].wait()
         first = chunk * rows
+        if chunk == 0:
+            q_ref[:, 0, :] = q_ref[:, 0, :] + added[3]
+        if chunk == CHUNKS - 1:
+            q_ref[:, height - 1, :] = q_ref[:, height - 1, :] + added[2]
 
         def block(i, carry):
-            r = pl.multiple_of(first + i * 8, 8)
-            here = pl.ds(r, 8)
+            r = pl.multiple_of(first + i * 16, 16)
+            here = pl.ds(r, 16)
+            side = sides[here, :].astype(BF16)
             sea8 = land_ref[here, :].astype(F32)
             link0 = coef_ref[tracers, here, :]
             inv1 = coef_ref[tracers + 1, here, :]
@@ -599,25 +595,28 @@
             down = [None, link0 * inv1]
             for level in range(2, levels):
                 down.append(k_ref[level - 1, here, :] * sea8 * ip_ref[level, here, :])
-            acc = jnp.zeros((8, width), F32)
+            acc = jnp.zeros((16, width), BF16)
             for t in range(tracers):
                 base = t * levels
-                q1 = q_ref[base + 1, here, :] * inv1
-                x = (q_ref[base, here, :] + coef_ref[t, here, :] + link0 * q1) * inv0
+                q = [
+                    q_ref[tl, here, :] + scatter_columns(lane, side, tl)
+                    for tl in range(base, base + levels)
+                ]
+                q[1] = q[1] * inv1
+                x = (q[0] + coef_ref[t, here, :] + link0 * q[1]) * inv0
                 for level in range(levels):
                     tl = base + level
-                    if level == 1:
-                        x = q1 + down[1] * x
-                    elif level > 1:
-                        x = q_ref[tl, here, :] + down[level] * x
-                    x_ref[tl, pl.ds(PAD + r, 8), :] = x
-                    acc = gather_columns(acc, lane, x, tl)
+                    if level > 0:
+                        x = q[level] + down[level] * x
+                    x_ref[tl, pl.ds(PAD + r, 16), :] = x
+                    acc = gather_columns(acc, lane, x.astype(BF16), tl)
+            acc = acc.astype(F32)
             for n, value in enumerate((link0, inv1, inv0)):
                 acc = gather_columns(acc, lane, value, count + n)
             cols[here, :] = acc
             return carry
 
-        lax.fori_loop(0, rows // 8, block, 0, unroll=2)
+        lax.fori_loop(0, rows // 16, block, 0)
     lines[...] = cols[...].T
     store_sends(
         sizes, lines, x_ref[:, PAD, :], x_ref[:, PAD + height - 1, :], (s0, s1, s2, s3)
@@ -632,7 +631,7 @@
         copy.wait()
 
 
-def middle_part(sizes, incoming, q, ip, mixing, land, velocity, edge, fields, levels, cap, window):
+def middle_part(sizes, incoming, q, ip, mixing, land, velocity, edge, added, fields, levels, cap, window):
     count, height, width = q.shape
     nodes, message_rows, _ = incoming.shape
     tracers = count // levels
@@ -650,7 +649,7 @@
             line, line, line, line,
             pltpu.HBM((tracers + 3, height, width), F32),
         ),
-        in_specs=[vmem()] + [hbm()] * 6,
+        in_specs=[vmem()] + [hbm()] * 7,
         out_specs=(vmem(),) * 13 + (hbm(),),
         scratch_shapes=[
             pltpu.VMEM(q.shape, F32),
@@ -658,11 +657,13 @@
             pltpu.VMEM((fields, height, width), F32),
             pltpu.VMEM((height, width), F32),
             pltpu.VMEM((width, height), F32),
-            pltpu.SemaphoreType.DMA((6 + CHUNKS,)),
+            pltpu.VMEM(added.shape, F32),
+            pltpu.VMEM((height, width), F32),
+            pltpu.SemaphoreType.DMA((7 + CHUNKS,)),
         ],
         compiler_params=params(10),
         name="middle_part",
-    )(incoming, *pin(q, ip, mixing, land, velocity, edge))
+    )(incoming, *pin(q, ip, mixing, land, velocity, edge, added))
 
 
 def top_level(coef_ref, here, t, tracers, q1, rhs):
@@ -681,7 +682,7 @@
 
     def finish(level, r, q, tops):
         if level == 0:
-            here = pl.ds(r, 8)
+            here = pl.ds(r, 16)
             for t in range(tracers):
                 _, x = top_level(coef_ref, here, t, tracers, q[t], tops[t])
                 top_ref[t, here, :] = x
@@ -735,7 +736,7 @@
     top[:, height - 1, :] = top[:, height - 1, :] + added[2, :tracers, :]
     top[:, 0, :] = top[:, 0, :] + added[3, :tracers, :]
     lane = lane_iota((height, width))
-    side = sides[...]
+    side = sides[...].astype(BF16)
     sea = land_ref[...].astype(F32)
     nodes = out_hbm.shape[0]
     per = cap * tracers
@@ -797,27 +798,31 @@
     early = copies_of(
         [
             (halo_hbm, halos), (vel_hbm, vel_ref), (k_hbm, k_ref), (land_hbm, land_ref),
-            (ip_hbm, ip_ref), (coef_hbm, coef_ref), (padded_hbm, padded),
+            (ip_hbm, ip_ref), (coef_hbm, coef_ref),
         ],
         sems,
     )
+    arrivals = chunk_copies(padded_hbm, PAD, padded, PAD, height, sems, len(early))
     early[0].wait()
-    lines[...] = jnp.zeros(lines.shape, F32)
-    lines[pl.ds(1, count, stride=2), :] = halos[0]
-    lines[pl.ds(2, count, stride=2), :] = halos[1]
-    sides[...] = lines[...].T
+    place_sides(halos, lines, sides)
     for copy in early[1:]:
         copy.wait()
     padded[:, PAD + height, :] = halos[2]
     padded[:, PAD - 1, :] = halos[3]
     outs = []
 
+    def wait(chunk):
+        if chunk == 0:
+            arrivals[0].wait()
+        if chunk + 1 < CHUNKS:
+            arrivals[chunk + 1].wait()
+
     def done(chunk):
         here = pl.ds(chunk * rows, rows)
         outs.extend(copies_of([(out_ref.at[:, here, :], out_hbm.at[:, here, :])], sems, chunk))
 
     def finish(level, r, q, tops):
-        here = pl.ds(r, 8)
+        here = pl.ds(r, 16)
         if level >= 2:
             for t in range(tracers):
                 out_ref[t * levels + level, here, :] = q[t]
@@ -835,7 +840,7 @@
                     x = out_ref[t * levels + lower, here, :] + down[lower] * x
                     out_ref[t * levels + lower, here, :] = x
 
-    sweep(padded, vel_ref, k_ref, land_ref, ip_ref, sides, finish, levels, done)
+    sweep(padded, vel_ref, k_ref, land_ref, ip_ref, sides, finish, levels, wait, done)
     for copy in outs:
         copy.wait()
 
@@ -859,7 +864,7 @@
             pltpu.VMEM(ip.shape, F32),
             pltpu.VMEM(coef.shape, F32),
             pltpu.VMEM((count, height, width), F32),
-            pltpu.SemaphoreType.DMA((7,)),
+            pltpu.SemaphoreType.DMA((6 + CHUNKS,)),
         ],
         compiler_params=params(16),
         name="last_part",
@@ -895,15 +900,21 @@
         wide[n * per : (n + 1) * per, :] = returned_ref[n].astype(F32)
     for copy in copies:
         copy.wait()
-    for p in range(pairs):
+    for p in range(0, pairs, 2):
         if p % per_step == 0:
             parts[p // per_step].wait()
-        lhs = wide[pl.ds(slot_ref[p] * tracers, 8), :].astype(BF16)
-        product = lax.dot_general(
-            lhs, weights_ref[p], (((1,), (1,)), ((), ())), preferred_element_type=F32
+        lhs = jnp.concatenate(
+            [wide[pl.ds(slot_ref[p + k] * tracers, 8), :] for k in range(2)], axis=0
         )
-        here = pl.ds(pl.multiple_of(atm_ref[p] * 8, 8), 8)
-        total[here, :] = total[here, :] + product
+        rhs = jnp.concatenate([weights_ref[p], weights_ref[p + 1]], axis=0)
+        both = lax.dot_general(
+            lhs.astype(BF16), rhs, (((1,), (1,)), ((), ())), preferred_element_type=F32
+        )
+        for k in range(2):
+            here = pl.ds(pl.multiple_of(atm_ref[p + k] * 8, 8), 8)
+            total[here, :] = total[here, :] + both[
+                k * 8 : (k + 1) * 8, k * cells : (k + 1) * cells
+            ]
     lane = lane_iota((8, cells))
 
     def mask(b, carry):
@@ -979,13 +990,14 @@
     incoming = all_to_all(message)
     padded, *lines = edges(mesh_sizes, slots, state)
     received = exchange(lines, mesh_sizes)
-    q, edge, ip, edge_far = first_part(padded, velocity, mixing, land, levels)
-    _, q = fix_part(mesh_sizes, q, edge, received, levels)
+    edge, q, ip, edge_far = first_part(padded, velocity, mixing, land, levels)
+    added = halo_part(mesh_sizes, edge, received, levels)
     (
         padded, coef, pick, ip_near, mixing_near, land_near, velocity_near, edge, top_edge,
         *lines, coef_far,
     ) = middle_part(
-        mesh_sizes, incoming, q, ip, mixing, land, velocity, edge_far, fields, levels, cap, window
+        mesh_sizes, incoming, q, ip, mixing, land, velocity, edge_far, added, fields, levels, cap,
+        window,
     )
     received = exchange(lines, mesh_sizes)
     top, state = inner_part(padded, velocity_near, mixing_near, land_near, ip_near, coef, levels)

time: 55.7 us -> 53.2 us (0.955)
  Pallas kernels: 30.4 us -> 27.1 us
  waiting for transfers between devices: 4.11 us -> 6.62 us
  starting transfers between devices: 20 us -> 18.4 us
    all_to_all x2, waiting for transfers between devices: 4.09 us -> 6.45 us  [all_to_all(): return lax.all_to_all(x, AXES, split_axis=0, concat_axis=0, tiled=True)]
    pallas_call x1, Pallas kernels: 2.49 us -> 0.73 us  [halo_part(): pl.pallas_call(functools.partial(halo_kernel, sizes=sizes, levels=levels)...]
    ppermute x8, starting transfers between devices: 9 us -> 7.23 us  [exchange(): return [lax.ppermute(line, AXES, perm) for line, perm in zip(lines, perms)]]
    pallas_call x1, Pallas kernels: 7.37 us -> 5.77 us  [last_part(): pl.pallas_call(functools.partial(last_kernel, levels=levels), out_shape=p...]
    pallas_call x1, Pallas kernels: 3.31 us -> 4.7 us  [first_part(): pl.pallas_call(functools.partial(first_kernel, levels=levels), out_shape=...]
    pallas_call x1, Pallas kernels: 4.04 us -> 3.26 us  [back(): pl.pallas_call(functools.partial(back_kernel, tracers=tracers, cells=cell...]
  transfers between devices with their start and end apart: 10 -> 10, of which waited for: 2 -> 3; matrix products, arithmetic and copies ran while one was open for 0% -> 0% of each run, Pallas kernels for 33% -> 29%
where the time goes in v4:
time: 53.2 us; the launch traced here: 52.9 us
  Pallas kernels  27.1 us (51%)
  starting transfers between devices  18.4 us (35%)
  waiting for transfers between devices  6.62 us (12%)
  between operations  0.8 us (2%)
    all_to_all x2, starting transfers between devices, all_to_all(): return lax.all_to_all(x, AXES, split_axis=0, concat_axis=0, tiled=True)  11.1 us
    ppermute x8, starting transfers between devices, exchange(): return [lax.ppermute(line, AXES, perm) for line, perm in zip(lines, perms)]  7.23 us
    all_to_all x2, waiting for transfers between devices, all_to_all(): return lax.all_to_all(x, AXES, split_axis=0, concat_axis=0, tiled=True)  6.45 us
    pallas_call x1, Pallas kernels, last_part(): pl.pallas_call(functools.partial(last_kernel, levels=levels), out_shape=p...  5.77 us
    pallas_call x1, Pallas kernels, first_part(): pl.pallas_call(functools.partial(first_kernel, levels=levels), out_shape=...  4.7 us
    pallas_call x1, Pallas kernels, middle_part(): pl.pallas_call(functools.partial(middle_kernel, sizes=sizes, levels=level...  3.76 us
    pallas_call x1, Pallas kernels, contributions(): pl.pallas_call(functools.partial(contrib_kernel, sizes=sizes, nodes=nodes...  3.35 us
    pallas_call x1, Pallas kernels, back(): pl.pallas_call(functools.partial(back_kernel, tracers=tracers, cells=cell...  3.26 us
  transfers between devices with their start and end apart: 10, of which 3 were waited for; matrix products, arithmetic and copies ran while one was open for 0% of the time, Pallas kernels for 29%

profile of v4, /device:TPU:0, one launch (start us, length us, event | category | flops | bytes accessed | tf_op | source)
XLA Modules:
  0.0 52.9 jit_solution(11995907826375145691)
XLA Ops:
  0.6 0.0 copy-start
  0.6 0.0 copy-start.1
  0.7 0.0 copy-start.2
  0.7 3.3 %contributions.1 = (bf16[16,104,128]{2,1,0:T(8,128)(2,1)}, s32[96]{0:T(128)}) custom-call(s32[96]{0:T(128)} %bitcast.7, s32[96]{0:T(128)} %atm_hbm.3, s32[96]{0:T(128)} %row_hbm.1, s32[48]{0:T(128)} %rows_hbm.3, bf16[48,8,128]{2,1,0:T(8,128)(2,1)} %flux_hbm.1, bf16[96,128,128]{2,1,0:T(8,128)(2,1)} %weights_hbm.3), custom_call_target="tpu_custom_call" | custom-call | tf_op jit(solution)/shard_map/contributions/pallas_call | solution.py:173
  4.0 7.4 %all-to-all-start = ((bf16[16,104,128]{2,1,0:T(8,128)(2,1)}), bf16[16,104,128]{2,1,0:T(8,128)(2,1)S(1)}, u32[]{:S(2)}, u32[]{:S(2)}) async-start(bf16[16,104,128]{2,1,0:T(8,128)(2,1)} %get-tuple-element.31), calls=%async_computation | async-start | bytes 851968 | tf_op jit(solution)/shard_map/all_to_all | solution.py:960
  11.4 2.3 %edges.1 = (f32[48,144,128]{2,1,0:T(8,128)S(1)}, f32[48,128]{1,0:T(8,128)S(1)}, f32[48,128]{1,0:T(8,128)S(1)}, f32[48,128]{1,0:T(8,128)S(1)}, f32[48,128]{1,0:T(8,128)S(1)}) custom-call(s32[96]{0:T(128)} %get-tuple-element.32.order.slot_hbm, f32[48,128,128]{2,1,0:T(8,128)} %bitcast.4), custom_call_target="tpu_custom_call" | custom-call | tf_op jit(solution)/shard_map/edges/pallas_call | solution.py:299
  13.7 2.0 %collective-permute-start = (f32[48,128]{1,0:T(8,128)S(1)}, f32[48,128]{1,0:T(8,128)S(1)}, u32[]{:S(2)}, u32[]{:S(2)}) collective-permute-start(f32[48,128]{1,0:T(8,128)S(1)} %get-tuple-element.38), channel_id=1, source_target_pairs={{0,4},{1,5},{2,6},{3,7},{4,0},{5,1},{6,2},{7,3},{8,12},{9,13},{10,... | collective-permute-start | bytes 73736 | tf_op jit(solution)/shard_map/ppermute | solution.py:260
  15.7 0.0 collective-permute-start.1
  15.7 0.5 collective-permute-start.2
  16.2 1.1 %collective-permute-start.3 = (f32[48,128]{1,0:T(8,128)S(1)}, f32[48,128]{1,0:T(8,128)S(1)}, u32[]{:S(2)}, u32[]{:S(2)}) collective-permute-start(f32[48,128]{1,0:T(8,128)S(1)} %get-tuple-element.41), channel_id=1, source_target_pairs={{0,3},{1,2},{2,1},{3,0},{4,7},{5,6},{6,5},{7,4},{8,11},{9,10},{10,... | collective-permute-start | bytes 73736 | tf_op jit(solution)/shard_map/ppermute | solution.py:260
  17.2 4.7 %first_part.1 = (f32[4,3,8,128]{3,2,1,0:T(8,128)S(1)}, f32[48,128,128]{2,1,0:T(8,128)}, f32[8,128,128]{2,1,0:T(8,128)}, f32[4,3,8,128]{3,2,1,0:T(8,128)}) custom-call(f32[48,144,128]{2,1,0:T(8,128)S(1)} %get-tuple-element.33.padded, f32[2,8,128,128]{3,2,1,0:T(8,128)S(1)} %copy-done, f32[7,128,128]{2,1,0:T(8,128)S(1)} %copy-done.1, s32[128,128]{1,0:T(8,128)S(1)} %copy-done.2), custom_call_target="tpu_custom_call" | custom-call | tf_op jit(solution)/shard_map/first_part/pallas_call | solution.py:460
  22.0 0.7 %halo_part.1.added_hbm = f32[4,48,128]{2,1,0:T(8,128)} custom-call(f32[4,3,8,128]{3,2,1,0:T(8,128)S(1)} %get-tuple-element.37.edge_ref, f32[48,128]{1,0:T(8,128)S(1)} %collective-permute-done.r0, f32[48,128]{1,0:T(8,128)S(1)} %collective-permute-done.1.r1, f32[48,128]{1,0:T(8,128)S(1)} %collective-permute-done.2.r2, f32[48,128]{1,0:T(8,128)S(1)} %collective-permute-done.3.r3), custom_call_target="tpu_custom_call" | custom-call | tf_op jit(solution)/shard_map/halo_part/pallas_call | solution.py:497
  22.7 1.7 %all-to-all-done.incoming_ref = bf16[16,104,128]{2,1,0:T(8,128)(2,1)S(1)} async-done(((bf16[16,104,128]{2,1,0:T(8,128)(2,1)}), bf16[16,104,128]{2,1,0:T(8,128)(2,1)S(1)}, u32[]{:S(2)}, u32[]{:S(2)}) %all-to-all-start) | async-done | bytes 426016 | tf_op jit(solution)/shard_map/all_to_all | solution.py:960
  24.4 3.8 %middle_part.1 = (f32[48,144,128]{2,1,0:T(8,128)S(1)}, f32[9,128,128]{2,1,0:T(8,128)S(1)}, bf16[256,128]{1,0:T(8,128)(2,1)S(1)}, f32[8,128,128]{2,1,0:T(8,128)S(...) custom-call(bf16[16,104,128]{2,1,0:T(8,128)(2,1)S(1)} %all-to-all-do, ...), custom_call_target="tpu_custom_call" | custom-call | tf_op jit(solution)/shard_map/middle_part/pallas_call | solution.py:641
  28.1 2.1 %collective-permute-start.4 = (f32[48,128]{1,0:T(8,128)S(1)}, f32[48,128]{1,0:T(8,128)S(1)}, u32[]{:S(2)}, u32[]{:S(2)}) collective-permute-start(f32[48,128]{1,0:T(8,128)S(1)} %get-tuple-element.50), channel_id=1, source_target_pairs={{0,4},{1,5},{2,6},{3,7},{4,0},{5,1},{6,2},{7,3},{8,12},{9,13},{10,... | collective-permute-start | bytes 73736 | tf_op jit(solution)/shard_map/ppermute | solution.py:260
  30.2 0.5 collective-permute-start.6
  30.7 1.1 %collective-permute-start.7 = (f32[48,128]{1,0:T(8,128)S(1)}, f32[48,128]{1,0:T(8,128)S(1)}, u32[]{:S(2)}, u32[]{:S(2)}) collective-permute-start(f32[48,128]{1,0:T(8,128)S(1)} %get-tuple-element.53), channel_id=1, source_target_pairs={{0,3},{1,2},{2,1},{3,0},{4,7},{5,6},{6,5},{7,4},{8,11},{9,10},{10,... | collective-permute-start | bytes 73736 | tf_op jit(solution)/shard_map/ppermute | solution.py:260
  31.8 2.1 %inner_part.1 = (f32[6,128,128]{2,1,0:T(8,128)S(1)}, f32[48,144,128]{2,1,0:T(8,128)}) custom-call(f32[48,144,128]{2,1,0:T(8,128)S(1)} %get-tuple-element.42.padded, f32[2,8,128,128]{3,2,1,0:T(8,128)S(1)} %get-tuple-element.43.vel_ref, f32[7,128,128]{2,1,0:T(8,128)S(1)} %get-tuple-element.44.k_ref, s32[128,128]{1,0:T(8,128)S(1)} %get-tuple-element.45.land_ref, ...), custom_call_target="tpu_custom_call" | custom-call | tf_op jit(solution)/shard_map/inner_part/pallas_call | solution.py:697
  33.9 0.2 collective-permute-done.7.r3
  34.1 1.2 %replies.1 = (f32[6,128,128]{2,1,0:T(8,128)S(1)}, f32[4,48,128]{2,1,0:T(8,128)}, bf16[16,72,128]{2,1,0:T(8,128)(2,1)}) custom-call(f32[6,128,128]{2,1,0:T(8,128)S(1)} %get-tuple-element.49.top_in, f32[48,128]{1,0:T(8,128)S(1)} %collective-permute-done.4.r0, f32[48,128]{1,0:T(8,128)S(1)} %collective-permute-done.5.r1, ...), custom_call_target="tpu_custom_call", output_to_operand_aliasing={{0}: (0, {})} | custom-call | tf_op jit(solution)/shard_map/replies/pallas_call | solution.py:766
  35.3 3.8 %all-to-all-start.1 = ((bf16[16,72,128]{2,1,0:T(8,128)(2,1)}), bf16[16,72,128]{2,1,0:T(8,128)(2,1)S(1)}, u32[]{:S(2)}, u32[]{:S(2)}) async-start(bf16[16,72,128]{2,1,0:T(8,128)(2,1)} %get-tuple-element.59), calls=%async_computation.1 | async-start | bytes 589824 | tf_op jit(solution)/shard_map/all_to_all | solution.py:960
  39.0 5.8 %last_part.1 = f32[48,128,128]{2,1,0:T(8,128)} custom-call(f32[48,144,128]{2,1,0:T(8,128)} %get-tuple-element.48.padded_hbm, f32[4,48,128]{2,1,0:T(8,128)} %get-tuple-element.57.halo_hbm, f32[2,8,128,128]{3,2,1,0:T(8,128)} %vel_hbm.3, f32[7,128,128]{2,1,0:T(8,128)} %k_hbm.3, s32[128,128]{1,0:T(8,128)} %land_hbm.3, f32[8,128,128]{2,1,0:T(8,128)} %get-tuple-element.35.ip_hbm, ...), custom_call_target="tpu_custom_call" | custom-call | tf_op jit(solution)/shard_map/last_part/pallas_call | solution.py:851
  44.8 4.8 %all-to-all-done.1.returned_ref = bf16[16,72,128]{2,1,0:T(8,128)(2,1)S(1)} async-done(((bf16[16,72,128]{2,1,0:T(8,128)(2,1)}), bf16[16,72,128]{2,1,0:T(8,128)(2,1)S(1)}, u32[]{:S(2)}, u32[]{:S(2)}) %all-to-all-start.1) | async-done | bytes 294944 | tf_op jit(solution)/shard_map/all_to_all | solution.py:960
  49.6 3.3 %back.1 = f32[6,48,128]{2,1,0:T(8,128)} custom-call(s32[96]{0:T(128)} %get-tuple-element.32.order.slot_hbm, s32[96]{0:T(128)} %atm_hbm.3, s32[48]{0:T(128)} %rows_hbm.3, bf16[16,72,128]{2,1,0:T(8,128)(2,1)S(1)} %all-to-all-done.1.returned_ref, bf16[96,128,128]{2,1,0:T(8,128)(2,1)} %weights_hbm.3), custom_call_target="tpu_custom_call" | custom-call | tf_op jit(solution)/shard_map/back/pallas_call | solution.py:938
  (11 shorter events, 0.0 us)
Async XLA Ops:
  0.6 16.6 %copy-start = (f32[2,8,128,128]{3,2,1,0:T(8,128)S(1)}, f32[2,8,128,128]{3,2,1,0:T(8,128)}, u32[]{:S(2)}) copy-start(f32[2,8,128,128]{3,2,1,0:T(8,128)} %vel_hbm.3) | copy-start | bytes 3145732
  0.6 16.6 %copy-start.1 = (f32[7,128,128]{2,1,0:T(8,128)S(1)}, f32[7,128,128]{2,1,0:T(8,128)}, u32[]{:S(2)}) copy-start(f32[7,128,128]{2,1,0:T(8,128)} %k_hbm.3) | copy-start | bytes 1376260
  0.7 16.6 %copy-start.2 = (s32[128,128]{1,0:T(8,128)S(1)}, s32[128,128]{1,0:T(8,128)}, u32[]{:S(2)}) copy-start(s32[128,128]{1,0:T(8,128)} %land_hbm.3) | copy-start | bytes 196612
  4.0 20.4 %all-to-all-start = ((bf16[16,104,128]{2,1,0:T(8,128)(2,1)}), bf16[16,104,128]{2,1,0:T(8,128)(2,1)S(1)}, u32[]{:S(2)}, u32[]{:S(2)}) async-start(bf16[16,104,128]{2,1,0:T(8,128)(2,1)} %get-tuple-element.31), calls=%async_computation | async-start | bytes 851968 | tf_op jit(solution)/shard_map/all_to_all | solution.py:960
  13.7 8.3 %collective-permute-start = (f32[48,128]{1,0:T(8,128)S(1)}, f32[48,128]{1,0:T(8,128)S(1)}, u32[]{:S(2)}, u32[]{:S(2)}) collective-permute-start(f32[48,128]{1,0:T(8,128)S(1)} %get-tuple-element.38), channel_id=1, source_target_pairs={{0,4},{1,5},{2,6},{3,7},{4,0},{5,1},{6,2},{7,3},{8,12},{9,13},{10,... | collective-permute-start | bytes 73736 | tf_op jit(solution)/shard_map/ppermute | solution.py:260
  15.7 6.3 %collective-permute-start.1 = (f32[48,128]{1,0:T(8,128)S(1)}, f32[48,128]{1,0:T(8,128)S(1)}, u32[]{:S(2)}, u32[]{:S(2)}) collective-permute-start(f32[48,128]{1,0:T(8,128)S(1)} %get-tuple-element.39), channel_id=1, source_target_pairs={{0,1},{1,0},{2,3},{3,2},{4,8},{5,9},{6,10},{7,11},{8,4},{9,5},{10,... | collective-permute-start | bytes 73736 | tf_op jit(solution)/shard_map/ppermute | solution.py:260
  15.7 6.3 %collective-permute-start.2 = (f32[48,128]{1,0:T(8,128)S(1)}, f32[48,128]{1,0:T(8,128)S(1)}, u32[]{:S(2)}, u32[]{:S(2)}) collective-permute-start(f32[48,128]{1,0:T(8,128)S(1)} %get-tuple-element.40), channel_id=1, source_target_pairs={{0,1},{1,0},{2,3},{3,2},{4,5},{5,4},{6,7},{7,6},{8,9},{9,8},{10,11... | collective-permute-start | bytes 73736 | tf_op jit(solution)/shard_map/ppermute | solution.py:260
  16.2 5.8 %collective-permute-start.3 = (f32[48,128]{1,0:T(8,128)S(1)}, f32[48,128]{1,0:T(8,128)S(1)}, u32[]{:S(2)}, u32[]{:S(2)}) collective-permute-start(f32[48,128]{1,0:T(8,128)S(1)} %get-tuple-element.41), channel_id=1, source_target_pairs={{0,3},{1,2},{2,1},{3,0},{4,7},{5,6},{6,5},{7,4},{8,11},{9,10},{10,... | collective-permute-start | bytes 73736 | tf_op jit(solution)/shard_map/ppermute | solution.py:260
  28.1 5.7 %collective-permute-start.4 = (f32[48,128]{1,0:T(8,128)S(1)}, f32[48,128]{1,0:T(8,128)S(1)}, u32[]{:S(2)}, u32[]{:S(2)}) collective-permute-start(f32[48,128]{1,0:T(8,128)S(1)} %get-tuple-element.50), channel_id=1, source_target_pairs={{0,4},{1,5},{2,6},{3,7},{4,0},{5,1},{6,2},{7,3},{8,12},{9,13},{10,... | collective-permute-start | bytes 73736 | tf_op jit(solution)/shard_map/ppermute | solution.py:260
  30.2 3.7 %collective-permute-start.5 = (f32[48,128]{1,0:T(8,128)S(1)}, f32[48,128]{1,0:T(8,128)S(1)}, u32[]{:S(2)}, u32[]{:S(2)}) collective-permute-start(f32[48,128]{1,0:T(8,128)S(1)} %get-tuple-element.51), channel_id=1, source_target_pairs={{0,1},{1,0},{2,3},{3,2},{4,8},{5,9},{6,10},{7,11},{8,4},{9,5},{10,... | collective-permute-start | bytes 73736 | tf_op jit(solution)/shard_map/ppermute | solution.py:260
  30.2 3.7 %collective-permute-start.6 = (f32[48,128]{1,0:T(8,128)S(1)}, f32[48,128]{1,0:T(8,128)S(1)}, u32[]{:S(2)}, u32[]{:S(2)}) collective-permute-start(f32[48,128]{1,0:T(8,128)S(1)} %get-tuple-element.52), channel_id=1, source_target_pairs={{0,1},{1,0},{2,3},{3,2},{4,5},{5,4},{6,7},{7,6},{8,9},{9,8},{10,11... | collective-permute-start | bytes 73736 | tf_op jit(solution)/shard_map/ppermute | solution.py:260
  30.7 3.3 %collective-permute-start.7 = (f32[48,128]{1,0:T(8,128)S(1)}, f32[48,128]{1,0:T(8,128)S(1)}, u32[]{:S(2)}, u32[]{:S(2)}) collective-permute-start(f32[48,128]{1,0:T(8,128)S(1)} %get-tuple-element.53), channel_id=1, source_target_pairs={{0,3},{1,2},{2,1},{3,0},{4,7},{5,6},{6,5},{7,4},{8,11},{9,10},{10,... | collective-permute-start | bytes 73736 | tf_op jit(solution)/shard_map/ppermute | solution.py:260
  35.3 14.3 %all-to-all-start.1 = ((bf16[16,72,128]{2,1,0:T(8,128)(2,1)}), bf16[16,72,128]{2,1,0:T(8,128)(2,1)S(1)}, u32[]{:S(2)}, u32[]{:S(2)}) async-start(bf16[16,72,128]{2,1,0:T(8,128)(2,1)} %get-tuple-element.59), calls=%async_computation.1 | async-start | bytes 589824 | tf_op jit(solution)/shard_map/all_to_all | solution.py:960

commit v5 on v4

--- a/solution.py
+++ b/solution.py
@@ -13,6 +13,7 @@
 BF16 = jnp.bfloat16
 AXES = ("tx", "ty", "tz")
 PAD = 8
+TOP_PLANES = 6
 CHUNKS = 4
 
 
@@ -39,6 +40,10 @@
     for copy in copies:
         copy.start()
     return copies
+
+
+def weight_parts(pairs):
+    return [0] + [pairs * eighths // 16 * 2 for eighths in (2, 4, 6)] + [pairs]
 
 
 def chunk_copies(src, src_pad, dst, dst_pad, height, sems, base=0):
@@ -78,7 +83,7 @@
     *, sizes, nodes, cap, window, steps, message_rows,
 ):
     pairs = weights_ref.shape[0]
-    per_step = pairs // steps
+    bounds = weight_parts(pairs)
     fields = flux_ref.shape[1]
     lanes = flux_ref.shape[2]
     width = weights_ref.shape[2]
@@ -93,11 +98,11 @@
     ]
     parts = [
         pltpu.make_async_copy(
-            weights_hbm.at[pl.ds(n * per_step, per_step)],
-            weights_ref.at[pl.ds(n * per_step, per_step)],
+            weights_hbm.at[pl.ds(first, last - first)],
+            weights_ref.at[pl.ds(first, last - first)],
             sems.at[len(small) + n],
         )
-        for n in range(steps)
+        for n, (first, last) in enumerate(zip(bounds, bounds[1:]))
     ]
     for copy in small + parts:
         copy.start()
@@ -126,7 +131,7 @@
         message[pl.ds(start, 8), :] = jnp.where(lane8 == base + s, named, tile)
         return carry
 
-    lax.fori_loop(0, pairs, place, 0, unroll=4)
+    lax.fori_loop(0, pairs, place, 0, unroll=16)
     slots_out = pltpu.make_async_copy(slot_ref, slot_hbm, sems.at[0])
     slots_out.start()
     small[2].wait()
@@ -139,9 +144,9 @@
         return carry
 
     lax.fori_loop(0, flux_ref.shape[0], mask, 0, unroll=8)
-    for n in range(steps):
-        parts[n].wait()
-        for p in range(n * per_step, (n + 1) * per_step, 2):
+    for part, first, last in zip(parts, bounds, bounds[1:]):
+        part.wait()
+        for p in range(first, last, 2):
             lhs = jnp.concatenate([masked[atm_ref[p]], masked[atm_ref[p + 1]]], axis=0)
             rhs = jnp.concatenate([weights_ref[p], weights_ref[p + 1]], axis=1)
             both = jnp.dot(lhs.astype(BF16), rhs, preferred_element_type=F32)
@@ -194,7 +199,7 @@
             pltpu.VMEM(flux.shape, F32),
             pltpu.VMEM((nodes * message_rows, width), F32),
             pltpu.VMEM((nodes, message_rows, width), BF16),
-            pltpu.SemaphoreType.DMA((5 + steps,)),
+            pltpu.SemaphoreType.DMA((9,)),
             pltpu.SemaphoreType.DMA((steps,)),
         ],
         compiler_params=params(10),
@@ -391,8 +396,8 @@
 
 
 def first_kernel(
-    padded, vel_ref, k_ref, land_ref, edge_ref, q_hbm, ip_hbm, edge_hbm,
-    q_ref, ip_ref, cols, lines, sems, *, levels,
+    padded, vel_ref, k_ref, land_ref, q_hbm, ip_hbm, down_hbm, edge_hbm,
+    q_ref, ip_ref, down_ref, edge_ref, cols, lines, sems, *, levels,
 ):
     height, width = land_ref.shape
     sea = land_ref[...].astype(F32)
@@ -406,10 +411,12 @@
             pivot = 1.0 + upper + lower - lower * lower * below
         below = 1.0 / pivot
         ip_ref[level] = below
+        down_ref[level] = upper * below
     lower = k_ref[1] * sea
-    ip_ref[1] = 1.0 + lower - lower * lower * below
-    ip_ref[0] = k_ref[0] * sea
-    outs = copies_of([(ip_ref, ip_hbm)], sems)
+    down_ref[1] = 1.0 + lower - lower * lower * below
+    down_ref[0] = k_ref[0] * sea
+    ip_ref[:2] = jnp.zeros((2, height, width), F32)
+    outs = copies_of([(ip_ref, ip_hbm), (down_ref, down_hbm)], sems, 2)
     lane = lane_iota((8, width))
 
     def coefficients(i, carry):
@@ -448,7 +455,7 @@
             q_ref[t * levels + level, pl.ds(r, 16), :] = value
 
     sweep(padded, vel_ref, k_ref, land_ref, ip_ref, None, finish, levels)
-    outs.extend(copies_of([(q_ref, q_hbm)], sems, 2))
+    outs.extend(copies_of([(q_ref, q_hbm)], sems, 0))
     for copy in outs:
         copy.wait()
 
@@ -460,53 +467,25 @@
     return pl.pallas_call(
         functools.partial(first_kernel, levels=levels),
         out_shape=(
-            jax.ShapeDtypeStruct(edge, F32),
             pltpu.HBM((count, height, width), F32),
+            pltpu.HBM((levels, height, width), F32),
             pltpu.HBM((levels, height, width), F32),
             pltpu.HBM(edge, F32),
         ),
         in_specs=[vmem()] * 4,
-        out_specs=(vmem(), hbm(), hbm(), hbm()),
+        out_specs=(hbm(),) * 4,
         scratch_shapes=[
             pltpu.VMEM((count, height, width), F32),
             pltpu.VMEM((levels, height, width), F32),
+            pltpu.VMEM((levels, height, width), F32),
+            pltpu.VMEM(edge, F32),
             pltpu.VMEM((height, width), F32),
             pltpu.VMEM((width, height), F32),
-            pltpu.SemaphoreType.DMA((3,)),
+            pltpu.SemaphoreType.DMA((4,)),
         ],
         compiler_params=params(8),
         name="first_part",
     )(padded, velocity, mixing, land)
-
-
-def halo_kernel(edge_ref, r0, r1, r2, r3, added_hbm, halos, added, sems, *, sizes, levels):
-    tracers = halos.shape[1] // levels
-    sort_halos(sizes, (r0, r1, r2, r3), halos)
-
-    def level_done(side, level, q, rhs):
-        value = rhs if level == 0 else q
-        added[side, pl.ds(level, tracers, stride=levels), :] = value
-
-    correct(edge_ref, halos, level_done, levels)
-    for copy in copies_of([(added, added_hbm)], sems):
-        copy.wait()
-
-
-def halo_part(sizes, edge, received, levels):
-    shape = (4,) + received[0].shape
-    return pl.pallas_call(
-        functools.partial(halo_kernel, sizes=sizes, levels=levels),
-        out_shape=pltpu.HBM(shape, F32),
-        in_specs=[vmem()] * 5,
-        out_specs=hbm(),
-        scratch_shapes=[
-            pltpu.VMEM(shape, F32),
-            pltpu.VMEM(shape, F32),
-            pltpu.SemaphoreType.DMA((1,)),
-        ],
-        compiler_params=params(4),
-        name="halo_part",
-    )(edge, *received)
 
 
 def place_sides(added, lines, sides):
@@ -518,10 +497,10 @@
 
 
 def middle_kernel(
-    incoming_ref, q_hbm, ip_hbm, k_hbm, land_hbm, vel_hbm, edge_hbm, added_hbm,
+    incoming_ref, q_hbm, down_hbm, ip_hbm, k_hbm, land_hbm, vel_hbm, edge_hbm, r0, r1, r2, r3,
     x_ref, coef_ref, pick_ref, ip_ref, k_ref, land_ref, vel_ref, edge_ref, top_edge_ref,
     s0, s1, s2, s3, coef_hbm,
-    q_ref, wide, flux, cols, lines, added, sides, sems, *, sizes, levels, cap, window,
+    q_ref, down_ref, wide, flux, cols, lines, halos, added, sides, sems, *, sizes, levels, cap, window,
 ):
     count, height, width = q_ref.shape
     tracers = count // levels
@@ -529,10 +508,10 @@
     fields = flux.shape[0]
     rows = height // CHUNKS
     early = copies_of(
-        [(added_hbm, added), (ip_hbm, ip_ref), (land_hbm, land_ref), (k_hbm, k_ref)], sems
+        [(edge_hbm, edge_ref), (down_hbm, down_ref), (land_hbm, land_ref)], sems
     )
     arrivals = chunk_copies(q_hbm, 0, q_ref, 0, height, sems, 6)
-    late = copies_of([(vel_hbm, vel_ref), (edge_hbm, edge_ref)], sems, 4)
+    late = copies_of([(vel_hbm, vel_ref), (ip_hbm, ip_ref), (k_hbm, k_ref)], sems, 3)
     clear_pads(x_ref)
     span = nodes * message_rows
     wide[span:, :] = jnp.zeros((wide.shape[0] - span, width), F32)
@@ -561,13 +540,20 @@
         flux[f] = jnp.dot(selector, stacked, preferred_element_type=F32)
     for copy in early:
         copy.wait()
+    sort_halos(sizes, (r0, r1, r2, r3), halos)
+
+    def level_done(side, level, q, rhs):
+        value = rhs if level == 0 else q
+        added[side, pl.ds(level, tracers, stride=levels), :] = value
+
+    correct(edge_ref, halos, level_done, levels)
     place_sides(added, lines, sides)
     sea = land_ref[...].astype(F32)
     stirring = 1.0 + 0.5 * (
         flux[fields - 2] * flux[fields - 2] + flux[fields - 1] * flux[fields - 1]
     )
-    top_link = ip_ref[0] * stirring
-    inverse1 = 1.0 / (ip_ref[1] + top_link)
+    top_link = down_ref[0] * stirring
+    inverse1 = 1.0 / (down_ref[1] + top_link)
     inverse0 = 1.0 / (1.0 + top_link - top_link * top_link * inverse1)
     coef_ref[tracers] = top_link
     coef_ref[tracers + 1] = inverse1
@@ -588,13 +574,12 @@
             r = pl.multiple_of(first + i * 16, 16)
             here = pl.ds(r, 16)
             side = sides[here, :].astype(BF16)
-            sea8 = land_ref[here, :].astype(F32)
             link0 = coef_ref[tracers, here, :]
             inv1 = coef_ref[tracers + 1, here, :]
             inv0 = coef_ref[tracers + 2, here, :]
             down = [None, link0 * inv1]
             for level in range(2, levels):
-                down.append(k_ref[level - 1, here, :] * sea8 * ip_ref[level, here, :])
+                down.append(down_ref[level, here, :])
             acc = jnp.zeros((16, width), BF16)
             for t in range(tracers):
                 base = t * levels
@@ -616,7 +601,7 @@
             cols[here, :] = acc
             return carry
 
-        lax.fori_loop(0, rows // 16, block, 0)
+        lax.fori_loop(0, rows // 16, block, 0, unroll=2)
     lines[...] = cols[...].T
     store_sends(
         sizes, lines, x_ref[:, PAD, :], x_ref[:, PAD + height - 1, :], (s0, s1, s2, s3)
@@ -631,7 +616,7 @@
         copy.wait()
 
 
-def middle_part(sizes, incoming, q, ip, mixing, land, velocity, edge, added, fields, levels, cap, window):
+def middle_part(sizes, incoming, q, down, ip, mixing, land, velocity, edge, received, fields, levels, cap, window):
     count, height, width = q.shape
     nodes, message_rows, _ = incoming.shape
     tracers = count // levels
@@ -645,25 +630,27 @@
             jax.ShapeDtypeStruct((tracers + 3, height, width), F32),
             jax.ShapeDtypeStruct((groups * 128, height), BF16),
             *near,
-            jax.ShapeDtypeStruct((4, 8, width), F32),
+            jax.ShapeDtypeStruct((TOP_PLANES, 8, width), F32),
             line, line, line, line,
             pltpu.HBM((tracers + 3, height, width), F32),
         ),
-        in_specs=[vmem()] + [hbm()] * 7,
+        in_specs=[vmem()] + [hbm()] * 7 + [vmem()] * 4,
         out_specs=(vmem(),) * 13 + (hbm(),),
         scratch_shapes=[
             pltpu.VMEM(q.shape, F32),
+            pltpu.VMEM(down.shape, F32),
             pltpu.VMEM((nodes * message_rows + window * fields, width), F32),
             pltpu.VMEM((fields, height, width), F32),
             pltpu.VMEM((height, width), F32),
             pltpu.VMEM((width, height), F32),
-            pltpu.VMEM(added.shape, F32),
+            pltpu.VMEM((4, count, width), F32),
+            pltpu.VMEM((4, count, width), F32),
             pltpu.VMEM((height, width), F32),
             pltpu.SemaphoreType.DMA((7 + CHUNKS,)),
         ],
         compiler_params=params(10),
         name="middle_part",
-    )(incoming, *pin(q, ip, mixing, land, velocity, edge, added))
+    )(incoming, *pin(q, down, ip, mixing, land, velocity, edge), *received)
 
 
 def top_level(coef_ref, here, t, tracers, q1, rhs):
@@ -874,22 +861,22 @@
 def back_kernel(
     slot_hbm, atm_hbm, rows_hbm, returned_ref, weights_hbm, out_hbm,
     slot_ref, atm_ref, rows_ref, weights_ref, out_ref, wide, total, sems,
-    *, tracers, cells, steps,
+    *, tracers, cells,
 ):
     nodes, per, width = returned_ref.shape
     pairs = weights_ref.shape[0]
     blocks = out_ref.shape[1]
-    per_step = pairs // steps
+    bounds = weight_parts(pairs)
     copies = copies_of(
         [(slot_hbm, slot_ref), (atm_hbm, atm_ref), (rows_hbm, rows_ref)], sems
     )
     parts = copies_of(
         [
             (
-                weights_hbm.at[pl.ds(n * per_step, per_step)],
-                weights_ref.at[pl.ds(n * per_step, per_step)],
+                weights_hbm.at[pl.ds(first, last - first)],
+                weights_ref.at[pl.ds(first, last - first)],
             )
-            for n in range(steps)
+            for first, last in zip(bounds, bounds[1:])
         ],
         sems,
         len(copies),
@@ -901,8 +888,8 @@
     for copy in copies:
         copy.wait()
     for p in range(0, pairs, 2):
-        if p % per_step == 0:
-            parts[p // per_step].wait()
+        if p in bounds:
+            parts[bounds.index(p)].wait()
         lhs = jnp.concatenate(
             [wide[pl.ds(slot_ref[p + k] * tracers, 8), :] for k in range(2)], axis=0
         )
@@ -934,9 +921,8 @@
     nodes, per, _ = returned.shape
     blocks = rows.shape[0]
     ints = jnp.int32
-    steps = 4
     by_tracer = pl.pallas_call(
-        functools.partial(back_kernel, tracers=tracers, cells=cells, steps=steps),
+        functools.partial(back_kernel, tracers=tracers, cells=cells),
         out_shape=pltpu.HBM((tracers, blocks, cells), F32),
         in_specs=[hbm()] * 3 + [vmem(), hbm()],
         out_specs=hbm(),
@@ -948,7 +934,7 @@
             pltpu.VMEM((tracers, blocks, cells), F32),
             pltpu.VMEM((nodes * per + 8, width), F32),
             pltpu.VMEM((blocks * 8, cells), F32),
-            pltpu.SemaphoreType.DMA((3 + steps,)),
+            pltpu.SemaphoreType.DMA((7,)),
         ],
         compiler_params=params(8),
         name="back",
@@ -990,13 +976,12 @@
     incoming = all_to_all(message)
     padded, *lines = edges(mesh_sizes, slots, state)
     received = exchange(lines, mesh_sizes)
-    edge, q, ip, edge_far = first_part(padded, velocity, mixing, land, levels)
-    added = halo_part(mesh_sizes, edge, received, levels)
+    q, ip, down, edge_far = first_part(padded, velocity, mixing, land, levels)
     (
         padded, coef, pick, ip_near, mixing_near, land_near, velocity_near, edge, top_edge,
         *lines, coef_far,
     ) = middle_part(
-        mesh_sizes, incoming, q, ip, mixing, land, velocity, edge_far, added, fields, levels, cap,
+        mesh_sizes, incoming, q, down, ip, mixing, land, velocity, edge_far, received, fields, levels, cap,
         window,
     )
     received = exchange(lines, mesh_sizes)

time: 53.2 us -> 52 us (0.977)
  Pallas kernels: 27.1 us -> 26 us
  starting transfers between devices: 18.4 us -> 17.6 us
  waiting for transfers between devices: 6.62 us -> 7.24 us
    ppermute x8, starting transfers between devices: 7.23 us -> 6.5 us  [exchange(): return [lax.ppermute(line, AXES, perm) for line, perm in zip(lines, perms)]]
    pallas_call x1 -> x0, Pallas kernels: 0.73 us -> none  [halo_part(): pl.pallas_call(functools.partial(halo_kernel, sizes=sizes, levels=levels)...]
    all_to_all x2, waiting for transfers between devices: 6.45 us -> 7.07 us  [all_to_all(): return lax.all_to_all(x, AXES, split_axis=0, concat_axis=0, tiled=True)]
where the time goes in v5:
time: 52 us; the launch traced here: 51.6 us
  Pallas kernels  26 us (50%)
  starting transfers between devices  17.6 us (34%)
  waiting for transfers between devices  7.24 us (14%)
  between operations  0.79 us (2%)
    all_to_all x2, starting transfers between devices, all_to_all(): return lax.all_to_all(x, AXES, split_axis=0, concat_axis=0, tiled=True)  11.1 us
    all_to_all x2, waiting for transfers between devices, all_to_all(): return lax.all_to_all(x, AXES, split_axis=0, concat_axis=0, tiled=True)  7.07 us
    ppermute x8, starting transfers between devices, exchange(): return [lax.ppermute(line, AXES, perm) for line, perm in zip(lines, perms)]  6.5 us
    pallas_call x1, Pallas kernels, last_part(): pl.pallas_call(functools.partial(last_kernel, levels=levels), out_shape=p...  5.77 us
    pallas_call x1, Pallas kernels, first_part(): pl.pallas_call(functools.partial(first_kernel, levels=levels), out_shape=...  4.81 us
    pallas_call x1, Pallas kernels, middle_part(): pl.pallas_call(functools.partial(middle_kernel, sizes=sizes, levels=level...  3.38 us
    pallas_call x1, Pallas kernels, back(): pl.pallas_call(functools.partial(back_kernel, tracers=tracers, cells=cell...  3.26 us
    pallas_call x1, Pallas kernels, contributions(): pl.pallas_call(functools.partial(contrib_kernel, sizes=sizes, nodes=nodes...  3.22 us
  transfers between devices with their start and end apart: 10, of which 3 were waited for; matrix products, arithmetic and copies ran while one was open for 0% of the time, Pallas kernels for 29%

profile of v5, /device:TPU:0, one launch (start us, length us, event | category | flops | bytes accessed | tf_op | source)
XLA Modules:
  0.0 51.6 jit_solution(14894266692088079584)
XLA Ops:
  0.6 0.0 copy-start
  0.6 0.0 copy-start.1
  0.7 0.0 copy-start.2
  0.7 3.2 %contributions.1 = (bf16[16,104,128]{2,1,0:T(8,128)(2,1)}, s32[96]{0:T(128)}) custom-call(s32[96]{0:T(128)} %bitcast.7, s32[96]{0:T(128)} %atm_hbm.3, s32[96]{0:T(128)} %row_hbm.1, s32[48]{0:T(128)} %rows_hbm.3, bf16[48,8,128]{2,1,0:T(8,128)(2,1)} %flux_hbm.1, bf16[96,128,128]{2,1,0:T(8,128)(2,1)} %weights_hbm.3), custom_call_target="tpu_custom_call" | custom-call | tf_op jit(solution)/shard_map/contributions/pallas_call | solution.py:178
  3.9 7.4 %all-to-all-start = ((bf16[16,104,128]{2,1,0:T(8,128)(2,1)}), bf16[16,104,128]{2,1,0:T(8,128)(2,1)S(1)}, u32[]{:S(2)}, u32[]{:S(2)}) async-start(bf16[16,104,128]{2,1,0:T(8,128)(2,1)} %get-tuple-element.31), calls=%async_computation | async-start | bytes 851968 | tf_op jit(solution)/shard_map/all_to_all | solution.py:946
  11.3 2.3 %edges.1 = (f32[48,144,128]{2,1,0:T(8,128)S(1)}, f32[48,128]{1,0:T(8,128)S(1)}, f32[48,128]{1,0:T(8,128)S(1)}, f32[48,128]{1,0:T(8,128)S(1)}, f32[48,128]{1,0:T(8,128)S(1)}) custom-call(s32[96]{0:T(128)} %get-tuple-element.32.order.slot_hbm, f32[48,128,128]{2,1,0:T(8,128)} %bitcast.4), custom_call_target="tpu_custom_call" | custom-call | tf_op jit(solution)/shard_map/edges/pallas_call | solution.py:304
  13.5 2.0 %collective-permute-start = (f32[48,128]{1,0:T(8,128)S(1)}, f32[48,128]{1,0:T(8,128)S(1)}, u32[]{:S(2)}, u32[]{:S(2)}) collective-permute-start(f32[48,128]{1,0:T(8,128)S(1)} %get-tuple-element.38), channel_id=1, source_target_pairs={{0,4},{1,5},{2,6},{3,7},{4,0},{5,1},{6,2},{7,3},{8,12},{9,13},{10,... | collective-permute-start | bytes 73736 | tf_op jit(solution)/shard_map/ppermute | solution.py:265
  15.5 0.5 collective-permute-start.2
  16.0 1.1 %collective-permute-start.3 = (f32[48,128]{1,0:T(8,128)S(1)}, f32[48,128]{1,0:T(8,128)S(1)}, u32[]{:S(2)}, u32[]{:S(2)}) collective-permute-start(f32[48,128]{1,0:T(8,128)S(1)} %get-tuple-element.41), channel_id=1, source_target_pairs={{0,3},{1,2},{2,1},{3,0},{4,7},{5,6},{6,5},{7,4},{8,11},{9,10},{10,... | collective-permute-start | bytes 73736 | tf_op jit(solution)/shard_map/ppermute | solution.py:265
  17.1 4.8 %first_part.1 = (f32[48,128,128]{2,1,0:T(8,128)}, f32[8,128,128]{2,1,0:T(8,128)}, f32[8,128,128]{2,1,0:T(8,128)}, f32[4,3,8,128]{3,2,1,0:T(8,128)}) custom-call(f32[48,144,128]{2,1,0:T(8,128)S(1)} %get-tuple-element.33.padded, f32[2,8,128,128]{3,2,1,0:T(8,128)S(1)} %copy-done, f32[7,128,128]{2,1,0:T(8,128)S(1)} %copy-done.1, s32[128,128]{1,0:T(8,128)S(1)} %copy-done.2), custom_call_target="tpu_custom_call" | custom-call | tf_op jit(solution)/shard_map/first_part/pallas_call | solution.py:467
  22.0 0.0 collective-permute-done.2.r2
  22.0 0.0 collective-permute-done.3.r3
  22.0 2.3 %all-to-all-done.incoming_ref = bf16[16,104,128]{2,1,0:T(8,128)(2,1)S(1)} async-done(((bf16[16,104,128]{2,1,0:T(8,128)(2,1)}), bf16[16,104,128]{2,1,0:T(8,128)(2,1)S(1)}, u32[]{:S(2)}, u32[]{:S(2)}) %all-to-all-start) | async-done | bytes 426016 | tf_op jit(solution)/shard_map/all_to_all | solution.py:946
  24.3 3.4 %middle_part.1 = (f32[48,144,128]{2,1,0:T(8,128)S(1)}, f32[9,128,128]{2,1,0:T(8,128)S(1)}, bf16[256,128]{1,0:T(8,128)(2,1)S(1)}, f32[8,128,128]{2,1,0:T(8,128)S(...) custom-call(bf16[16,104,128]{2,1,0:T(8,128)(2,1)S(1)} %all-to-all-do, ...), custom_call_target="tpu_custom_call" | custom-call | tf_op jit(solution)/shard_map/middle_part/pallas_call | solution.py:626
  27.6 1.3 %collective-permute-start.4 = (f32[48,128]{1,0:T(8,128)S(1)}, f32[48,128]{1,0:T(8,128)S(1)}, u32[]{:S(2)}, u32[]{:S(2)}) collective-permute-start(f32[48,128]{1,0:T(8,128)S(1)} %get-tuple-element.50), channel_id=1, source_target_pairs={{0,4},{1,5},{2,6},{3,7},{4,0},{5,1},{6,2},{7,3},{8,12},{9,13},{10,... | collective-permute-start | bytes 73736 | tf_op jit(solution)/shard_map/ppermute | solution.py:265
  29.0 0.5 collective-permute-start.6
  29.5 1.1 %collective-permute-start.7 = (f32[48,128]{1,0:T(8,128)S(1)}, f32[48,128]{1,0:T(8,128)S(1)}, u32[]{:S(2)}, u32[]{:S(2)}) collective-permute-start(f32[48,128]{1,0:T(8,128)S(1)} %get-tuple-element.53), channel_id=1, source_target_pairs={{0,3},{1,2},{2,1},{3,0},{4,7},{5,6},{6,5},{7,4},{8,11},{9,10},{10,... | collective-permute-start | bytes 73736 | tf_op jit(solution)/shard_map/ppermute | solution.py:265
  30.6 2.1 %inner_part.1 = (f32[6,128,128]{2,1,0:T(8,128)S(1)}, f32[48,144,128]{2,1,0:T(8,128)}) custom-call(f32[48,144,128]{2,1,0:T(8,128)S(1)} %get-tuple-element.42.padded, f32[2,8,128,128]{3,2,1,0:T(8,128)S(1)} %get-tuple-element.43.vel_ref, f32[7,128,128]{2,1,0:T(8,128)S(1)} %get-tuple-element.44.k_ref, s32[128,128]{1,0:T(8,128)S(1)} %get-tuple-element.45.land_ref, ...), custom_call_target="tpu_custom_call" | custom-call | tf_op jit(solution)/shard_map/inner_part/pallas_call | solution.py:684
  32.7 0.2 collective-permute-done.7.r3
  32.8 1.2 %replies.1 = (f32[6,128,128]{2,1,0:T(8,128)S(1)}, f32[4,48,128]{2,1,0:T(8,128)}, bf16[16,72,128]{2,1,0:T(8,128)(2,1)}) custom-call(f32[6,128,128]{2,1,0:T(8,128)S(1)} %get-tuple-element.49.top_in, f32[48,128]{1,0:T(8,128)S(1)} %collective-permute-done.4.r0, f32[48,128]{1,0:T(8,128)S(1)} %collective-permute-done.5.r1, ...), custom_call_target="tpu_custom_call", output_to_operand_aliasing={{0}: (0, {})} | custom-call | tf_op jit(solution)/shard_map/replies/pallas_call | solution.py:753
  34.1 3.8 %all-to-all-start.1 = ((bf16[16,72,128]{2,1,0:T(8,128)(2,1)}), bf16[16,72,128]{2,1,0:T(8,128)(2,1)S(1)}, u32[]{:S(2)}, u32[]{:S(2)}) async-start(bf16[16,72,128]{2,1,0:T(8,128)(2,1)} %get-tuple-element.59), calls=%async_computation.1 | async-start | bytes 589824 | tf_op jit(solution)/shard_map/all_to_all | solution.py:946
  37.8 5.8 %last_part.1 = f32[48,128,128]{2,1,0:T(8,128)} custom-call(f32[48,144,128]{2,1,0:T(8,128)} %get-tuple-element.48.padded_hbm, f32[4,48,128]{2,1,0:T(8,128)} %get-tuple-element.57.halo_hbm, f32[2,8,128,128]{3,2,1,0:T(8,128)} %vel_hbm.3, f32[7,128,128]{2,1,0:T(8,128)} %k_hbm.3, s32[128,128]{1,0:T(8,128)} %land_hbm.3, f32[8,128,128]{2,1,0:T(8,128)} %get-tuple-element.36.ip_hbm, ...), custom_call_target="tpu_custom_call" | custom-call | tf_op jit(solution)/shard_map/last_part/pallas_call | solution.py:838
  43.6 4.8 %all-to-all-done.1.returned_ref = bf16[16,72,128]{2,1,0:T(8,128)(2,1)S(1)} async-done(((bf16[16,72,128]{2,1,0:T(8,128)(2,1)}), bf16[16,72,128]{2,1,0:T(8,128)(2,1)S(1)}, u32[]{:S(2)}, u32[]{:S(2)}) %all-to-all-start.1) | async-done | bytes 294944 | tf_op jit(solution)/shard_map/all_to_all | solution.py:946
  48.4 3.3 %back.1 = f32[6,48,128]{2,1,0:T(8,128)} custom-call(s32[96]{0:T(128)} %get-tuple-element.32.order.slot_hbm, s32[96]{0:T(128)} %atm_hbm.3, s32[48]{0:T(128)} %rows_hbm.3, bf16[16,72,128]{2,1,0:T(8,128)(2,1)S(1)} %all-to-all-done.1.returned_ref, bf16[96,128,128]{2,1,0:T(8,128)(2,1)} %weights_hbm.3), custom_call_target="tpu_custom_call" | custom-call | tf_op jit(solution)/shard_map/back/pallas_call | solution.py:924
  (10 shorter events, 0.0 us)
Async XLA Ops:
  0.6 16.5 %copy-start = (f32[2,8,128,128]{3,2,1,0:T(8,128)S(1)}, f32[2,8,128,128]{3,2,1,0:T(8,128)}, u32[]{:S(2)}) copy-start(f32[2,8,128,128]{3,2,1,0:T(8,128)} %vel_hbm.3) | copy-start | bytes 3145732
  0.6 16.5 %copy-start.1 = (f32[7,128,128]{2,1,0:T(8,128)S(1)}, f32[7,128,128]{2,1,0:T(8,128)}, u32[]{:S(2)}) copy-start(f32[7,128,128]{2,1,0:T(8,128)} %k_hbm.3) | copy-start | bytes 1376260
  0.7 16.5 %copy-start.2 = (s32[128,128]{1,0:T(8,128)S(1)}, s32[128,128]{1,0:T(8,128)}, u32[]{:S(2)}) copy-start(s32[128,128]{1,0:T(8,128)} %land_hbm.3) | copy-start | bytes 196612
  3.9 20.4 %all-to-all-start = ((bf16[16,104,128]{2,1,0:T(8,128)(2,1)}), bf16[16,104,128]{2,1,0:T(8,128)(2,1)S(1)}, u32[]{:S(2)}, u32[]{:S(2)}) async-start(bf16[16,104,128]{2,1,0:T(8,128)(2,1)} %get-tuple-element.31), calls=%async_computation | async-start | bytes 851968 | tf_op jit(solution)/shard_map/all_to_all | solution.py:946
  13.5 8.4 %collective-permute-start = (f32[48,128]{1,0:T(8,128)S(1)}, f32[48,128]{1,0:T(8,128)S(1)}, u32[]{:S(2)}, u32[]{:S(2)}) collective-permute-start(f32[48,128]{1,0:T(8,128)S(1)} %get-tuple-element.38), channel_id=1, source_target_pairs={{0,4},{1,5},{2,6},{3,7},{4,0},{5,1},{6,2},{7,3},{8,12},{9,13},{10,... | collective-permute-start | bytes 73736 | tf_op jit(solution)/shard_map/ppermute | solution.py:265
  15.5 6.4 %collective-permute-start.1 = (f32[48,128]{1,0:T(8,128)S(1)}, f32[48,128]{1,0:T(8,128)S(1)}, u32[]{:S(2)}, u32[]{:S(2)}) collective-permute-start(f32[48,128]{1,0:T(8,128)S(1)} %get-tuple-element.39), channel_id=1, source_target_pairs={{0,1},{1,0},{2,3},{3,2},{4,8},{5,9},{6,10},{7,11},{8,4},{9,5},{10,... | collective-permute-start | bytes 73736 | tf_op jit(solution)/shard_map/ppermute | solution.py:265
  15.5 6.4 %collective-permute-start.2 = (f32[48,128]{1,0:T(8,128)S(1)}, f32[48,128]{1,0:T(8,128)S(1)}, u32[]{:S(2)}, u32[]{:S(2)}) collective-permute-start(f32[48,128]{1,0:T(8,128)S(1)} %get-tuple-element.40), channel_id=1, source_target_pairs={{0,1},{1,0},{2,3},{3,2},{4,5},{5,4},{6,7},{7,6},{8,9},{9,8},{10,11... | collective-permute-start | bytes 73736 | tf_op jit(solution)/shard_map/ppermute | solution.py:265
  16.0 5.9 %collective-permute-start.3 = (f32[48,128]{1,0:T(8,128)S(1)}, f32[48,128]{1,0:T(8,128)S(1)}, u32[]{:S(2)}, u32[]{:S(2)}) collective-permute-start(f32[48,128]{1,0:T(8,128)S(1)} %get-tuple-element.41), channel_id=1, source_target_pairs={{0,3},{1,2},{2,1},{3,0},{4,7},{5,6},{6,5},{7,4},{8,11},{9,10},{10,... | collective-permute-start | bytes 73736 | tf_op jit(solution)/shard_map/ppermute | solution.py:265
  27.6 5.0 %collective-permute-start.4 = (f32[48,128]{1,0:T(8,128)S(1)}, f32[48,128]{1,0:T(8,128)S(1)}, u32[]{:S(2)}, u32[]{:S(2)}) collective-permute-start(f32[48,128]{1,0:T(8,128)S(1)} %get-tuple-element.50), channel_id=1, source_target_pairs={{0,4},{1,5},{2,6},{3,7},{4,0},{5,1},{6,2},{7,3},{8,12},{9,13},{10,... | collective-permute-start | bytes 73736 | tf_op jit(solution)/shard_map/ppermute | solution.py:265
  29.0 3.7 %collective-permute-start.5 = (f32[48,128]{1,0:T(8,128)S(1)}, f32[48,128]{1,0:T(8,128)S(1)}, u32[]{:S(2)}, u32[]{:S(2)}) collective-permute-start(f32[48,128]{1,0:T(8,128)S(1)} %get-tuple-element.51), channel_id=1, source_target_pairs={{0,1},{1,0},{2,3},{3,2},{4,8},{5,9},{6,10},{7,11},{8,4},{9,5},{10,... | collective-permute-start | bytes 73736 | tf_op jit(solution)/shard_map/ppermute | solution.py:265
  29.0 3.7 %collective-permute-start.6 = (f32[48,128]{1,0:T(8,128)S(1)}, f32[48,128]{1,0:T(8,128)S(1)}, u32[]{:S(2)}, u32[]{:S(2)}) collective-permute-start(f32[48,128]{1,0:T(8,128)S(1)} %get-tuple-element.52), channel_id=1, source_target_pairs={{0,1},{1,0},{2,3},{3,2},{4,5},{5,4},{6,7},{7,6},{8,9},{9,8},{10,11... | collective-permute-start | bytes 73736 | tf_op jit(solution)/shard_map/ppermute | solution.py:265
  29.5 3.3 %collective-permute-start.7 = (f32[48,128]{1,0:T(8,128)S(1)}, f32[48,128]{1,0:T(8,128)S(1)}, u32[]{:S(2)}, u32[]{:S(2)}) collective-permute-start(f32[48,128]{1,0:T(8,128)S(1)} %get-tuple-element.53), channel_id=1, source_target_pairs={{0,3},{1,2},{2,1},{3,0},{4,7},{5,6},{6,5},{7,4},{8,11},{9,10},{10,... | collective-permute-start | bytes 73736 | tf_op jit(solution)/shard_map/ppermute | solution.py:265
  34.1 14.3 %all-to-all-start.1 = ((bf16[16,72,128]{2,1,0:T(8,128)(2,1)}), bf16[16,72,128]{2,1,0:T(8,128)(2,1)S(1)}, u32[]{:S(2)}, u32[]{:S(2)}) async-start(bf16[16,72,128]{2,1,0:T(8,128)(2,1)} %get-tuple-element.59), calls=%async_computation.1 | async-start | bytes 589824 | tf_op jit(solution)/shard_map/all_to_all | solution.py:946

commit v6 on v5

--- a/solution.py
+++ b/solution.py
@@ -13,7 +13,7 @@
 BF16 = jnp.bfloat16
 AXES = ("tx", "ty", "tz")
 PAD = 8
-TOP_PLANES = 6
+TOP_PLANES = 4
 CHUNKS = 4
 
 
@@ -396,8 +396,8 @@
 
 
 def first_kernel(
-    padded, vel_ref, k_ref, land_ref, q_hbm, ip_hbm, down_hbm, edge_hbm,
-    q_ref, ip_ref, down_ref, edge_ref, cols, lines, sems, *, levels,
+    padded, vel_ref, k_ref, land_ref, edge_ref, q_hbm, ip_hbm, down_hbm, edge_hbm,
+    q_ref, ip_ref, down_ref, cols, lines, sems, *, levels,
 ):
     height, width = land_ref.shape
     sea = land_ref[...].astype(F32)
@@ -467,18 +467,18 @@
     return pl.pallas_call(
         functools.partial(first_kernel, levels=levels),
         out_shape=(
+            jax.ShapeDtypeStruct(edge, F32),
             pltpu.HBM((count, height, width), F32),
             pltpu.HBM((levels, height, width), F32),
             pltpu.HBM((levels, height, width), F32),
             pltpu.HBM(edge, F32),
         ),
         in_specs=[vmem()] * 4,
-        out_specs=(hbm(),) * 4,
+        out_specs=(vmem(),) + (hbm(),) * 4,
         scratch_shapes=[
             pltpu.VMEM((count, height, width), F32),
             pltpu.VMEM((levels, height, width), F32),
             pltpu.VMEM((levels, height, width), F32),
-            pltpu.VMEM(edge, F32),
             pltpu.VMEM((height, width), F32),
             pltpu.VMEM((width, height), F32),
             pltpu.SemaphoreType.DMA((4,)),
@@ -488,6 +488,35 @@
     )(padded, velocity, mixing, land)
 
 
+def halo_kernel(edge_ref, r0, r1, r2, r3, added, sides, halos, lines, *, sizes, levels):
+    tracers = halos.shape[1] // levels
+    sort_halos(sizes, (r0, r1, r2, r3), halos)
+
+    def level_done(side, level, q, rhs):
+        value = rhs if level == 0 else q
+        added[side, pl.ds(level, tracers, stride=levels), :] = value
+
+    correct(edge_ref, halos, level_done, levels)
+    place_sides(added, lines, sides)
+
+
+def halo_part(sizes, edge, received, levels):
+    count, width = received[0].shape
+    shape = (4, count, width)
+    return pl.pallas_call(
+        functools.partial(halo_kernel, sizes=sizes, levels=levels),
+        out_shape=(
+            jax.ShapeDtypeStruct(shape, F32),
+            jax.ShapeDtypeStruct((width, width), F32),
+        ),
+        in_specs=[vmem()] * 5,
+        out_specs=(vmem(),) * 2,
+        scratch_shapes=[pltpu.VMEM(shape, F32), pltpu.VMEM((width, width), F32)],
+        compiler_params=params(2),
+        name="halo_part",
+    )(edge, *received)
+
+
 def place_sides(added, lines, sides):
     count = added.shape[1]
     lines[...] = jnp.zeros(lines.shape, F32)
@@ -497,21 +526,21 @@
 
 
 def middle_kernel(
-    incoming_ref, q_hbm, down_hbm, ip_hbm, k_hbm, land_hbm, vel_hbm, edge_hbm, r0, r1, r2, r3,
+    incoming_ref, q_hbm, down_hbm, ip_hbm, k_hbm, land_hbm, vel_hbm, edge_hbm, added, sides,
     x_ref, coef_ref, pick_ref, ip_ref, k_ref, land_ref, vel_ref, edge_ref, top_edge_ref,
     s0, s1, s2, s3, coef_hbm,
-    q_ref, down_ref, wide, flux, cols, lines, halos, added, sides, sems, *, sizes, levels, cap, window,
+    q_ref, down_ref, wide, flux, cols, lines, sems, *, sizes, levels, cap, window,
 ):
     count, height, width = q_ref.shape
     tracers = count // levels
     nodes, message_rows, _ = incoming_ref.shape
     fields = flux.shape[0]
     rows = height // CHUNKS
-    early = copies_of(
-        [(edge_hbm, edge_ref), (down_hbm, down_ref), (land_hbm, land_ref)], sems
-    )
+    early = copies_of([(down_hbm, down_ref), (land_hbm, land_ref)], sems)
     arrivals = chunk_copies(q_hbm, 0, q_ref, 0, height, sems, 6)
-    late = copies_of([(vel_hbm, vel_ref), (ip_hbm, ip_ref), (k_hbm, k_ref)], sems, 3)
+    late = copies_of(
+        [(vel_hbm, vel_ref), (ip_hbm, ip_ref), (k_hbm, k_ref), (edge_hbm, edge_ref)], sems, 2
+    )
     clear_pads(x_ref)
     span = nodes * message_rows
     wide[span:, :] = jnp.zeros((wide.shape[0] - span, width), F32)
@@ -540,14 +569,6 @@
         flux[f] = jnp.dot(selector, stacked, preferred_element_type=F32)
     for copy in early:
         copy.wait()
-    sort_halos(sizes, (r0, r1, r2, r3), halos)
-
-    def level_done(side, level, q, rhs):
-        value = rhs if level == 0 else q
-        added[side, pl.ds(level, tracers, stride=levels), :] = value
-
-    correct(edge_ref, halos, level_done, levels)
-    place_sides(added, lines, sides)
     sea = land_ref[...].astype(F32)
     stirring = 1.0 + 0.5 * (
         flux[fields - 2] * flux[fields - 2] + flux[fields - 1] * flux[fields - 1]
@@ -616,7 +637,7 @@
         copy.wait()
 
 
-def middle_part(sizes, incoming, q, down, ip, mixing, land, velocity, edge, received, fields, levels, cap, window):
+def middle_part(sizes, incoming, q, down, ip, mixing, land, velocity, edge, added, sides, fields, levels, cap, window):
     count, height, width = q.shape
     nodes, message_rows, _ = incoming.shape
     tracers = count // levels
@@ -634,7 +655,7 @@
             line, line, line, line,
             pltpu.HBM((tracers + 3, height, width), F32),
         ),
-        in_specs=[vmem()] + [hbm()] * 7 + [vmem()] * 4,
+        in_specs=[vmem()] + [hbm()] * 7 + [vmem()] * 2,
         out_specs=(vmem(),) * 13 + (hbm(),),
         scratch_shapes=[
             pltpu.VMEM(q.shape, F32),
@@ -643,14 +664,11 @@
             pltpu.VMEM((fields, height, width), F32),
             pltpu.VMEM((height, width), F32),
             pltpu.VMEM((width, height), F32),
-            pltpu.VMEM((4, count, width), F32),
-            pltpu.VMEM((4, count, width), F32),
-            pltpu.VMEM((height, width), F32),
             pltpu.SemaphoreType.DMA((7 + CHUNKS,)),
         ],
         compiler_params=params(10),
         name="middle_part",
-    )(incoming, *pin(q, down, ip, mixing, land, velocity, edge), *received)
+    )(incoming, *pin(q, down, ip, mixing, land, velocity, edge), added, sides)
 
 
 def top_level(coef_ref, here, t, tracers, q1, rhs):
@@ -775,8 +793,8 @@
 
 
 def last_kernel(
-    padded_hbm, halo_hbm, vel_hbm, k_hbm, land_hbm, ip_hbm, coef_hbm,
-    out_hbm, padded, halos, lines, sides, vel_ref, k_ref, land_ref, ip_ref, coef_ref, out_ref,
+    padded_hbm, halo_hbm, vel_hbm, k_hbm, land_hbm, ip_hbm, coef_hbm, weights_hbm,
+    out_hbm, near_ref, padded, halos, lines, sides, vel_ref, k_ref, land_ref, ip_ref, coef_ref, out_ref,
     sems, *, levels,
 ):
     count, height, width = out_ref.shape
@@ -790,6 +808,12 @@
         sems,
     )
     arrivals = chunk_copies(padded_hbm, PAD, padded, PAD, height, sems, len(early))
+    near = near_ref.shape[0]
+    kept = copies_of(
+        [(weights_hbm.at[pl.ds(weights_hbm.shape[0] - near, near)], near_ref)],
+        sems,
+        len(early) + CHUNKS,
+    )
     early[0].wait()
     place_sides(halos, lines, sides)
     for copy in early[1:]:
@@ -828,18 +852,21 @@
                     out_ref[t * levels + lower, here, :] = x
 
     sweep(padded, vel_ref, k_ref, land_ref, ip_ref, sides, finish, levels, wait, done)
-    for copy in outs:
+    for copy in outs + kept:
         copy.wait()
 
 
-def last_part(padded, halos, velocity, mixing, land, ip, coef, levels):
+def last_part(padded, halos, velocity, mixing, land, ip, coef, weights, levels):
     count, height, width = padded.shape
     height -= 2 * PAD
     return pl.pallas_call(
         functools.partial(last_kernel, levels=levels),
-        out_shape=pltpu.HBM((count, height, width), F32),
-        in_specs=[hbm()] * 7,
-        out_specs=hbm(),
+        out_shape=(
+            pltpu.HBM((count, height, width), F32),
+            jax.ShapeDtypeStruct((weights.shape[0] // 2,) + weights.shape[1:], BF16),
+        ),
+        in_specs=[hbm()] * 8,
+        out_specs=(hbm(), vmem()),
         scratch_shapes=[
             pltpu.VMEM(padded.shape, F32),
             pltpu.VMEM(halos.shape, F32),
@@ -851,22 +878,23 @@
             pltpu.VMEM(ip.shape, F32),
             pltpu.VMEM(coef.shape, F32),
             pltpu.VMEM((count, height, width), F32),
-            pltpu.SemaphoreType.DMA((6 + CHUNKS,)),
+            pltpu.SemaphoreType.DMA((7 + CHUNKS,)),
         ],
         compiler_params=params(16),
         name="last_part",
-    )(*pin(padded, halos, velocity, mixing, land, ip, coef))
+    )(*pin(padded, halos, velocity, mixing, land, ip, coef, weights))
 
 
 def back_kernel(
-    slot_hbm, atm_hbm, rows_hbm, returned_ref, weights_hbm, out_hbm,
+    slot_hbm, atm_hbm, rows_hbm, returned_ref, weights_hbm, near_ref, out_hbm,
     slot_ref, atm_ref, rows_ref, weights_ref, out_ref, wide, total, sems,
     *, tracers, cells,
 ):
     nodes, per, width = returned_ref.shape
-    pairs = weights_ref.shape[0]
+    far = weights_ref.shape[0]
+    pairs = far + near_ref.shape[0]
     blocks = out_ref.shape[1]
-    bounds = weight_parts(pairs)
+    bounds = weight_parts(far)
     copies = copies_of(
         [(slot_hbm, slot_ref), (atm_hbm, atm_ref), (rows_hbm, rows_ref)], sems
     )
@@ -887,13 +915,14 @@
         wide[n * per : (n + 1) * per, :] = returned_ref[n].astype(F32)
     for copy in copies:
         copy.wait()
-    for p in range(0, pairs, 2):
-        if p in bounds:
+    for p in list(range(far, pairs, 2)) + list(range(0, far, 2)):
+        if p in bounds[:-1]:
             parts[bounds.index(p)].wait()
         lhs = jnp.concatenate(
             [wide[pl.ds(slot_ref[p + k] * tracers, 8), :] for k in range(2)], axis=0
         )
-        rhs = jnp.concatenate([weights_ref[p], weights_ref[p + 1]], axis=0)
+        source, at = (weights_ref, p) if p < far else (near_ref, p - far)
+        rhs = jnp.concatenate([source[at], source[at + 1]], axis=0)
         both = lax.dot_general(
             lhs.astype(BF16), rhs, (((1,), (1,)), ((), ())), preferred_element_type=F32
         )
@@ -916,7 +945,7 @@
         copy.wait()
 
 
-def back(slots, atm, rows, returned, weights, tracers):
+def back(slots, atm, rows, returned, weights, near, tracers):
     pairs, cells, width = weights.shape
     nodes, per, _ = returned.shape
     blocks = rows.shape[0]
@@ -924,13 +953,13 @@
     by_tracer = pl.pallas_call(
         functools.partial(back_kernel, tracers=tracers, cells=cells),
         out_shape=pltpu.HBM((tracers, blocks, cells), F32),
-        in_specs=[hbm()] * 3 + [vmem(), hbm()],
+        in_specs=[hbm()] * 3 + [vmem(), hbm(), vmem()],
         out_specs=hbm(),
         scratch_shapes=[
             pltpu.SMEM((pairs,), ints),
             pltpu.SMEM((pairs,), ints),
             pltpu.SMEM((blocks,), ints),
-            pltpu.VMEM(weights.shape, BF16),
+            pltpu.VMEM((pairs - near.shape[0], cells, width), BF16),
             pltpu.VMEM((tracers, blocks, cells), F32),
             pltpu.VMEM((nodes * per + 8, width), F32),
             pltpu.VMEM((blocks * 8, cells), F32),
@@ -938,7 +967,7 @@
         ],
         compiler_params=params(8),
         name="back",
-    )(*pin(slots, atm, rows), returned, *pin(weights))
+    )(*pin(slots, atm, rows), returned, *pin(weights), near)
     return by_tracer.transpose(1, 0, 2)
 
 
@@ -976,13 +1005,14 @@
     incoming = all_to_all(message)
     padded, *lines = edges(mesh_sizes, slots, state)
     received = exchange(lines, mesh_sizes)
-    q, ip, down, edge_far = first_part(padded, velocity, mixing, land, levels)
+    edge, q, ip, down, edge_far = first_part(padded, velocity, mixing, land, levels)
+    added, sides = halo_part(mesh_sizes, edge, received, levels)
     (
         padded, coef, pick, ip_near, mixing_near, land_near, velocity_near, edge, top_edge,
         *lines, coef_far,
     ) = middle_part(
-        mesh_sizes, incoming, q, down, ip, mixing, land, velocity, edge_far, received, fields, levels, cap,
-        window,
+        mesh_sizes, incoming, q, down, ip, mixing, land, velocity, edge_far, added, sides, fields, levels,
+        cap, window,
     )
     received = exchange(lines, mesh_sizes)
     top, state = inner_part(padded, velocity_near, mixing_near, land_near, ip_near, coef, levels)
@@ -990,8 +1020,10 @@
         mesh_sizes, top, received, edge, top_edge, land_near, pick, nodes, levels, cap, window
     )
     returned = all_to_all(answer)
-    out = last_part(state, halos, velocity, mixing, land, ip, coef_far, levels)
-    atm_surface = back(slots, pair_atm, atm_rows, returned, regrid_weights, tracer_count)
+    out, near = last_part(
+        state, halos, velocity, mixing, land, ip, coef_far, regrid_weights, levels
+    )
+    atm_surface = back(slots, pair_atm, atm_rows, returned, regrid_weights, near, tracer_count)
     return (out.reshape(tracers.shape), atm_surface)
 
 

time: 52 us -> 51.7 us (level)
    pallas_call x1 -> x2, Pallas kernels: 5.77 us -> 5.93 us  [the longest x1 5.75 us: last_part(): pl.pallas_call(functools.partial(last_kernel, levels=levels), out_shape=(...]
where the time goes in v6:
time: 51.7 us; the launch traced here: 51.3 us
  Pallas kernels  25.6 us (50%)
  starting transfers between devices  17.8 us (34%)
  waiting for transfers between devices  7.15 us (14%)
  between operations  0.8 us (2%)
    all_to_all x2, starting transfers between devices, all_to_all(): return lax.all_to_all(x, AXES, split_axis=0, concat_axis=0, tiled=True)  11.1 us
    all_to_all x2, waiting for transfers between devices, all_to_all(): return lax.all_to_all(x, AXES, split_axis=0, concat_axis=0, tiled=True)  6.97 us
    ppermute x8, starting transfers between devices, exchange(): return [lax.ppermute(line, AXES, perm) for line, perm in zip(lines, perms)]  6.68 us
    pallas_call x1, Pallas kernels, last_part(): pl.pallas_call(functools.partial(last_kernel, levels=levels), out_shape=(...  5.75 us
    pallas_call x1, Pallas kernels, first_part(): pl.pallas_call(functools.partial(first_kernel, levels=levels), out_shape=...  4.75 us
    pallas_call x1, Pallas kernels, contributions(): pl.pallas_call(functools.partial(contrib_kernel, sizes=sizes, nodes=nodes...  3.22 us
    pallas_call x1, Pallas kernels, middle_part(): pl.pallas_call(functools.partial(middle_kernel, sizes=sizes, levels=level...  3.19 us
    pallas_call x1, Pallas kernels, back(): pl.pallas_call(functools.partial(back_kernel, tracers=tracers, cells=cell...  2.93 us
  transfers between devices with their start and end apart: 10, of which 3 were waited for; matrix products, arithmetic and copies ran while one was open for 0% of the time, Pallas kernels for 29%

profile of v6, /device:TPU:0, one launch (start us, length us, event | category | flops | bytes accessed | tf_op | source)
XLA Modules:
  0.0 51.3 jit_solution(2587066508087449064)
XLA Ops:
  0.6 0.0 copy-start
  0.6 0.0 copy-start.1
  0.7 0.0 copy-start.2
  0.7 3.2 %contributions.1 = (bf16[16,104,128]{2,1,0:T(8,128)(2,1)}, s32[96]{0:T(128)}) custom-call(s32[96]{0:T(128)} %bitcast.6, s32[96]{0:T(128)} %atm_hbm.3, s32[96]{0:T(128)} %row_hbm.1, s32[48]{0:T(128)} %rows_hbm.3, bf16[48,8,128]{2,1,0:T(8,128)(2,1)} %flux_hbm.1, bf16[96,128,128]{2,1,0:T(8,128)(2,1)} %weights_hbm.5), custom_call_target="tpu_custom_call" | custom-call | tf_op jit(solution)/shard_map/contributions/pallas_call | solution.py:178
  3.9 7.4 %all-to-all-start = ((bf16[16,104,128]{2,1,0:T(8,128)(2,1)}), bf16[16,104,128]{2,1,0:T(8,128)(2,1)S(1)}, u32[]{:S(2)}, u32[]{:S(2)}) async-start(bf16[16,104,128]{2,1,0:T(8,128)(2,1)} %get-tuple-element.36), calls=%async_computation | async-start | bytes 851968 | tf_op jit(solution)/shard_map/all_to_all | solution.py:975
  11.3 2.3 %edges.1 = (f32[48,144,128]{2,1,0:T(8,128)S(1)}, f32[48,128]{1,0:T(8,128)S(1)}, f32[48,128]{1,0:T(8,128)S(1)}, f32[48,128]{1,0:T(8,128)S(1)}, f32[48,128]{1,0:T(8,128)S(1)}) custom-call(s32[96]{0:T(128)} %get-tuple-element.37.order.slot_hbm, f32[48,128,128]{2,1,0:T(8,128)} %bitcast.4), custom_call_target="tpu_custom_call" | custom-call | tf_op jit(solution)/shard_map/edges/pallas_call | solution.py:304
  13.5 2.0 %collective-permute-start = (f32[48,128]{1,0:T(8,128)S(1)}, f32[48,128]{1,0:T(8,128)S(1)}, u32[]{:S(2)}, u32[]{:S(2)}) collective-permute-start(f32[48,128]{1,0:T(8,128)S(1)} %get-tuple-element.44), channel_id=1, source_target_pairs={{0,4},{1,5},{2,6},{3,7},{4,0},{5,1},{6,2},{7,3},{8,12},{9,13},{10,... | collective-permute-start | bytes 73736 | tf_op jit(solution)/shard_map/ppermute | solution.py:265
  15.5 0.5 collective-permute-start.2
  16.0 1.1 %collective-permute-start.3 = (f32[48,128]{1,0:T(8,128)S(1)}, f32[48,128]{1,0:T(8,128)S(1)}, u32[]{:S(2)}, u32[]{:S(2)}) collective-permute-start(f32[48,128]{1,0:T(8,128)S(1)} %get-tuple-element.47), channel_id=1, source_target_pairs={{0,3},{1,2},{2,1},{3,0},{4,7},{5,6},{6,5},{7,4},{8,11},{9,10},{10,... | collective-permute-start | bytes 73736 | tf_op jit(solution)/shard_map/ppermute | solution.py:265
  17.1 4.7 %first_part.1 = (f32[4,3,8,128]{3,2,1,0:T(8,128)S(1)}, f32[48,128,128]{2,1,0:T(8,128)}, f32[8,128,128]{2,1,0:T(8,128)}, f32[8,128,128]{2,1,0:T(8,128)}, f32[4,3,8,128]{3,2,1,0:T(8,128)}) custom-call(f32[48,144,128]{2,1,0:T(8,128)S(1)} %get-tuple-element.38.padded, f32[2,8,128,128]{3,2,1,0:T(8,128)S(1)} %copy-done, f32[7,128,128]{2,1,0:T(8,128)S(1)} %copy-done.1, ...), custom_call_target="tpu_custom_call" | custom-call | tf_op jit(solution)/shard_map/first_part/pallas_call | solution.py:467
  21.9 0.0 collective-permute-done.1.r1
  21.9 0.2 halo_part.1
  22.1 2.2 %all-to-all-done.incoming_ref = bf16[16,104,128]{2,1,0:T(8,128)(2,1)S(1)} async-done(((bf16[16,104,128]{2,1,0:T(8,128)(2,1)}), bf16[16,104,128]{2,1,0:T(8,128)(2,1)S(1)}, u32[]{:S(2)}, u32[]{:S(2)}) %all-to-all-start) | async-done | bytes 426016 | tf_op jit(solution)/shard_map/all_to_all | solution.py:975
  24.3 3.2 %middle_part.1 = (f32[48,144,128]{2,1,0:T(8,128)S(1)}, f32[9,128,128]{2,1,0:T(8,128)S(1)}, bf16[256,128]{1,0:T(8,128)(2,1)S(1)}, f32[8,128,128]{2,1,0:T(8,128)S(...) custom-call(bf16[16,104,128]{2,1,0:T(8,128)(2,1)S(1)} %all-to-all-do, ...), custom_call_target="tpu_custom_call" | custom-call | tf_op jit(solution)/shard_map/middle_part/pallas_call | solution.py:647
  27.5 1.5 %collective-permute-start.4 = (f32[48,128]{1,0:T(8,128)S(1)}, f32[48,128]{1,0:T(8,128)S(1)}, u32[]{:S(2)}, u32[]{:S(2)}) collective-permute-start(f32[48,128]{1,0:T(8,128)S(1)} %get-tuple-element.58), channel_id=1, source_target_pairs={{0,4},{1,5},{2,6},{3,7},{4,0},{5,1},{6,2},{7,3},{8,12},{9,13},{10,... | collective-permute-start | bytes 73736 | tf_op jit(solution)/shard_map/ppermute | solution.py:265
  29.0 0.5 collective-permute-start.6
  29.5 1.1 %collective-permute-start.7 = (f32[48,128]{1,0:T(8,128)S(1)}, f32[48,128]{1,0:T(8,128)S(1)}, u32[]{:S(2)}, u32[]{:S(2)}) collective-permute-start(f32[48,128]{1,0:T(8,128)S(1)} %get-tuple-element.61), channel_id=1, source_target_pairs={{0,3},{1,2},{2,1},{3,0},{4,7},{5,6},{6,5},{7,4},{8,11},{9,10},{10,... | collective-permute-start | bytes 73736 | tf_op jit(solution)/shard_map/ppermute | solution.py:265
  30.6 2.1 %inner_part.1 = (f32[6,128,128]{2,1,0:T(8,128)S(1)}, f32[48,144,128]{2,1,0:T(8,128)}) custom-call(f32[48,144,128]{2,1,0:T(8,128)S(1)} %get-tuple-element.50.padded, f32[2,8,128,128]{3,2,1,0:T(8,128)S(1)} %get-tuple-element.51.vel_ref, f32[7,128,128]{2,1,0:T(8,128)S(1)} %get-tuple-element.52.k_ref, s32[128,128]{1,0:T(8,128)S(1)} %get-tuple-element.53.land_ref, ...), custom_call_target="tpu_custom_call" | custom-call | tf_op jit(solution)/shard_map/inner_part/pallas_call | solution.py:702
  32.7 0.2 collective-permute-done.7.r3
  32.8 1.2 %replies.1 = (f32[6,128,128]{2,1,0:T(8,128)S(1)}, f32[4,48,128]{2,1,0:T(8,128)}, bf16[16,72,128]{2,1,0:T(8,128)(2,1)}) custom-call(f32[6,128,128]{2,1,0:T(8,128)S(1)} %get-tuple-element.57.top_in, f32[48,128]{1,0:T(8,128)S(1)} %collective-permute-done.4.r0, f32[48,128]{1,0:T(8,128)S(1)} %collective-permute-done.5.r1, ...), custom_call_target="tpu_custom_call", output_to_operand_aliasing={{0}: (0, {})} | custom-call | tf_op jit(solution)/shard_map/replies/pallas_call | solution.py:771
  34.1 3.8 %all-to-all-start.1 = ((bf16[16,72,128]{2,1,0:T(8,128)(2,1)}), bf16[16,72,128]{2,1,0:T(8,128)(2,1)S(1)}, u32[]{:S(2)}, u32[]{:S(2)}) async-start(bf16[16,72,128]{2,1,0:T(8,128)(2,1)} %get-tuple-element.68), calls=%async_computation.1 | async-start | bytes 589824 | tf_op jit(solution)/shard_map/all_to_all | solution.py:975
  37.8 5.8 %last_part.1 = (f32[48,128,128]{2,1,0:T(8,128)}, bf16[48,128,128]{2,1,0:T(8,128)(2,1)S(1)}) custom-call(f32[48,144,128]{2,1,0:T(8,128)} %get-tuple-element.56.padded_hbm, f32[4,48,128]{2,1,0:T(8,128)} %get-tuple-element.65.halo_hbm, f32[2,8,128,128]{3,2,1,0:T(8,128)} %vel_hbm.3, f32[7,128,128]{2,1,0:T(8,128)} %k_hbm.3, s32[128,128]{1,0:T(8,128)} %land_hbm.3, ...), custom_call_target="tpu_custom_call" | custom-call | tf_op jit(solution)/shard_map/last_part/pallas_call | solution.py:862
  43.6 4.8 %all-to-all-done.1.returned_ref = bf16[16,72,128]{2,1,0:T(8,128)(2,1)S(1)} async-done(((bf16[16,72,128]{2,1,0:T(8,128)(2,1)}), bf16[16,72,128]{2,1,0:T(8,128)(2,1)S(1)}, u32[]{:S(2)}, u32[]{:S(2)}) %all-to-all-start.1) | async-done | bytes 294944 | tf_op jit(solution)/shard_map/all_to_all | solution.py:975
  48.4 2.9 %back.1 = f32[6,48,128]{2,1,0:T(8,128)} custom-call(s32[96]{0:T(128)} %get-tuple-element.37.order.slot_hbm, s32[96]{0:T(128)} %atm_hbm.3, s32[48]{0:T(128)} %rows_hbm.3, bf16[16,72,128]{2,1,0:T(8,128)(2,1)S(1)} %all-to-all-done.1.returned_ref, bf16[96,128,128]{2,1,0:T(8,128)(2,1)} %weights_hbm.5, bf16[48,128,128]{2,1,0:T(8,128)(2,1)S(1)} %get-tuple-element.69.near_ref), custom_call_target="tpu_custom_call" | custom-call | tf_op jit(solution)/shard_map/back/pallas_call | solution.py:953
  (11 shorter events, 0.0 us)
Async XLA Ops:
  0.6 16.5 %copy-start = (f32[2,8,128,128]{3,2,1,0:T(8,128)S(1)}, f32[2,8,128,128]{3,2,1,0:T(8,128)}, u32[]{:S(2)}) copy-start(f32[2,8,128,128]{3,2,1,0:T(8,128)} %vel_hbm.3) | copy-start | bytes 3145732
  0.6 16.5 %copy-start.1 = (f32[7,128,128]{2,1,0:T(8,128)S(1)}, f32[7,128,128]{2,1,0:T(8,128)}, u32[]{:S(2)}) copy-start(f32[7,128,128]{2,1,0:T(8,128)} %k_hbm.3) | copy-start | bytes 1376260
  0.7 16.5 %copy-start.2 = (s32[128,128]{1,0:T(8,128)S(1)}, s32[128,128]{1,0:T(8,128)}, u32[]{:S(2)}) copy-start(s32[128,128]{1,0:T(8,128)} %land_hbm.3) | copy-start | bytes 196612
  3.9 20.4 %all-to-all-start = ((bf16[16,104,128]{2,1,0:T(8,128)(2,1)}), bf16[16,104,128]{2,1,0:T(8,128)(2,1)S(1)}, u32[]{:S(2)}, u32[]{:S(2)}) async-start(bf16[16,104,128]{2,1,0:T(8,128)(2,1)} %get-tuple-element.36), calls=%async_computation | async-start | bytes 851968 | tf_op jit(solution)/shard_map/all_to_all | solution.py:975
  13.5 8.3 %collective-permute-start = (f32[48,128]{1,0:T(8,128)S(1)}, f32[48,128]{1,0:T(8,128)S(1)}, u32[]{:S(2)}, u32[]{:S(2)}) collective-permute-start(f32[48,128]{1,0:T(8,128)S(1)} %get-tuple-element.44), channel_id=1, source_target_pairs={{0,4},{1,5},{2,6},{3,7},{4,0},{5,1},{6,2},{7,3},{8,12},{9,13},{10,... | collective-permute-start | bytes 73736 | tf_op jit(solution)/shard_map/ppermute | solution.py:265
  15.5 6.4 %collective-permute-start.1 = (f32[48,128]{1,0:T(8,128)S(1)}, f32[48,128]{1,0:T(8,128)S(1)}, u32[]{:S(2)}, u32[]{:S(2)}) collective-permute-start(f32[48,128]{1,0:T(8,128)S(1)} %get-tuple-element.45), channel_id=1, source_target_pairs={{0,1},{1,0},{2,3},{3,2},{4,8},{5,9},{6,10},{7,11},{8,4},{9,5},{10,... | collective-permute-start | bytes 73736 | tf_op jit(solution)/shard_map/ppermute | solution.py:265
  15.5 6.4 %collective-permute-start.2 = (f32[48,128]{1,0:T(8,128)S(1)}, f32[48,128]{1,0:T(8,128)S(1)}, u32[]{:S(2)}, u32[]{:S(2)}) collective-permute-start(f32[48,128]{1,0:T(8,128)S(1)} %get-tuple-element.46), channel_id=1, source_target_pairs={{0,1},{1,0},{2,3},{3,2},{4,5},{5,4},{6,7},{7,6},{8,9},{9,8},{10,11... | collective-permute-start | bytes 73736 | tf_op jit(solution)/shard_map/ppermute | solution.py:265
  16.0 5.9 %collective-permute-start.3 = (f32[48,128]{1,0:T(8,128)S(1)}, f32[48,128]{1,0:T(8,128)S(1)}, u32[]{:S(2)}, u32[]{:S(2)}) collective-permute-start(f32[48,128]{1,0:T(8,128)S(1)} %get-tuple-element.47), channel_id=1, source_target_pairs={{0,3},{1,2},{2,1},{3,0},{4,7},{5,6},{6,5},{7,4},{8,11},{9,10},{10,... | collective-permute-start | bytes 73736 | tf_op jit(solution)/shard_map/ppermute | solution.py:265
  27.5 5.2 %collective-permute-start.4 = (f32[48,128]{1,0:T(8,128)S(1)}, f32[48,128]{1,0:T(8,128)S(1)}, u32[]{:S(2)}, u32[]{:S(2)}) collective-permute-start(f32[48,128]{1,0:T(8,128)S(1)} %get-tuple-element.58), channel_id=1, source_target_pairs={{0,4},{1,5},{2,6},{3,7},{4,0},{5,1},{6,2},{7,3},{8,12},{9,13},{10,... | collective-permute-start | bytes 73736 | tf_op jit(solution)/shard_map/ppermute | solution.py:265
  29.0 3.7 %collective-permute-start.5 = (f32[48,128]{1,0:T(8,128)S(1)}, f32[48,128]{1,0:T(8,128)S(1)}, u32[]{:S(2)}, u32[]{:S(2)}) collective-permute-start(f32[48,128]{1,0:T(8,128)S(1)} %get-tuple-element.59), channel_id=1, source_target_pairs={{0,1},{1,0},{2,3},{3,2},{4,8},{5,9},{6,10},{7,11},{8,4},{9,5},{10,... | collective-permute-start | bytes 73736 | tf_op jit(solution)/shard_map/ppermute | solution.py:265
  29.0 3.7 %collective-permute-start.6 = (f32[48,128]{1,0:T(8,128)S(1)}, f32[48,128]{1,0:T(8,128)S(1)}, u32[]{:S(2)}, u32[]{:S(2)}) collective-permute-start(f32[48,128]{1,0:T(8,128)S(1)} %get-tuple-element.60), channel_id=1, source_target_pairs={{0,1},{1,0},{2,3},{3,2},{4,5},{5,4},{6,7},{7,6},{8,9},{9,8},{10,11... | collective-permute-start | bytes 73736 | tf_op jit(solution)/shard_map/ppermute | solution.py:265
  29.5 3.3 %collective-permute-start.7 = (f32[48,128]{1,0:T(8,128)S(1)}, f32[48,128]{1,0:T(8,128)S(1)}, u32[]{:S(2)}, u32[]{:S(2)}) collective-permute-start(f32[48,128]{1,0:T(8,128)S(1)} %get-tuple-element.61), channel_id=1, source_target_pairs={{0,3},{1,2},{2,1},{3,0},{4,7},{5,6},{6,5},{7,4},{8,11},{9,10},{10,... | collective-permute-start | bytes 73736 | tf_op jit(solution)/shard_map/ppermute | solution.py:265
  34.1 14.3 %all-to-all-start.1 = ((bf16[16,72,128]{2,1,0:T(8,128)(2,1)}), bf16[16,72,128]{2,1,0:T(8,128)(2,1)S(1)}, u32[]{:S(2)}, u32[]{:S(2)}) async-start(bf16[16,72,128]{2,1,0:T(8,128)(2,1)} %get-tuple-element.68), calls=%async_computation.1 | async-start | bytes 589824 | tf_op jit(solution)/shard_map/all_to_all | solution.py:975

commit v7 on v6

--- a/solution.py
+++ b/solution.py
@@ -15,6 +15,7 @@
 PAD = 8
 TOP_PLANES = 4
 CHUNKS = 4
+PRODUCTS = 2
 
 
 def vmem():
@@ -228,15 +229,15 @@
     g_even = lax.rem(group, 2) == 0
     sends[0][...] = jnp.where(tx_even, east, west)
     sends[1][...] = jnp.where(tx_even, west, east)
-    sends[2][...] = jnp.where(g_even, row_last, row_first)
-    sends[3][...] = jnp.where(g_even, row_first, row_last)
+    sends[3][...] = jnp.where(g_even, row_last, row_first)
+    sends[2][...] = jnp.where(g_even, row_first, row_last)
 
 
 def sort_halos(sizes, received, halos):
     tx, group, groups = place_of(sizes)
     tx_even = lax.rem(tx, 2) == 0
     g_even = lax.rem(group, 2) == 0
-    r0, r1, r2, r3 = (r[...] for r in received)
+    r0, r1, r3, r2 = (r[...] for r in received)
     zero = jnp.zeros(r0.shape, F32)
     r1 = jnp.where((tx == 0) | (tx == sizes[0] - 1), zero, r1)
     r3 = jnp.where((group == 0) | (group == groups - 1), zero, r3)
@@ -259,9 +260,9 @@
                 perms[1].append((here, inner_x * groups + g))
             else:
                 perms[1].append((here, x * groups + (g ^ 1)))
-            perms[2].append((here, x * groups + (g ^ 1)))
+            perms[3].append((here, x * groups + (g ^ 1)))
             inner_g = g + 1 if g % 2 == 1 else g - 1
-            perms[3].append((here, x * groups + inner_g % groups))
+            perms[2].append((here, x * groups + inner_g % groups))
     return [lax.ppermute(line, AXES, perm) for line, perm in zip(lines, perms)]
 
 
@@ -316,13 +317,30 @@
     )(*pin(order, state))
 
 
-def sweep(padded, vel_ref, k_ref, land_ref, ip_ref, sides, finish, levels, wait=None, done=None):
+def shift_matrix(width):
+    k = lax.broadcasted_iota(jnp.int32, (2 * width, 2 * width), 0) % width
+    n = lax.broadcasted_iota(jnp.int32, (2 * width, 2 * width), 1)
+    source = jnp.where(n < width, n + 1, n - width - 1)
+    return jnp.where(k == source, 1.0, 0.0).astype(BF16)
+
+
+def neighbours(tiles, matrix):
+    high = tiles.astype(BF16)
+    low = (tiles - high.astype(F32)).astype(BF16)
+    return jnp.dot(
+        jnp.concatenate([high, low], axis=1), matrix, preferred_element_type=F32
+    )
+
+
+def sweep(padded, vel_ref, k_ref, land_ref, ip_ref, sides, finish, levels, wait=None, done=None, matrix=None, products=0):
     count, padded_height, width = padded.shape
     height = padded_height - 2 * PAD
     tracers = count // levels
     chunks = 1 if wait is None and done is None else CHUNKS
     rows = height // chunks
     lane = lane_iota((16, width))
+    if products:
+        matrix[...] = shift_matrix(width)
     for chunk in range(chunks):
         if wait is not None:
             wait(chunk)
@@ -336,6 +354,10 @@
             diffuse = DIFFUSION * sea
             c_here = 1.0 - 4.0 * diffuse
             q = [None] * tracers
+            moved = {}
+            for t in range(tracers - products, tracers):
+                tiles = padded[t * levels : (t + 1) * levels, pl.ds(PAD + r, 16), :]
+                moved[t] = neighbours(tiles.reshape(levels * 16, width), matrix[...])
             for level in range(levels - 1, -1, -1):
                 half_u = 0.5 * sea * vel_ref[0, level, pl.ds(r, 16), :]
                 half_v = 0.5 * sea * vel_ref[1, level, pl.ds(r, 16), :]
@@ -356,8 +378,12 @@
                     c = padded[tl, pl.ds(PAD + r, 16), :]
                     north = padded[tl, pl.ds(PAD + r + 1, 16), :]
                     south = padded[tl, pl.ds(PAD + r - 1, 16), :]
-                    east = pltpu.roll(c, width - 1, 1)
-                    west = pltpu.roll(c, 1, 1)
+                    if t in moved:
+                        here = moved[t][level * 16 : (level + 1) * 16]
+                        east, west = here[:, :width], here[:, width:]
+                    else:
+                        east = pltpu.roll(c, width - 1, 1)
+                        west = pltpu.roll(c, 1, 1)
                     rhs = c_here * c + (c_east * east + c_west * west)
                     rhs = rhs + (c_north * north + c_south * south)
                     if sides is not None:
@@ -664,7 +690,7 @@
             pltpu.VMEM((fields, height, width), F32),
             pltpu.VMEM((height, width), F32),
             pltpu.VMEM((width, height), F32),
-            pltpu.SemaphoreType.DMA((7 + CHUNKS,)),
+            pltpu.SemaphoreType.DMA((10 + CHUNKS,)),
         ],
         compiler_params=params(10),
         name="middle_part",
@@ -680,7 +706,7 @@
 
 
 def inner_kernel(
-    padded, vel_ref, k_ref, land_ref, ip_ref, coef_ref, top_ref, state_hbm, sems, *, levels
+    padded, vel_ref, k_ref, land_ref, ip_ref, coef_ref, top_ref, state_hbm, matrix, sems, *, levels
 ):
     tracers = top_ref.shape[0]
     kept = copies_of([(padded, state_hbm)], sems)
@@ -692,7 +718,10 @@
                 _, x = top_level(coef_ref, here, t, tracers, q[t], tops[t])
                 top_ref[t, here, :] = x
 
-    sweep(padded, vel_ref, k_ref, land_ref, ip_ref, None, finish, levels)
+    sweep(
+        padded, vel_ref, k_ref, land_ref, ip_ref, None, finish, levels,
+        matrix=matrix, products=PRODUCTS,
+    )
     kept[0].wait()
 
 
@@ -707,7 +736,10 @@
         ),
         in_specs=[vmem()] * 6,
         out_specs=(vmem(), hbm()),
-        scratch_shapes=[pltpu.SemaphoreType.DMA((1,))],
+        scratch_shapes=[
+            pltpu.VMEM((2 * width, 2 * width), BF16),
+            pltpu.SemaphoreType.DMA((1,)),
+        ],
         compiler_params=params(4),
         name="inner_part",
     )(padded, velocity, mixing, land, ip, coef)
@@ -794,7 +826,7 @@
 
 def last_kernel(
     padded_hbm, halo_hbm, vel_hbm, k_hbm, land_hbm, ip_hbm, coef_hbm, weights_hbm,
-    out_hbm, near_ref, padded, halos, lines, sides, vel_ref, k_ref, land_ref, ip_ref, coef_ref, out_ref,
+    slot_hbm, atm_hbm, rows_hbm, out_hbm, near_ref, slot_ref, atm_ref, rows_ref, padded, halos, lines, sides, vel_ref, k_ref, land_ref, ip_ref, coef_ref, out_ref,
     sems, *, levels,
 ):
     count, height, width = out_ref.shape
@@ -810,7 +842,10 @@
     arrivals = chunk_copies(padded_hbm, PAD, padded, PAD, height, sems, len(early))
     near = near_ref.shape[0]
     kept = copies_of(
-        [(weights_hbm.at[pl.ds(weights_hbm.shape[0] - near, near)], near_ref)],
+        [
+            (weights_hbm.at[pl.ds(weights_hbm.shape[0] - near, near)], near_ref),
+            (slot_hbm, slot_ref), (atm_hbm, atm_ref), (rows_hbm, rows_ref),
+        ],
         sems,
         len(early) + CHUNKS,
     )
@@ -856,7 +891,7 @@
         copy.wait()
 
 
-def last_part(padded, halos, velocity, mixing, land, ip, coef, weights, levels):
+def last_part(padded, halos, velocity, mixing, land, ip, coef, weights, indices, levels):
     count, height, width = padded.shape
     height -= 2 * PAD
     return pl.pallas_call(
@@ -864,9 +899,10 @@
         out_shape=(
             pltpu.HBM((count, height, width), F32),
             jax.ShapeDtypeStruct((weights.shape[0] // 2,) + weights.shape[1:], BF16),
+            *[jax.ShapeDtypeStruct(x.shape, x.dtype) for x in indices],
         ),
-        in_specs=[hbm()] * 8,
-        out_specs=(hbm(), vmem()),
+        in_specs=[hbm()] * 11,
+        out_specs=(hbm(),) + (vmem(),) * 4,
         scratch_shapes=[
             pltpu.VMEM(padded.shape, F32),
             pltpu.VMEM(halos.shape, F32),
@@ -878,11 +914,11 @@
             pltpu.VMEM(ip.shape, F32),
             pltpu.VMEM(coef.shape, F32),
             pltpu.VMEM((count, height, width), F32),
-            pltpu.SemaphoreType.DMA((7 + CHUNKS,)),
+            pltpu.SemaphoreType.DMA((10 + CHUNKS,)),
         ],
         compiler_params=params(16),
         name="last_part",
-    )(*pin(padded, halos, velocity, mixing, land, ip, coef, weights))
+    )(*pin(padded, halos, velocity, mixing, land, ip, coef, weights, *indices))
 
 
 def back_kernel(
@@ -953,7 +989,7 @@
     by_tracer = pl.pallas_call(
         functools.partial(back_kernel, tracers=tracers, cells=cells),
         out_shape=pltpu.HBM((tracers, blocks, cells), F32),
-        in_specs=[hbm()] * 3 + [vmem(), hbm(), vmem()],
+        in_specs=[vmem()] * 4 + [hbm(), vmem()],
         out_specs=hbm(),
         scratch_shapes=[
             pltpu.SMEM((pairs,), ints),
@@ -967,7 +1003,7 @@
         ],
         compiler_params=params(8),
         name="back",
-    )(*pin(slots, atm, rows), returned, *pin(weights), near)
+    )(slots, atm, rows, returned, *pin(weights), near)
     return by_tracer.transpose(1, 0, 2)
 
 
@@ -1020,10 +1056,11 @@
         mesh_sizes, top, received, edge, top_edge, land_near, pick, nodes, levels, cap, window
     )
     returned = all_to_all(answer)
-    out, near = last_part(
-        state, halos, velocity, mixing, land, ip, coef_far, regrid_weights, levels
-    )
-    atm_surface = back(slots, pair_atm, atm_rows, returned, regrid_weights, near, tracer_count)
+    out, near, *indices = last_part(
+        state, halos, velocity, mixing, land, ip, coef_far, regrid_weights,
+        (slots, pair_atm, atm_rows), levels,
+    )
+    atm_surface = back(*indices, returned, regrid_weights, near, tracer_count)
     return (out.reshape(tracers.shape), atm_surface)
 
 

time: 51.7 us -> 51.1 us (0.988)
  transfers between devices with their start and end apart: 10 -> 10, of which waited for: 3 -> 2; matrix products, arithmetic and copies ran while one was open for 0% -> 0% of each run, Pallas kernels for 29% -> 29%
where the time goes in v7:
time: 51.1 us; the launch traced here: 50.8 us
  Pallas kernels  25.3 us (50%)
  starting transfers between devices  17.7 us (35%)
  waiting for transfers between devices  6.95 us (14%)
  between operations  0.81 us (2%)
    all_to_all x2, starting transfers between devices, all_to_all(): return lax.all_to_all(x, AXES, split_axis=0, concat_axis=0, tiled=True)  11 us
    all_to_all x2, waiting for transfers between devices, all_to_all(): return lax.all_to_all(x, AXES, split_axis=0, concat_axis=0, tiled=True)  6.93 us
    ppermute x8, starting transfers between devices, exchange(): return [lax.ppermute(line, AXES, perm) for line, perm in zip(lines, perms)]  6.68 us
    pallas_call x1, Pallas kernels, last_part(): pl.pallas_call(functools.partial(last_kernel, levels=levels), out_shape=(...  5.79 us
    pallas_call x1, Pallas kernels, first_part(): pl.pallas_call(functools.partial(first_kernel, levels=levels), out_shape=...  4.75 us
    pallas_call x1, Pallas kernels, contributions(): pl.pallas_call(functools.partial(contrib_kernel, sizes=sizes, nodes=nodes...  3.22 us
    pallas_call x1, Pallas kernels, middle_part(): pl.pallas_call(functools.partial(middle_kernel, sizes=sizes, levels=level...  3.22 us
    pallas_call x1, Pallas kernels, back(): pl.pallas_call(functools.partial(back_kernel, tracers=tracers, cells=cell...  2.81 us
  transfers between devices with their start and end apart: 10, of which 2 were waited for; matrix products, arithmetic and copies ran while one was open for 0% of the time, Pallas kernels for 29%

profile of v7, /device:TPU:0, one launch (start us, length us, event | category | flops | bytes accessed | tf_op | source)
XLA Modules:
  0.0 50.8 jit_solution(14328430853035614173)
XLA Ops:
  0.6 0.0 copy-start
  0.6 0.0 copy-start.1
  0.7 0.0 copy-start.2
  0.7 3.2 %contributions.1 = (bf16[16,104,128]{2,1,0:T(8,128)(2,1)}, s32[96]{0:T(128)}) custom-call(s32[96]{0:T(128)} %bitcast.6, s32[96]{0:T(128)} %atm_hbm.3, s32[96]{0:T(128)} %row_hbm.1, s32[48]{0:T(128)} %rows_hbm.3, bf16[48,8,128]{2,1,0:T(8,128)(2,1)} %flux_hbm.1, bf16[96,128,128]{2,1,0:T(8,128)(2,1)} %weights_hbm.5), custom_call_target="tpu_custom_call" | custom-call | tf_op jit(solution)/shard_map/contributions/pallas_call | solution.py:179
  3.9 7.4 %all-to-all-start = ((bf16[16,104,128]{2,1,0:T(8,128)(2,1)}), bf16[16,104,128]{2,1,0:T(8,128)(2,1)S(1)}, u32[]{:S(2)}, u32[]{:S(2)}) async-start(bf16[16,104,128]{2,1,0:T(8,128)(2,1)} %get-tuple-element.39), calls=%async_computation | async-start | bytes 851968 | tf_op jit(solution)/shard_map/all_to_all | solution.py:1011
  11.3 2.3 %edges.1 = (f32[48,144,128]{2,1,0:T(8,128)S(1)}, f32[48,128]{1,0:T(8,128)S(1)}, f32[48,128]{1,0:T(8,128)S(1)}, f32[48,128]{1,0:T(8,128)S(1)}, f32[48,128]{1,0:T(8,128)S(1)}) custom-call(s32[96]{0:T(128)} %get-tuple-element.40.order.slot_hbm, f32[48,128,128]{2,1,0:T(8,128)} %bitcast.4), custom_call_target="tpu_custom_call" | custom-call | tf_op jit(solution)/shard_map/edges/pallas_call | solution.py:305
  13.5 2.0 %collective-permute-start = (f32[48,128]{1,0:T(8,128)S(1)}, f32[48,128]{1,0:T(8,128)S(1)}, u32[]{:S(2)}, u32[]{:S(2)}) collective-permute-start(f32[48,128]{1,0:T(8,128)S(1)} %get-tuple-element.47), channel_id=1, source_target_pairs={{0,4},{1,5},{2,6},{3,7},{4,0},{5,1},{6,2},{7,3},{8,12},{9,13},{10,... | collective-permute-start | bytes 73736 | tf_op jit(solution)/shard_map/ppermute | solution.py:266
  15.5 1.6 %collective-permute-start.2 = (f32[48,128]{1,0:T(8,128)S(1)}, f32[48,128]{1,0:T(8,128)S(1)}, u32[]{:S(2)}, u32[]{:S(2)}) collective-permute-start(f32[48,128]{1,0:T(8,128)S(1)} %get-tuple-element.49), channel_id=1, source_target_pairs={{0,3},{1,2},{2,1},{3,0},{4,7},{5,6},{6,5},{7,4},{8,11},{9,10},{10,... | collective-permute-start | bytes 73736 | tf_op jit(solution)/shard_map/ppermute | solution.py:266
  17.1 0.0 collective-permute-start.3
  17.1 4.7 %first_part.1 = (f32[4,3,8,128]{3,2,1,0:T(8,128)S(1)}, f32[48,128,128]{2,1,0:T(8,128)}, f32[8,128,128]{2,1,0:T(8,128)}, f32[8,128,128]{2,1,0:T(8,128)}, f32[4,3,8,128]{3,2,1,0:T(8,128)}) custom-call(f32[48,144,128]{2,1,0:T(8,128)S(1)} %get-tuple-element.41.padded, f32[2,8,128,128]{3,2,1,0:T(8,128)S(1)} %copy-done, f32[7,128,128]{2,1,0:T(8,128)S(1)} %copy-done.1, ...), custom_call_target="tpu_custom_call" | custom-call | tf_op jit(solution)/shard_map/first_part/pallas_call | solution.py:493
  21.9 0.0 collective-permute-done.2.r2
  21.9 0.0 collective-permute-done.3.r3
  21.9 0.2 halo_part.1
  22.1 2.2 %all-to-all-done.incoming_ref = bf16[16,104,128]{2,1,0:T(8,128)(2,1)S(1)} async-done(((bf16[16,104,128]{2,1,0:T(8,128)(2,1)}), bf16[16,104,128]{2,1,0:T(8,128)(2,1)S(1)}, u32[]{:S(2)}, u32[]{:S(2)}) %all-to-all-start) | async-done | bytes 426016 | tf_op jit(solution)/shard_map/all_to_all | solution.py:1011
  24.3 3.2 %middle_part.1 = (f32[48,144,128]{2,1,0:T(8,128)S(1)}, f32[9,128,128]{2,1,0:T(8,128)S(1)}, bf16[256,128]{1,0:T(8,128)(2,1)S(1)}, f32[8,128,128]{2,1,0:T(8,128)S(...) custom-call(bf16[16,104,128]{2,1,0:T(8,128)(2,1)S(1)} %all-to-all-do, ...), custom_call_target="tpu_custom_call" | custom-call | tf_op jit(solution)/shard_map/middle_part/pallas_call | solution.py:673
  27.5 1.5 %collective-permute-start.4 = (f32[48,128]{1,0:T(8,128)S(1)}, f32[48,128]{1,0:T(8,128)S(1)}, u32[]{:S(2)}, u32[]{:S(2)}) collective-permute-start(f32[48,128]{1,0:T(8,128)S(1)} %get-tuple-element.61), channel_id=1, source_target_pairs={{0,4},{1,5},{2,6},{3,7},{4,0},{5,1},{6,2},{7,3},{8,12},{9,13},{10,... | collective-permute-start | bytes 73736 | tf_op jit(solution)/shard_map/ppermute | solution.py:266
  29.0 1.6 %collective-permute-start.6 = (f32[48,128]{1,0:T(8,128)S(1)}, f32[48,128]{1,0:T(8,128)S(1)}, u32[]{:S(2)}, u32[]{:S(2)}) collective-permute-start(f32[48,128]{1,0:T(8,128)S(1)} %get-tuple-element.63), channel_id=1, source_target_pairs={{0,3},{1,2},{2,1},{3,0},{4,7},{5,6},{6,5},{7,4},{8,11},{9,10},{10,... | collective-permute-start | bytes 73736 | tf_op jit(solution)/shard_map/ppermute | solution.py:266
  30.6 0.0 collective-permute-start.7
  30.6 1.9 %inner_part.1 = (f32[6,128,128]{2,1,0:T(8,128)S(1)}, f32[48,144,128]{2,1,0:T(8,128)}) custom-call(f32[48,144,128]{2,1,0:T(8,128)S(1)} %get-tuple-element.53.padded, f32[2,8,128,128]{3,2,1,0:T(8,128)S(1)} %get-tuple-element.54.vel_ref, f32[7,128,128]{2,1,0:T(8,128)S(1)} %get-tuple-element.55.k_ref, s32[128,128]{1,0:T(8,128)S(1)} %get-tuple-element.56.land_ref, ...), custom_call_target="tpu_custom_call" | custom-call | tf_op jit(solution)/shard_map/inner_part/pallas_call | solution.py:731
  32.5 1.2 %replies.1 = (f32[6,128,128]{2,1,0:T(8,128)S(1)}, f32[4,48,128]{2,1,0:T(8,128)}, bf16[16,72,128]{2,1,0:T(8,128)(2,1)}) custom-call(f32[6,128,128]{2,1,0:T(8,128)S(1)} %get-tuple-element.60.top_in, f32[48,128]{1,0:T(8,128)S(1)} %collective-permute-done.4.r0, f32[48,128]{1,0:T(8,128)S(1)} %collective-permute-done.5.r1, ...), custom_call_target="tpu_custom_call", output_to_operand_aliasing={{0}: (0, {})} | custom-call | tf_op jit(solution)/shard_map/replies/pallas_call | solution.py:803
  33.8 3.6 %all-to-all-start.1 = ((bf16[16,72,128]{2,1,0:T(8,128)(2,1)}), bf16[16,72,128]{2,1,0:T(8,128)(2,1)S(1)}, u32[]{:S(2)}, u32[]{:S(2)}) async-start(bf16[16,72,128]{2,1,0:T(8,128)(2,1)} %get-tuple-element.74), calls=%async_computation.1 | async-start | bytes 589824 | tf_op jit(solution)/shard_map/all_to_all | solution.py:1011
  37.4 5.8 %last_part.1 = (f32[48,128,128]{2,1,0:T(8,128)}, bf16[48,128,128]{2,1,0:T(8,128)(2,1)S(1)}, s32[96]{0:T(128)S(1)}, s32[96]{0:T(128)S(1)}, s32[48]{0:T(128)S(1)}) custom-call(f32[48,144,128]{2,1,0:T(8,128)} %get-tuple-element.59.padded_hbm, f32[4,48,128]{2,1,0:T(8,128)} %get-tuple-element.68.halo_hbm, f32[2,8,128,128]{3,2,1,0:T(8,128)} %vel_hbm.3, ...), custom_call_target="tpu_custom_call" | custom-call | tf_op jit(solution)/shard_map/last_part/pallas_call | solution.py:897
  43.2 4.8 %all-to-all-done.1.returned_ref = bf16[16,72,128]{2,1,0:T(8,128)(2,1)S(1)} async-done(((bf16[16,72,128]{2,1,0:T(8,128)(2,1)}), bf16[16,72,128]{2,1,0:T(8,128)(2,1)S(1)}, u32[]{:S(2)}, u32[]{:S(2)}) %all-to-all-start.1) | async-done | bytes 294944 | tf_op jit(solution)/shard_map/all_to_all | solution.py:1011
  48.0 2.8 %back.1 = f32[6,48,128]{2,1,0:T(8,128)} custom-call(s32[96]{0:T(128)S(1)} %get-tuple-element.71.slot_hbm, s32[96]{0:T(128)S(1)} %get-tuple-element.72.atm_hbm, s32[48]{0:T(128)S(1)} %get-tuple-element.73.rows_hbm, bf16[16,72,128]{2,1,0:T(8,128)(2,1)S(1)} %all-to-all-done.1.returned_ref, bf16[96,128,128]{2,1,0:T(8,128)(2,1)} %weights_hbm.5, ...), custom_call_target="tpu_custom_call" | custom-call | tf_op jit(solution)/shard_map/back/pallas_call | solution.py:989
  (11 shorter events, 0.0 us)
Async XLA Ops:
  0.6 16.5 %copy-start = (f32[2,8,128,128]{3,2,1,0:T(8,128)S(1)}, f32[2,8,128,128]{3,2,1,0:T(8,128)}, u32[]{:S(2)}) copy-start(f32[2,8,128,128]{3,2,1,0:T(8,128)} %vel_hbm.3) | copy-start | bytes 3145732
  0.6 16.5 %copy-start.1 = (f32[7,128,128]{2,1,0:T(8,128)S(1)}, f32[7,128,128]{2,1,0:T(8,128)}, u32[]{:S(2)}) copy-start(f32[7,128,128]{2,1,0:T(8,128)} %k_hbm.3) | copy-start | bytes 1376260
  0.7 16.5 %copy-start.2 = (s32[128,128]{1,0:T(8,128)S(1)}, s32[128,128]{1,0:T(8,128)}, u32[]{:S(2)}) copy-start(s32[128,128]{1,0:T(8,128)} %land_hbm.3) | copy-start | bytes 196612
  3.9 20.4 %all-to-all-start = ((bf16[16,104,128]{2,1,0:T(8,128)(2,1)}), bf16[16,104,128]{2,1,0:T(8,128)(2,1)S(1)}, u32[]{:S(2)}, u32[]{:S(2)}) async-start(bf16[16,104,128]{2,1,0:T(8,128)(2,1)} %get-tuple-element.39), calls=%async_computation | async-start | bytes 851968 | tf_op jit(solution)/shard_map/all_to_all | solution.py:1011
  13.5 8.3 %collective-permute-start = (f32[48,128]{1,0:T(8,128)S(1)}, f32[48,128]{1,0:T(8,128)S(1)}, u32[]{:S(2)}, u32[]{:S(2)}) collective-permute-start(f32[48,128]{1,0:T(8,128)S(1)} %get-tuple-element.47), channel_id=1, source_target_pairs={{0,4},{1,5},{2,6},{3,7},{4,0},{5,1},{6,2},{7,3},{8,12},{9,13},{10,... | collective-permute-start | bytes 73736 | tf_op jit(solution)/shard_map/ppermute | solution.py:266
  15.5 6.4 %collective-permute-start.1 = (f32[48,128]{1,0:T(8,128)S(1)}, f32[48,128]{1,0:T(8,128)S(1)}, u32[]{:S(2)}, u32[]{:S(2)}) collective-permute-start(f32[48,128]{1,0:T(8,128)S(1)} %get-tuple-element.48), channel_id=1, source_target_pairs={{0,1},{1,0},{2,3},{3,2},{4,8},{5,9},{6,10},{7,11},{8,4},{9,5},{10,... | collective-permute-start | bytes 73736 | tf_op jit(solution)/shard_map/ppermute | solution.py:266
  15.5 6.4 %collective-permute-start.2 = (f32[48,128]{1,0:T(8,128)S(1)}, f32[48,128]{1,0:T(8,128)S(1)}, u32[]{:S(2)}, u32[]{:S(2)}) collective-permute-start(f32[48,128]{1,0:T(8,128)S(1)} %get-tuple-element.49), channel_id=1, source_target_pairs={{0,3},{1,2},{2,1},{3,0},{4,7},{5,6},{6,5},{7,4},{8,11},{9,10},{10,... | collective-permute-start | bytes 73736 | tf_op jit(solution)/shard_map/ppermute | solution.py:266
  17.1 4.8 %collective-permute-start.3 = (f32[48,128]{1,0:T(8,128)S(1)}, f32[48,128]{1,0:T(8,128)S(1)}, u32[]{:S(2)}, u32[]{:S(2)}) collective-permute-start(f32[48,128]{1,0:T(8,128)S(1)} %get-tuple-element.50), channel_id=1, source_target_pairs={{0,1},{1,0},{2,3},{3,2},{4,5},{5,4},{6,7},{7,6},{8,9},{9,8},{10,11... | collective-permute-start | bytes 73736 | tf_op jit(solution)/shard_map/ppermute | solution.py:266
  27.5 5.0 %collective-permute-start.4 = (f32[48,128]{1,0:T(8,128)S(1)}, f32[48,128]{1,0:T(8,128)S(1)}, u32[]{:S(2)}, u32[]{:S(2)}) collective-permute-start(f32[48,128]{1,0:T(8,128)S(1)} %get-tuple-element.61), channel_id=1, source_target_pairs={{0,4},{1,5},{2,6},{3,7},{4,0},{5,1},{6,2},{7,3},{8,12},{9,13},{10,... | collective-permute-start | bytes 73736 | tf_op jit(solution)/shard_map/ppermute | solution.py:266
  29.0 3.5 %collective-permute-start.5 = (f32[48,128]{1,0:T(8,128)S(1)}, f32[48,128]{1,0:T(8,128)S(1)}, u32[]{:S(2)}, u32[]{:S(2)}) collective-permute-start(f32[48,128]{1,0:T(8,128)S(1)} %get-tuple-element.62), channel_id=1, source_target_pairs={{0,1},{1,0},{2,3},{3,2},{4,8},{5,9},{6,10},{7,11},{8,4},{9,5},{10,... | collective-permute-start | bytes 73736 | tf_op jit(solution)/shard_map/ppermute | solution.py:266
  29.0 3.5 %collective-permute-start.6 = (f32[48,128]{1,0:T(8,128)S(1)}, f32[48,128]{1,0:T(8,128)S(1)}, u32[]{:S(2)}, u32[]{:S(2)}) collective-permute-start(f32[48,128]{1,0:T(8,128)S(1)} %get-tuple-element.63), channel_id=1, source_target_pairs={{0,3},{1,2},{2,1},{3,0},{4,7},{5,6},{6,5},{7,4},{8,11},{9,10},{10,... | collective-permute-start | bytes 73736 | tf_op jit(solution)/shard_map/ppermute | solution.py:266
  30.6 1.9 %collective-permute-start.7 = (f32[48,128]{1,0:T(8,128)S(1)}, f32[48,128]{1,0:T(8,128)S(1)}, u32[]{:S(2)}, u32[]{:S(2)}) collective-permute-start(f32[48,128]{1,0:T(8,128)S(1)} %get-tuple-element.64), channel_id=1, source_target_pairs={{0,1},{1,0},{2,3},{3,2},{4,5},{5,4},{6,7},{7,6},{8,9},{9,8},{10,11... | collective-permute-start | bytes 73736 | tf_op jit(solution)/shard_map/ppermute | solution.py:266
  33.8 14.2 %all-to-all-start.1 = ((bf16[16,72,128]{2,1,0:T(8,128)(2,1)}), bf16[16,72,128]{2,1,0:T(8,128)(2,1)S(1)}, u32[]{:S(2)}, u32[]{:S(2)}) async-start(bf16[16,72,128]{2,1,0:T(8,128)(2,1)} %get-tuple-element.74), calls=%async_computation.1 | async-start | bytes 589824 | tf_op jit(solution)/shard_map/all_to_all | solution.py:1011

commit v8 on v7

--- a/solution.py
+++ b/solution.py
@@ -826,7 +826,7 @@
 
 def last_kernel(
     padded_hbm, halo_hbm, vel_hbm, k_hbm, land_hbm, ip_hbm, coef_hbm, weights_hbm,
-    slot_hbm, atm_hbm, rows_hbm, out_hbm, near_ref, slot_ref, atm_ref, rows_ref, padded, halos, lines, sides, vel_ref, k_ref, land_ref, ip_ref, coef_ref, out_ref,
+    slot_hbm, atm_hbm, rows_hbm, out_hbm, near_ref, slot_ref, atm_ref, rows_ref, arrived, padded, halos, lines, sides, vel_ref, k_ref, land_ref, ip_ref, coef_ref, out_ref,
     sems, *, levels,
 ):
     count, height, width = out_ref.shape
@@ -843,7 +843,7 @@
     near = near_ref.shape[0]
     kept = copies_of(
         [
-            (weights_hbm.at[pl.ds(weights_hbm.shape[0] - near, near)], near_ref),
+            (weights_hbm.at[pl.ds(weights_hbm.shape[0] - near, near)], arrived),
             (slot_hbm, slot_ref), (atm_hbm, atm_ref), (rows_hbm, rows_ref),
         ],
         sems,
@@ -887,7 +887,11 @@
                     out_ref[t * levels + lower, here, :] = x
 
     sweep(padded, vel_ref, k_ref, land_ref, ip_ref, sides, finish, levels, wait, done)
-    for copy in outs + kept:
+    for copy in kept:
+        copy.wait()
+    for p in range(near):
+        near_ref[p] = arrived[p].T
+    for copy in outs:
         copy.wait()
 
 
@@ -898,12 +902,13 @@
         functools.partial(last_kernel, levels=levels),
         out_shape=(
             pltpu.HBM((count, height, width), F32),
-            jax.ShapeDtypeStruct((weights.shape[0] // 2,) + weights.shape[1:], BF16),
+            jax.ShapeDtypeStruct((weights.shape[0] // 2, width, weights.shape[1]), BF16),
             *[jax.ShapeDtypeStruct(x.shape, x.dtype) for x in indices],
         ),
         in_specs=[hbm()] * 11,
         out_specs=(hbm(),) + (vmem(),) * 4,
         scratch_shapes=[
+            pltpu.VMEM((weights.shape[0] // 2,) + weights.shape[1:], BF16),
             pltpu.VMEM(padded.shape, F32),
             pltpu.VMEM(halos.shape, F32),
             pltpu.VMEM((width, height), F32),
@@ -916,7 +921,7 @@
             pltpu.VMEM((count, height, width), F32),
             pltpu.SemaphoreType.DMA((10 + CHUNKS,)),
         ],
-        compiler_params=params(16),
+        compiler_params=params(18),
         name="last_part",
     )(*pin(padded, halos, velocity, mixing, land, ip, coef, weights, *indices))
 
@@ -957,10 +962,14 @@
         lhs = jnp.concatenate(
             [wide[pl.ds(slot_ref[p + k] * tracers, 8), :] for k in range(2)], axis=0
         )
-        source, at = (weights_ref, p) if p < far else (near_ref, p - far)
-        rhs = jnp.concatenate([source[at], source[at + 1]], axis=0)
+        if p < far:
+            rhs = jnp.concatenate([weights_ref[p], weights_ref[p + 1]], axis=0)
+            contract = 1
+        else:
+            rhs = jnp.concatenate([near_ref[p - far], near_ref[p - far + 1]], axis=1)
+            contract = 0
         both = lax.dot_general(
-            lhs.astype(BF16), rhs, (((1,), (1,)), ((), ())), preferred_element_type=F32
+            lhs.astype(BF16), rhs, (((1,), (contract,)), ((), ())), preferred_element_type=F32
         )
         for k in range(2):
             here = pl.ds(pl.multiple_of(atm_ref[p + k] * 8, 8), 8)

time: 51.1 us -> 51 us (level)
  no operation moved by 1% of the time
where the time goes in v8:
time: 51 us; the launch traced here: 50.7 us
  Pallas kernels  25.2 us (49%)
  starting transfers between devices  17.7 us (35%)
  waiting for transfers between devices  6.96 us (14%)
  between operations  0.81 us (2%)
    all_to_all x2, starting transfers between devices, all_to_all(): return lax.all_to_all(x, AXES, split_axis=0, concat_axis=0, tiled=True)  11 us
    all_to_all x2, waiting for transfers between devices, all_to_all(): return lax.all_to_all(x, AXES, split_axis=0, concat_axis=0, tiled=True)  6.93 us
    ppermute x8, starting transfers between devices, exchange(): return [lax.ppermute(line, AXES, perm) for line, perm in zip(lines, perms)]  6.68 us
    pallas_call x1, Pallas kernels, last_part(): pl.pallas_call(functools.partial(last_kernel, levels=levels), out_shape=(...  5.78 us
    pallas_call x1, Pallas kernels, first_part(): pl.pallas_call(functools.partial(first_kernel, levels=levels), out_shape=...  4.75 us
    pallas_call x1, Pallas kernels, contributions(): pl.pallas_call(functools.partial(contrib_kernel, sizes=sizes, nodes=nodes...  3.22 us
    pallas_call x1, Pallas kernels, middle_part(): pl.pallas_call(functools.partial(middle_kernel, sizes=sizes, levels=level...  3.22 us
    pallas_call x1, Pallas kernels, back(): pl.pallas_call(functools.partial(back_kernel, tracers=tracers, cells=cell...  2.71 us
  transfers between devices with their start and end apart: 10, of which 2 were waited for; matrix products, arithmetic and copies ran while one was open for 0% of the time, Pallas kernels for 29%

profile of v8, /device:TPU:0, one launch (start us, length us, event | category | flops | bytes accessed | tf_op | source)
XLA Modules:
  0.0 50.7 jit_solution(3202175322243912217)
XLA Ops:
  0.6 0.0 copy-start
  0.6 0.0 copy-start.1
  0.7 0.0 copy-start.2
  0.7 3.2 %contributions.1 = (bf16[16,104,128]{2,1,0:T(8,128)(2,1)}, s32[96]{0:T(128)}) custom-call(s32[96]{0:T(128)} %bitcast.6, s32[96]{0:T(128)} %atm_hbm.3, s32[96]{0:T(128)} %row_hbm.1, s32[48]{0:T(128)} %rows_hbm.3, bf16[48,8,128]{2,1,0:T(8,128)(2,1)} %flux_hbm.1, bf16[96,128,128]{2,1,0:T(8,128)(2,1)} %weights_hbm.5), custom_call_target="tpu_custom_call" | custom-call | tf_op jit(solution)/shard_map/contributions/pallas_call | solution.py:179
  3.9 7.4 %all-to-all-start = ((bf16[16,104,128]{2,1,0:T(8,128)(2,1)}), bf16[16,104,128]{2,1,0:T(8,128)(2,1)S(1)}, u32[]{:S(2)}, u32[]{:S(2)}) async-start(bf16[16,104,128]{2,1,0:T(8,128)(2,1)} %get-tuple-element.39), calls=%async_computation | async-start | bytes 851968 | tf_op jit(solution)/shard_map/all_to_all | solution.py:1020
  11.3 2.3 %edges.1 = (f32[48,144,128]{2,1,0:T(8,128)S(1)}, f32[48,128]{1,0:T(8,128)S(1)}, f32[48,128]{1,0:T(8,128)S(1)}, f32[48,128]{1,0:T(8,128)S(1)}, f32[48,128]{1,0:T(8,128)S(1)}) custom-call(s32[96]{0:T(128)} %get-tuple-element.40.order.slot_hbm, f32[48,128,128]{2,1,0:T(8,128)} %bitcast.4), custom_call_target="tpu_custom_call" | custom-call | tf_op jit(solution)/shard_map/edges/pallas_call | solution.py:305
  13.5 2.0 %collective-permute-start = (f32[48,128]{1,0:T(8,128)S(1)}, f32[48,128]{1,0:T(8,128)S(1)}, u32[]{:S(2)}, u32[]{:S(2)}) collective-permute-start(f32[48,128]{1,0:T(8,128)S(1)} %get-tuple-element.47), channel_id=1, source_target_pairs={{0,4},{1,5},{2,6},{3,7},{4,0},{5,1},{6,2},{7,3},{8,12},{9,13},{10,... | collective-permute-start | bytes 73736 | tf_op jit(solution)/shard_map/ppermute | solution.py:266
  15.5 0.0 collective-permute-start.1
  15.5 1.6 %collective-permute-start.2 = (f32[48,128]{1,0:T(8,128)S(1)}, f32[48,128]{1,0:T(8,128)S(1)}, u32[]{:S(2)}, u32[]{:S(2)}) collective-permute-start(f32[48,128]{1,0:T(8,128)S(1)} %get-tuple-element.49), channel_id=1, source_target_pairs={{0,3},{1,2},{2,1},{3,0},{4,7},{5,6},{6,5},{7,4},{8,11},{9,10},{10,... | collective-permute-start | bytes 73736 | tf_op jit(solution)/shard_map/ppermute | solution.py:266
  17.1 0.0 collective-permute-start.3
  17.1 4.7 %first_part.1 = (f32[4,3,8,128]{3,2,1,0:T(8,128)S(1)}, f32[48,128,128]{2,1,0:T(8,128)}, f32[8,128,128]{2,1,0:T(8,128)}, f32[8,128,128]{2,1,0:T(8,128)}, f32[4,3,8,128]{3,2,1,0:T(8,128)}) custom-call(f32[48,144,128]{2,1,0:T(8,128)S(1)} %get-tuple-element.41.padded, f32[2,8,128,128]{3,2,1,0:T(8,128)S(1)} %copy-done, f32[7,128,128]{2,1,0:T(8,128)S(1)} %copy-done.1, ...), custom_call_target="tpu_custom_call" | custom-call | tf_op jit(solution)/shard_map/first_part/pallas_call | solution.py:493
  21.9 0.0 collective-permute-done.1.r1
  21.9 0.2 halo_part.1
  22.1 2.2 %all-to-all-done.incoming_ref = bf16[16,104,128]{2,1,0:T(8,128)(2,1)S(1)} async-done(((bf16[16,104,128]{2,1,0:T(8,128)(2,1)}), bf16[16,104,128]{2,1,0:T(8,128)(2,1)S(1)}, u32[]{:S(2)}, u32[]{:S(2)}) %all-to-all-start) | async-done | bytes 426016 | tf_op jit(solution)/shard_map/all_to_all | solution.py:1020
  24.3 3.2 %middle_part.1 = (f32[48,144,128]{2,1,0:T(8,128)S(1)}, f32[9,128,128]{2,1,0:T(8,128)S(1)}, bf16[256,128]{1,0:T(8,128)(2,1)S(1)}, f32[8,128,128]{2,1,0:T(8,128)S(...) custom-call(bf16[16,104,128]{2,1,0:T(8,128)(2,1)S(1)} %all-to-all-do, ...), custom_call_target="tpu_custom_call" | custom-call | tf_op jit(solution)/shard_map/middle_part/pallas_call | solution.py:673
  27.5 1.5 %collective-permute-start.4 = (f32[48,128]{1,0:T(8,128)S(1)}, f32[48,128]{1,0:T(8,128)S(1)}, u32[]{:S(2)}, u32[]{:S(2)}) collective-permute-start(f32[48,128]{1,0:T(8,128)S(1)} %get-tuple-element.61), channel_id=1, source_target_pairs={{0,4},{1,5},{2,6},{3,7},{4,0},{5,1},{6,2},{7,3},{8,12},{9,13},{10,... | collective-permute-start | bytes 73736 | tf_op jit(solution)/shard_map/ppermute | solution.py:266
  29.0 1.6 %collective-permute-start.6 = (f32[48,128]{1,0:T(8,128)S(1)}, f32[48,128]{1,0:T(8,128)S(1)}, u32[]{:S(2)}, u32[]{:S(2)}) collective-permute-start(f32[48,128]{1,0:T(8,128)S(1)} %get-tuple-element.63), channel_id=1, source_target_pairs={{0,3},{1,2},{2,1},{3,0},{4,7},{5,6},{6,5},{7,4},{8,11},{9,10},{10,... | collective-permute-start | bytes 73736 | tf_op jit(solution)/shard_map/ppermute | solution.py:266
  30.6 0.0 collective-permute-start.7
  30.6 1.9 %inner_part.1 = (f32[6,128,128]{2,1,0:T(8,128)S(1)}, f32[48,144,128]{2,1,0:T(8,128)}) custom-call(f32[48,144,128]{2,1,0:T(8,128)S(1)} %get-tuple-element.53.padded, f32[2,8,128,128]{3,2,1,0:T(8,128)S(1)} %get-tuple-element.54.vel_ref, f32[7,128,128]{2,1,0:T(8,128)S(1)} %get-tuple-element.55.k_ref, s32[128,128]{1,0:T(8,128)S(1)} %get-tuple-element.56.land_ref, ...), custom_call_target="tpu_custom_call" | custom-call | tf_op jit(solution)/shard_map/inner_part/pallas_call | solution.py:731
  32.5 1.2 %replies.1 = (f32[6,128,128]{2,1,0:T(8,128)S(1)}, f32[4,48,128]{2,1,0:T(8,128)}, bf16[16,72,128]{2,1,0:T(8,128)(2,1)}) custom-call(f32[6,128,128]{2,1,0:T(8,128)S(1)} %get-tuple-element.60.top_in, f32[48,128]{1,0:T(8,128)S(1)} %collective-permute-done.4.r0, f32[48,128]{1,0:T(8,128)S(1)} %collective-permute-done.5.r1, ...), custom_call_target="tpu_custom_call", output_to_operand_aliasing={{0}: (0, {})} | custom-call | tf_op jit(solution)/shard_map/replies/pallas_call | solution.py:803
  33.8 3.6 %all-to-all-start.1 = ((bf16[16,72,128]{2,1,0:T(8,128)(2,1)}), bf16[16,72,128]{2,1,0:T(8,128)(2,1)S(1)}, u32[]{:S(2)}, u32[]{:S(2)}) async-start(bf16[16,72,128]{2,1,0:T(8,128)(2,1)} %get-tuple-element.74), calls=%async_computation.1 | async-start | bytes 589824 | tf_op jit(solution)/shard_map/all_to_all | solution.py:1020
  37.4 5.8 %last_part.1 = (f32[48,128,128]{2,1,0:T(8,128)}, bf16[48,128,128]{2,1,0:T(8,128)(2,1)S(1)}, s32[96]{0:T(128)S(1)}, s32[96]{0:T(128)S(1)}, s32[48]{0:T(128)S(1)}) custom-call(f32[48,144,128]{2,1,0:T(8,128)} %get-tuple-element.59.padded_hbm, f32[4,48,128]{2,1,0:T(8,128)} %get-tuple-element.68.halo_hbm, f32[2,8,128,128]{3,2,1,0:T(8,128)} %vel_hbm.3, ...), custom_call_target="tpu_custom_call" | custom-call | tf_op jit(solution)/shard_map/last_part/pallas_call | solution.py:901
  43.2 4.8 %all-to-all-done.1.returned_ref = bf16[16,72,128]{2,1,0:T(8,128)(2,1)S(1)} async-done(((bf16[16,72,128]{2,1,0:T(8,128)(2,1)}), bf16[16,72,128]{2,1,0:T(8,128)(2,1)S(1)}, u32[]{:S(2)}, u32[]{:S(2)}) %all-to-all-start.1) | async-done | bytes 294944 | tf_op jit(solution)/shard_map/all_to_all | solution.py:1020
  48.0 2.7 %back.1 = f32[6,48,128]{2,1,0:T(8,128)} custom-call(s32[96]{0:T(128)S(1)} %get-tuple-element.71.slot_hbm, s32[96]{0:T(128)S(1)} %get-tuple-element.72.atm_hbm, s32[48]{0:T(128)S(1)} %get-tuple-element.73.rows_hbm, bf16[16,72,128]{2,1,0:T(8,128)(2,1)S(1)} %all-to-all-done.1.returned_ref, bf16[96,128,128]{2,1,0:T(8,128)(2,1)} %weights_hbm.5, ...), custom_call_target="tpu_custom_call" | custom-call | tf_op jit(solution)/shard_map/back/pallas_call | solution.py:998
  (11 shorter events, 0.0 us)
Async XLA Ops:
  0.6 16.5 %copy-start = (f32[2,8,128,128]{3,2,1,0:T(8,128)S(1)}, f32[2,8,128,128]{3,2,1,0:T(8,128)}, u32[]{:S(2)}) copy-start(f32[2,8,128,128]{3,2,1,0:T(8,128)} %vel_hbm.3) | copy-start | bytes 3145732
  0.6 16.5 %copy-start.1 = (f32[7,128,128]{2,1,0:T(8,128)S(1)}, f32[7,128,128]{2,1,0:T(8,128)}, u32[]{:S(2)}) copy-start(f32[7,128,128]{2,1,0:T(8,128)} %k_hbm.3) | copy-start | bytes 1376260
  0.7 16.5 %copy-start.2 = (s32[128,128]{1,0:T(8,128)S(1)}, s32[128,128]{1,0:T(8,128)}, u32[]{:S(2)}) copy-start(s32[128,128]{1,0:T(8,128)} %land_hbm.3) | copy-start | bytes 196612
  3.9 20.4 %all-to-all-start = ((bf16[16,104,128]{2,1,0:T(8,128)(2,1)}), bf16[16,104,128]{2,1,0:T(8,128)(2,1)S(1)}, u32[]{:S(2)}, u32[]{:S(2)}) async-start(bf16[16,104,128]{2,1,0:T(8,128)(2,1)} %get-tuple-element.39), calls=%async_computation | async-start | bytes 851968 | tf_op jit(solution)/shard_map/all_to_all | solution.py:1020
  13.5 8.3 %collective-permute-start = (f32[48,128]{1,0:T(8,128)S(1)}, f32[48,128]{1,0:T(8,128)S(1)}, u32[]{:S(2)}, u32[]{:S(2)}) collective-permute-start(f32[48,128]{1,0:T(8,128)S(1)} %get-tuple-element.47), channel_id=1, source_target_pairs={{0,4},{1,5},{2,6},{3,7},{4,0},{5,1},{6,2},{7,3},{8,12},{9,13},{10,... | collective-permute-start | bytes 73736 | tf_op jit(solution)/shard_map/ppermute | solution.py:266
  15.5 6.4 %collective-permute-start.1 = (f32[48,128]{1,0:T(8,128)S(1)}, f32[48,128]{1,0:T(8,128)S(1)}, u32[]{:S(2)}, u32[]{:S(2)}) collective-permute-start(f32[48,128]{1,0:T(8,128)S(1)} %get-tuple-element.48), channel_id=1, source_target_pairs={{0,1},{1,0},{2,3},{3,2},{4,8},{5,9},{6,10},{7,11},{8,4},{9,5},{10,... | collective-permute-start | bytes 73736 | tf_op jit(solution)/shard_map/ppermute | solution.py:266
  15.5 6.4 %collective-permute-start.2 = (f32[48,128]{1,0:T(8,128)S(1)}, f32[48,128]{1,0:T(8,128)S(1)}, u32[]{:S(2)}, u32[]{:S(2)}) collective-permute-start(f32[48,128]{1,0:T(8,128)S(1)} %get-tuple-element.49), channel_id=1, source_target_pairs={{0,3},{1,2},{2,1},{3,0},{4,7},{5,6},{6,5},{7,4},{8,11},{9,10},{10,... | collective-permute-start | bytes 73736 | tf_op jit(solution)/shard_map/ppermute | solution.py:266
  17.1 4.8 %collective-permute-start.3 = (f32[48,128]{1,0:T(8,128)S(1)}, f32[48,128]{1,0:T(8,128)S(1)}, u32[]{:S(2)}, u32[]{:S(2)}) collective-permute-start(f32[48,128]{1,0:T(8,128)S(1)} %get-tuple-element.50), channel_id=1, source_target_pairs={{0,1},{1,0},{2,3},{3,2},{4,5},{5,4},{6,7},{7,6},{8,9},{9,8},{10,11... | collective-permute-start | bytes 73736 | tf_op jit(solution)/shard_map/ppermute | solution.py:266
  27.5 5.0 %collective-permute-start.4 = (f32[48,128]{1,0:T(8,128)S(1)}, f32[48,128]{1,0:T(8,128)S(1)}, u32[]{:S(2)}, u32[]{:S(2)}) collective-permute-start(f32[48,128]{1,0:T(8,128)S(1)} %get-tuple-element.61), channel_id=1, source_target_pairs={{0,4},{1,5},{2,6},{3,7},{4,0},{5,1},{6,2},{7,3},{8,12},{9,13},{10,... | collective-permute-start | bytes 73736 | tf_op jit(solution)/shard_map/ppermute | solution.py:266
  29.0 3.5 %collective-permute-start.5 = (f32[48,128]{1,0:T(8,128)S(1)}, f32[48,128]{1,0:T(8,128)S(1)}, u32[]{:S(2)}, u32[]{:S(2)}) collective-permute-start(f32[48,128]{1,0:T(8,128)S(1)} %get-tuple-element.62), channel_id=1, source_target_pairs={{0,1},{1,0},{2,3},{3,2},{4,8},{5,9},{6,10},{7,11},{8,4},{9,5},{10,... | collective-permute-start | bytes 73736 | tf_op jit(solution)/shard_map/ppermute | solution.py:266
  29.0 3.5 %collective-permute-start.6 = (f32[48,128]{1,0:T(8,128)S(1)}, f32[48,128]{1,0:T(8,128)S(1)}, u32[]{:S(2)}, u32[]{:S(2)}) collective-permute-start(f32[48,128]{1,0:T(8,128)S(1)} %get-tuple-element.63), channel_id=1, source_target_pairs={{0,3},{1,2},{2,1},{3,0},{4,7},{5,6},{6,5},{7,4},{8,11},{9,10},{10,... | collective-permute-start | bytes 73736 | tf_op jit(solution)/shard_map/ppermute | solution.py:266
  30.6 1.9 %collective-permute-start.7 = (f32[48,128]{1,0:T(8,128)S(1)}, f32[48,128]{1,0:T(8,128)S(1)}, u32[]{:S(2)}, u32[]{:S(2)}) collective-permute-start(f32[48,128]{1,0:T(8,128)S(1)} %get-tuple-element.64), channel_id=1, source_target_pairs={{0,1},{1,0},{2,3},{3,2},{4,5},{5,4},{6,7},{7,6},{8,9},{9,8},{10,11... | collective-permute-start | bytes 73736 | tf_op jit(solution)/shard_map/ppermute | solution.py:266
  33.8 14.2 %all-to-all-start.1 = ((bf16[16,72,128]{2,1,0:T(8,128)(2,1)}), bf16[16,72,128]{2,1,0:T(8,128)(2,1)S(1)}, u32[]{:S(2)}, u32[]{:S(2)}) async-start(bf16[16,72,128]{2,1,0:T(8,128)(2,1)} %get-tuple-element.74), calls=%async_computation.1 | async-start | bytes 589824 | tf_op jit(solution)/shard_map/all_to_all | solution.py:1020
